TPU v7x, 256 devices: a whole 4x4x8 slice. The times are simulated.
256 devices in a mesh: blk: 32 (over y_hi, z, core), grp: 8 (over y_lo, x).
Axes of the slice: x: 4, y: 4 (y_hi: 2, y_lo: 2; y = y_hi * 2 + y_lo), z: 8, core: 2. Of those that a mesh axis runs over, the one named last changes fastest.
Arguments:
- images: bfloat16 [16384, 1152], P(('blk', 'grp')), may hold values from -0.1875 to 0.1875
- texts: bfloat16 [16384, 1152], P(('blk', 'grp')), may hold values from -0.1875 to 0.1875
- logit_scale: float32 [1], replicated, may hold values from 4 to 16
- logit_bias: float32 [1], replicated, may hold values from -6 to -4
Outputs:
- image_grad: float32 [16384, 1152], P(('blk', 'grp'))
- text_grad: float32 [16384, 1152], P(('blk', 'grp'))
All inputs are finite; a program needn't handle non-finite values.
Results may differ from a plain program's by a relative error of at most 0.015.
Values may be sent and summed in bfloat16 or wider, within the bound.
No kernel may reach another device: no remote copies, remote signals or barrier semaphores. Data moves between devices by JAX's collectives and lax.ppermute only.
A program may use at most 64 MiB of HBM per device.

v0:
```python
import jax
import jax.numpy as jnp
from jax import lax
from jax.sharding import PartitionSpec as P

epsilon = 1e-06


def shifted(value, axis, steps):
    count = lax.axis_size(axis)
    pairs = [(source, (source + steps) % count) for source in range(count)]
    return lax.ppermute(value, axis, pairs)


def unit_rows(values):
    widened = values.astype(jnp.float32)
    inverse = lax.rsqrt(jnp.sum(widened * widened, axis=1, keepdims=True) + epsilon)
    return (widened * inverse, inverse)


def through_norm(unit_part, inverse, along_unit):
    projected = jnp.sum(unit_part * along_unit, axis=1, keepdims=True)
    return (along_unit - unit_part * projected) * inverse


def tile_terms(text_block, text_rows, image_block, image_rows, factor, offset):
    logits = lax.dot_general(
        text_block, image_block, (((1,), (1,)), ((), ())), preferred_element_type=jnp.float32
    )
    logits = factor * logits + offset
    paired = (text_rows[:, None] == image_rows[None, :]).astype(jnp.float32)
    weights = (factor * (jax.nn.sigmoid(logits) - paired)).astype(jnp.bfloat16)
    image_part = lax.dot_general(
        weights, text_block, (((0,), (0,)), ((), ())), preferred_element_type=jnp.float32
    )
    text_part = jnp.dot(weights, image_block, preferred_element_type=jnp.float32)
    return (image_part, text_part)


def local(images, texts, logit_scale, logit_bias):
    shard_rows = texts.shape[0]
    features = texts.shape[1]
    cycle_size = lax.axis_size("blk")
    group_size = lax.axis_size("grp")
    cycle_index = lax.axis_index("blk")
    group_index = lax.axis_index("grp")
    factor = logit_scale[0]
    offset = logit_bias[0]
    image_unit, image_inverse = unit_rows(images)
    text_unit, text_inverse = unit_rows(texts)
    text_send = text_unit.astype(jnp.bfloat16)
    group_images = lax.all_gather(image_unit.astype(jnp.bfloat16), "grp", axis=0, tiled=True)
    group_rows = group_size * shard_rows
    image_rows = cycle_index * group_rows + jnp.arange(group_rows, dtype=jnp.int32)

    def piece_rows(anchor, length, skipped):
        return (
            (anchor * group_size + group_index) * shard_rows
            + skipped
            + jnp.arange(length, dtype=jnp.int32)
        )

    def visit_tile(text_block, text_rows):
        return tile_terms(text_block, text_rows, group_images, image_rows, factor, offset)

    image_start = jnp.zeros((group_rows, features), jnp.float32)
    final_turn = cycle_size - 1

    def carried_turn(travelled, loop_state):
        text_piece, running, image_total = loop_state
        anchor = (cycle_index - travelled) % cycle_size
        image_part, text_part = visit_tile(text_piece, piece_rows(anchor, shard_rows, 0))
        text_piece = shifted(text_piece, "blk", 1)
        running = shifted(running + text_part, "blk", 1)
        return (text_piece, running, image_total + image_part)

    empty_sums = jnp.zeros((shard_rows, features), jnp.float32)
    text_piece, running, image_total = lax.fori_loop(
        0, final_turn, carried_turn, (text_send, empty_sums, image_start)
    )
    anchor = (cycle_index - final_turn) % cycle_size
    image_part, text_part = visit_tile(text_piece, piece_rows(anchor, shard_rows, 0))
    image_total = image_total + image_part
    text_total = shifted((running + text_part).astype(jnp.bfloat16), "blk", 1).astype(jnp.float32)
    image_sum = lax.psum_scatter(
        image_total.astype(jnp.bfloat16), "grp", scatter_dimension=0, tiled=True
    ).astype(jnp.float32)
    image_grad = through_norm(image_unit, image_inverse, image_sum)
    text_grad = through_norm(text_unit, text_inverse, text_total)
    return (image_grad, text_grad)


def solution(mesh):
    in_specs = (P(("blk", "grp"), None), P(("blk", "grp"), None), P(), P())
    out_specs = (P(("blk", "grp"), None), P(("blk", "grp"), None))
    return jax.shard_map(local, mesh=mesh, in_specs=in_specs, out_specs=out_specs, check_vma=False)
```

profile of v0, /device:TPU:8, one launch (start us, length us, event | category | flops | bytes accessed | tf_op | source)
XLA Modules:
  0.0 622.9 jit_solution(12039312099627436552)
XLA Ops:
  14.6 39.4 %all-gather.2.cloned.1.call-done = bf16[512,1152]{1,0:T(8,128)(2,1)} async-done(((bf16[64,1152]{1,0:T(8,128)(2,1)}), bf16[512,1152]{1,0:T(8,128)(2,1)}) %all-gather.2.cloned.1.call-update) | async-done | bytes 1179664 | tf_op jit(solution)/shard_map/all_gather | solution.py:52
  54.8 517.0 %while.20 = (s32[]{:T(128)}, bf16[64,1152]{1,0:T(8,128)(2,1)}, f32[64,1152]{1,0:T(8,128)}, f32[512,1152]{1,0:T(8,128)S(1)}, f32[]{:T(128)}, /*index=5*/bf16[512,...) while((s32[]{:T(128)}, bf16[64,1152]{1,0:T(8,128)(2,1)}, ...), condition=%wide.region_3.4_spmd.clone, body=%wide.region_2.3_spmd.clone.sunk | while | flops 228074064 | bytes 17568780 | solution.py:78
  81.6 5.8 collective-permute-done.1
  115.0 5.8 collective-permute-done.1
  131.7 5.8 collective-permute-done.1
  165.0 5.8 collective-permute-done.1
  198.4 5.8 collective-permute-done.1
  215.1 5.8 collective-permute-done.1
  231.7 5.8 collective-permute-done.1
  248.4 5.8 collective-permute-done.1
  281.8 5.8 collective-permute-done.1
  315.1 5.8 collective-permute-done.1
  331.8 5.8 collective-permute-done.1
  348.5 5.8 collective-permute-done.1
  365.2 5.8 collective-permute-done.1
  398.5 5.8 collective-permute-done.1
  431.9 5.8 collective-permute-done.1
  448.6 5.8 collective-permute-done.1
  465.2 5.8 collective-permute-done.1
  481.9 5.8 collective-permute-done.1
  515.3 5.8 collective-permute-done.1
  548.6 5.8 collective-permute-done.1
  577.8 8.2 %collective-permute-done.2 = bf16[64,1152]{1,0:T(8,128)(2,1)S(1)} collective-permute-done((bf16[64,1152]{1,0:T(8,128)(2,1)S(1)}, bf16[64,1152]{1,0:T(8,128)(2,1)S(1)}, u32[]{:S(2)}, u32[]{:S(2)}) %collective-permute-start.2) | collective-permute-done | bytes 147488 | tf_op jit(solution)/shard_map/ppermute | solution.py:12
  587.0 26.1 %reduce-scatter.2.cloned.1.call-done = bf16[64,1152]{1,0:T(8,128)(2,1)} async-done(((bf16[512,1152]{1,0:T(8,128)(2,1)}), bf16[64,1152]{1,0:T(8,128)(2,1)}) %reduce-scatter.2.cloned.1.call-update) | async-done | bytes 147472 | tf_op jit(solution)/shard_map/reduce_scatter | solution.py:85
  (568 shorter events, 416.2 us)
Async XLA Ops:
  7.2 46.9 %all-gather.2.cloned.1.call-start = ((), (), s32[]{:S(2)}) async-start(), calls=%async_computation.1 | async-start | bytes 1327104 | tf_op jit(solution)/shard_map/all_gather | solution.py:52
  10.0 603.2 %reduce-scatter.2.cloned.1.call-start = ((), (), s32[]{:S(2)}) async-start(), calls=%async_computation.2 | async-start | bytes 1327104 | tf_op jit(solution)/shard_map/reduce_scatter | solution.py:85
  60.8 10.0 %collective-permute-start.1 = (f32[64,1152]{1,0:T(8,128)}, f32[64,1152]{1,0:T(8,128)S(1)}, u32[]{:S(2)}, u32[]{:S(2)}) collective-permute-start(f32[64,1152]{1,0:T(8,128)} %convolution_add_fusion.6), channel_id=1, source_target_pairs={{0,8},{8,16},{16,24},{24,32},{32,40},{40,48},{48,56},{56,64},{64,7... | collective-permute-start | bytes 884744 | tf_op jit(solution)/shard_map/while/body/eval_jaxpr/ppermute | solution.py:12
  77.5 10.0 %collective-permute-start.1 = (f32[64,1152]{1,0:T(8,128)}, f32[64,1152]{1,0:T(8,128)S(1)}, u32[]{:S(2)}, u32[]{:S(2)}) collective-permute-start(f32[64,1152]{1,0:T(8,128)} %convolution_add_fusion.6), channel_id=1, source_target_pairs={{0,8},{8,16},{16,24},{24,32},{32,40},{40,48},{48,56},{56,64},{64,7... | collective-permute-start | bytes 884744 | tf_op jit(solution)/shard_map/while/body/eval_jaxpr/ppermute | solution.py:12
  94.1 10.0 %collective-permute-start.1 = (f32[64,1152]{1,0:T(8,128)}, f32[64,1152]{1,0:T(8,128)S(1)}, u32[]{:S(2)}, u32[]{:S(2)}) collective-permute-start(f32[64,1152]{1,0:T(8,128)} %convolution_add_fusion.6), channel_id=1, source_target_pairs={{0,8},{8,16},{16,24},{24,32},{32,40},{40,48},{48,56},{56,64},{64,7... | collective-permute-start | bytes 884744 | tf_op jit(solution)/shard_map/while/body/eval_jaxpr/ppermute | solution.py:12
  110.8 10.0 %collective-permute-start.1 = (f32[64,1152]{1,0:T(8,128)}, f32[64,1152]{1,0:T(8,128)S(1)}, u32[]{:S(2)}, u32[]{:S(2)}) collective-permute-start(f32[64,1152]{1,0:T(8,128)} %convolution_add_fusion.6), channel_id=1, source_target_pairs={{0,8},{8,16},{16,24},{24,32},{32,40},{40,48},{48,56},{56,64},{64,7... | collective-permute-start | bytes 884744 | tf_op jit(solution)/shard_map/while/body/eval_jaxpr/ppermute | solution.py:12
  127.5 10.0 %collective-permute-start.1 = (f32[64,1152]{1,0:T(8,128)}, f32[64,1152]{1,0:T(8,128)S(1)}, u32[]{:S(2)}, u32[]{:S(2)}) collective-permute-start(f32[64,1152]{1,0:T(8,128)} %convolution_add_fusion.6), channel_id=1, source_target_pairs={{0,8},{8,16},{16,24},{24,32},{32,40},{40,48},{48,56},{56,64},{64,7... | collective-permute-start | bytes 884744 | tf_op jit(solution)/shard_map/while/body/eval_jaxpr/ppermute | solution.py:12
  144.2 10.0 %collective-permute-start.1 = (f32[64,1152]{1,0:T(8,128)}, f32[64,1152]{1,0:T(8,128)S(1)}, u32[]{:S(2)}, u32[]{:S(2)}) collective-permute-start(f32[64,1152]{1,0:T(8,128)} %convolution_add_fusion.6), channel_id=1, source_target_pairs={{0,8},{8,16},{16,24},{24,32},{32,40},{40,48},{48,56},{56,64},{64,7... | collective-permute-start | bytes 884744 | tf_op jit(solution)/shard_map/while/body/eval_jaxpr/ppermute | solution.py:12
  160.8 10.0 %collective-permute-start.1 = (f32[64,1152]{1,0:T(8,128)}, f32[64,1152]{1,0:T(8,128)S(1)}, u32[]{:S(2)}, u32[]{:S(2)}) collective-permute-start(f32[64,1152]{1,0:T(8,128)} %convolution_add_fusion.6), channel_id=1, source_target_pairs={{0,8},{8,16},{16,24},{24,32},{32,40},{40,48},{48,56},{56,64},{64,7... | collective-permute-start | bytes 884744 | tf_op jit(solution)/shard_map/while/body/eval_jaxpr/ppermute | solution.py:12
  177.5 10.0 %collective-permute-start.1 = (f32[64,1152]{1,0:T(8,128)}, f32[64,1152]{1,0:T(8,128)S(1)}, u32[]{:S(2)}, u32[]{:S(2)}) collective-permute-start(f32[64,1152]{1,0:T(8,128)} %convolution_add_fusion.6), channel_id=1, source_target_pairs={{0,8},{8,16},{16,24},{24,32},{32,40},{40,48},{48,56},{56,64},{64,7... | collective-permute-start | bytes 884744 | tf_op jit(solution)/shard_map/while/body/eval_jaxpr/ppermute | solution.py:12
  194.2 10.0 %collective-permute-start.1 = (f32[64,1152]{1,0:T(8,128)}, f32[64,1152]{1,0:T(8,128)S(1)}, u32[]{:S(2)}, u32[]{:S(2)}) collective-permute-start(f32[64,1152]{1,0:T(8,128)} %convolution_add_fusion.6), channel_id=1, source_target_pairs={{0,8},{8,16},{16,24},{24,32},{32,40},{40,48},{48,56},{56,64},{64,7... | collective-permute-start | bytes 884744 | tf_op jit(solution)/shard_map/while/body/eval_jaxpr/ppermute | solution.py:12
  210.9 10.0 %collective-permute-start.1 = (f32[64,1152]{1,0:T(8,128)}, f32[64,1152]{1,0:T(8,128)S(1)}, u32[]{:S(2)}, u32[]{:S(2)}) collective-permute-start(f32[64,1152]{1,0:T(8,128)} %convolution_add_fusion.6), channel_id=1, source_target_pairs={{0,8},{8,16},{16,24},{24,32},{32,40},{40,48},{48,56},{56,64},{64,7... | collective-permute-start | bytes 884744 | tf_op jit(solution)/shard_map/while/body/eval_jaxpr/ppermute | solution.py:12
  260.9 10.0 %collective-permute-start.1 = (f32[64,1152]{1,0:T(8,128)}, f32[64,1152]{1,0:T(8,128)S(1)}, u32[]{:S(2)}, u32[]{:S(2)}) collective-permute-start(f32[64,1152]{1,0:T(8,128)} %convolution_add_fusion.6), channel_id=1, source_target_pairs={{0,8},{8,16},{16,24},{24,32},{32,40},{40,48},{48,56},{56,64},{64,7... | collective-permute-start | bytes 884744 | tf_op jit(solution)/shard_map/while/body/eval_jaxpr/ppermute | solution.py:12
  294.3 10.0 %collective-permute-start.1 = (f32[64,1152]{1,0:T(8,128)}, f32[64,1152]{1,0:T(8,128)S(1)}, u32[]{:S(2)}, u32[]{:S(2)}) collective-permute-start(f32[64,1152]{1,0:T(8,128)} %convolution_add_fusion.6), channel_id=1, source_target_pairs={{0,8},{8,16},{16,24},{24,32},{32,40},{40,48},{48,56},{56,64},{64,7... | collective-permute-start | bytes 884744 | tf_op jit(solution)/shard_map/while/body/eval_jaxpr/ppermute | solution.py:12
  311.0 10.0 %collective-permute-start.1 = (f32[64,1152]{1,0:T(8,128)}, f32[64,1152]{1,0:T(8,128)S(1)}, u32[]{:S(2)}, u32[]{:S(2)}) collective-permute-start(f32[64,1152]{1,0:T(8,128)} %convolution_add_fusion.6), channel_id=1, source_target_pairs={{0,8},{8,16},{16,24},{24,32},{32,40},{40,48},{48,56},{56,64},{64,7... | collective-permute-start | bytes 884744 | tf_op jit(solution)/shard_map/while/body/eval_jaxpr/ppermute | solution.py:12
  327.6 10.0 %collective-permute-start.1 = (f32[64,1152]{1,0:T(8,128)}, f32[64,1152]{1,0:T(8,128)S(1)}, u32[]{:S(2)}, u32[]{:S(2)}) collective-permute-start(f32[64,1152]{1,0:T(8,128)} %convolution_add_fusion.6), channel_id=1, source_target_pairs={{0,8},{8,16},{16,24},{24,32},{32,40},{40,48},{48,56},{56,64},{64,7... | collective-permute-start | bytes 884744 | tf_op jit(solution)/shard_map/while/body/eval_jaxpr/ppermute | solution.py:12
  344.3 10.0 %collective-permute-start.1 = (f32[64,1152]{1,0:T(8,128)}, f32[64,1152]{1,0:T(8,128)S(1)}, u32[]{:S(2)}, u32[]{:S(2)}) collective-permute-start(f32[64,1152]{1,0:T(8,128)} %convolution_add_fusion.6), channel_id=1, source_target_pairs={{0,8},{8,16},{16,24},{24,32},{32,40},{40,48},{48,56},{56,64},{64,7... | collective-permute-start | bytes 884744 | tf_op jit(solution)/shard_map/while/body/eval_jaxpr/ppermute | solution.py:12
  361.0 10.0 %collective-permute-start.1 = (f32[64,1152]{1,0:T(8,128)}, f32[64,1152]{1,0:T(8,128)S(1)}, u32[]{:S(2)}, u32[]{:S(2)}) collective-permute-start(f32[64,1152]{1,0:T(8,128)} %convolution_add_fusion.6), channel_id=1, source_target_pairs={{0,8},{8,16},{16,24},{24,32},{32,40},{40,48},{48,56},{56,64},{64,7... | collective-permute-start | bytes 884744 | tf_op jit(solution)/shard_map/while/body/eval_jaxpr/ppermute | solution.py:12
  377.7 10.0 %collective-permute-start.1 = (f32[64,1152]{1,0:T(8,128)}, f32[64,1152]{1,0:T(8,128)S(1)}, u32[]{:S(2)}, u32[]{:S(2)}) collective-permute-start(f32[64,1152]{1,0:T(8,128)} %convolution_add_fusion.6), channel_id=1, source_target_pairs={{0,8},{8,16},{16,24},{24,32},{32,40},{40,48},{48,56},{56,64},{64,7... | collective-permute-start | bytes 884744 | tf_op jit(solution)/shard_map/while/body/eval_jaxpr/ppermute | solution.py:12
  394.3 10.0 %collective-permute-start.1 = (f32[64,1152]{1,0:T(8,128)}, f32[64,1152]{1,0:T(8,128)S(1)}, u32[]{:S(2)}, u32[]{:S(2)}) collective-permute-start(f32[64,1152]{1,0:T(8,128)} %convolution_add_fusion.6), channel_id=1, source_target_pairs={{0,8},{8,16},{16,24},{24,32},{32,40},{40,48},{48,56},{56,64},{64,7... | collective-permute-start | bytes 884744 | tf_op jit(solution)/shard_map/while/body/eval_jaxpr/ppermute | solution.py:12
  411.0 10.0 %collective-permute-start.1 = (f32[64,1152]{1,0:T(8,128)}, f32[64,1152]{1,0:T(8,128)S(1)}, u32[]{:S(2)}, u32[]{:S(2)}) collective-permute-start(f32[64,1152]{1,0:T(8,128)} %convolution_add_fusion.6), channel_id=1, source_target_pairs={{0,8},{8,16},{16,24},{24,32},{32,40},{40,48},{48,56},{56,64},{64,7... | collective-permute-start | bytes 884744 | tf_op jit(solution)/shard_map/while/body/eval_jaxpr/ppermute | solution.py:12
  461.1 10.0 %collective-permute-start.1 = (f32[64,1152]{1,0:T(8,128)}, f32[64,1152]{1,0:T(8,128)S(1)}, u32[]{:S(2)}, u32[]{:S(2)}) collective-permute-start(f32[64,1152]{1,0:T(8,128)} %convolution_add_fusion.6), channel_id=1, source_target_pairs={{0,8},{8,16},{16,24},{24,32},{32,40},{40,48},{48,56},{56,64},{64,7... | collective-permute-start | bytes 884744 | tf_op jit(solution)/shard_map/while/body/eval_jaxpr/ppermute | solution.py:12
  477.7 10.0 %collective-permute-start.1 = (f32[64,1152]{1,0:T(8,128)}, f32[64,1152]{1,0:T(8,128)S(1)}, u32[]{:S(2)}, u32[]{:S(2)}) collective-permute-start(f32[64,1152]{1,0:T(8,128)} %convolution_add_fusion.6), channel_id=1, source_target_pairs={{0,8},{8,16},{16,24},{24,32},{32,40},{40,48},{48,56},{56,64},{64,7... | collective-permute-start | bytes 884744 | tf_op jit(solution)/shard_map/while/body/eval_jaxpr/ppermute | solution.py:12
  511.1 10.0 %collective-permute-start.1 = (f32[64,1152]{1,0:T(8,128)}, f32[64,1152]{1,0:T(8,128)S(1)}, u32[]{:S(2)}, u32[]{:S(2)}) collective-permute-start(f32[64,1152]{1,0:T(8,128)} %convolution_add_fusion.6), channel_id=1, source_target_pairs={{0,8},{8,16},{16,24},{24,32},{32,40},{40,48},{48,56},{56,64},{64,7... | collective-permute-start | bytes 884744 | tf_op jit(solution)/shard_map/while/body/eval_jaxpr/ppermute | solution.py:12
  (169 other events, 719.8 us)
Sparse Core Ops, SparseCore 0:
  10.4 43.6 all-gather.1
  576.3 36.8 reduce-scatter.1
where the time goes:
time: 626 us; the launch traced here: 623 us
  waiting for transfers between devices  324 us (52%)
  matrix products  193 us (31%)
  local copies, waits for them, and re-layouts  76.4 us (12%)
  between operations  15.4 us (2%)
  other arithmetic  10.2 us (2%)
    ppermute x63, waiting for transfers between devices, shifted(): return lax.ppermute(value, axis, pairs)  259 us
    dot_general x32, matrix products, tile_terms(): lax.dot_general(text_block, image_block, (((1,), (1,)), ((), ())), prefer...  101 us
    while x279, local copies, waits for them, and re-layouts  74.5 us
    dot_general x32, matrix products, tile_terms(): lax.dot_general(weights, text_block, (((0,), (0,)), ((), ())), preferred_...  59.2 us
    all_gather x1, waiting for transfers between devices, local(): lax.all_gather(image_unit.astype(jnp.bfloat16), 'grp', axis=0, tiled=True)  39.4 us
    dot_general x32, matrix products, tile_terms(): jnp.dot(weights, image_block, preferred_element_type=jnp.float32)  32.7 us
    reduce_scatter x1, waiting for transfers between devices, local(): lax.psum_scatter(image_total.astype(jnp.bfloat16), 'grp', scatter_dimensi...  26.1 us
  transfers between devices with their start and end apart: 65, of which 65 were waited for; matrix products, arithmetic and copies ran while one was open for 31% of the time, Pallas kernels for 0%

commit v1 on v0

v1 whole, which is shorter than its diff:
```python
import jax
import jax.numpy as jnp
from jax import lax
from jax.sharding import PartitionSpec as P

epsilon = 1e-06
AXES = ("blk", "grp")


def place(x, y, z, core):
    return ((((y >> 1) * 8 + z) * 2 + core) * 2 + (y & 1)) * 4 + x


def partner(position, size, first):
    step = 1 if (position % 2 == 0) == first else -1
    return (position + step) % size


def pairs_of(axis, first):
    pairs = []
    for x in range(4):
        for y in range(4):
            for z in range(8):
                for core in range(2):
                    side = first == (core == 0)
                    to = [x, y, z, core]
                    if axis == "x":
                        to[0] = partner(x, 4, side)
                    elif axis == "y":
                        to[1] = partner(y, 4, side)
                    elif axis == "z":
                        to[2] = partner(z, 8, side)
                    else:
                        to[3] = 1 - core
                    pairs.append((place(x, y, z, core), place(*to)))
    return sorted(pairs)


def exchange(axis, first=True):
    pairs = pairs_of(axis, first)
    return lambda value: lax.ppermute(value, AXES, pairs)


def unit_rows(values):
    widened = values.astype(jnp.float32)
    inverse = lax.rsqrt(jnp.sum(widened * widened, axis=1, keepdims=True) + epsilon)
    return (widened * inverse, inverse)


def through_norm(unit_part, inverse, along_unit):
    projected = jnp.sum(unit_part * along_unit, axis=1, keepdims=True)
    return (along_unit - unit_part * projected) * inverse


def tile_terms(texts, images, factor, offset):
    logits = lax.dot_general(
        texts, images, (((1,), (1,)), ((), ())), preferred_element_type=jnp.float32
    )
    weights = (factor * jax.nn.sigmoid(factor * logits + offset)).astype(jnp.bfloat16)
    image_part = lax.dot_general(
        weights, texts, (((0,), (0,)), ((), ())), preferred_element_type=jnp.float32
    )
    text_part = jnp.dot(weights, images, preferred_element_type=jnp.float32)
    return (image_part, text_part)


def rounded(value):
    return value.astype(jnp.bfloat16)


def widened(value):
    return value.astype(jnp.float32)


def join(*parts):
    return jnp.concatenate(parts, axis=0)


def local(images, texts, logit_scale, logit_bias):
    x1, x2 = exchange("x", True), exchange("x", False)
    y1, y2 = exchange("y", True), exchange("y", False)
    z1, z2 = exchange("z", True), exchange("z", False)
    sibling = exchange("core")
    route_a = (x1, x2, y1, y2)
    route_b = (y1, y2, x1, x2)
    half = images.shape[0] // 2
    factor = logit_scale[0]
    offset = logit_bias[0]
    image_unit, image_inverse = unit_rows(images)
    text_unit, text_inverse = unit_rows(texts)
    image_send = rounded(image_unit)
    text_send = rounded(text_unit)

    a, b = image_send[:half], image_send[half:]
    t0 = text_send
    r1 = z1(t0)
    a = join(a, route_a[0](a))
    b = join(b, route_b[0](b))
    near = join(t0, r1)
    r2 = z2(near)
    a = join(a, route_a[1](a))
    b = join(b, route_b[1](b))
    r3 = z1(r2)
    a = join(a, route_a[2](a))
    b = join(b, route_b[2](b))
    first_text = join(near, r2)
    first_other = sibling(first_text)
    r4 = z2(r3)
    late_a = route_a[3](a)
    late_b = route_b[3](b)
    second_text = join(r3, r4)
    second_other = sibling(second_text)
    all_texts = join(first_text, second_text, first_other, second_other)

    early_images = join(a, b)
    late_images = join(late_a, late_b)
    early_sum, text_early = tile_terms(all_texts, early_images, factor, offset)
    late_sum, text_late = tile_terms(all_texts, late_images, factor, offset)
    text_sum = text_early + text_late

    count = early_images.shape[0] // 2
    keep_a, keep_b = early_sum[:count], early_sum[count:]
    give_a, give_b = late_sum[:count], late_sum[count:]
    own_texts = t0.shape[0] * 8
    column = text_sum[:own_texts] + widened(sibling(rounded(text_sum[own_texts:])))
    s0, s1 = column[:64], column[64:128]
    s2, s3, s4 = column[128:256], column[256:384], column[384:]
    for step in (3, 2, 1, 0):
        keep_a = keep_a + widened(route_a[step](rounded(give_a)))
        keep_b = keep_b + widened(route_b[step](rounded(give_b)))
        if step > 0:
            count = count // 2
            keep_a, give_a = keep_a[:count], keep_a[count:]
            keep_b, give_b = keep_b[:count], keep_b[count:]
    s3 = s3 + widened(z2(rounded(s4)))
    s2 = s2 + widened(z1(rounded(s3)))
    s01 = join(s0, s1) + widened(z2(rounded(s2)))
    text_total = s01[:64] + widened(z1(rounded(s01[64:])))
    image_total = join(keep_a, keep_b) - factor * widened(text_send)
    text_total = text_total - factor * widened(image_send)
    image_grad = through_norm(image_unit, image_inverse, image_total)
    text_grad = through_norm(text_unit, text_inverse, text_total)
    return (image_grad, text_grad)


def solution(mesh):
    in_specs = (P(AXES, None), P(AXES, None), P(), P())
    out_specs = (P(AXES, None), P(AXES, None))
    return jax.shard_map(local, mesh=mesh, in_specs=in_specs, out_specs=out_specs, check_vma=False)
```

time: 626 us -> 111 us (0.18)
  waiting for transfers between devices: 324 us -> 51.4 us
  matrix products: 193 us -> 9.85 us
  local copies, waits for them, and re-layouts: 76.4 us -> 0.93 us
  starting transfers between devices: 1.99 us -> 39.1 us
  between operations: 15.4 us -> 2.4 us
    ppermute x63 -> x27, waiting for transfers between devices: 259 us -> 51.4 us  [exchange(): return lambda value: lax.ppermute(value, AXES, pairs)]
    dot_general x96 -> x6, matrix products: 193 us -> 9.85 us  [the longest x2 3.67 us: tile_terms(): lax.dot_general(texts, images, (((1,), (1,)), ((), ())), preferred_elemen...]
    while x279 -> x0, local copies, waits for them, and re-layouts: 74.5 us -> none
    all_gather x1 -> x0, waiting for transfers between devices: 39.4 us -> none  [local(): lax.all_gather(image_unit.astype(jnp.bfloat16), 'grp', axis=0, tiled=True)]
    ppermute x63 -> x27, starting transfers between devices: 1.91 us -> 39.1 us  [exchange(): return lambda value: lax.ppermute(value, AXES, pairs)]
    reduce_scatter x1 -> x0, waiting for transfers between devices: 26.1 us -> none  [local(): lax.psum_scatter(image_total.astype(jnp.bfloat16), 'grp', scatter_dimensi...]
  transfers between devices with their start and end apart: 65 -> 27, of which waited for: 65 -> 14; matrix products, arithmetic and copies ran while one was open for 31% -> 10% of each run, Pallas kernels for 0% -> 0%
where the time goes in v1:
time: 111 us
  waiting for transfers between devices  51.4 us (46%)
  starting transfers between devices  39.1 us (35%)
  matrix products  9.85 us (9%)
  other arithmetic  7.34 us (7%)
  between operations  2.4 us (2%)
    ppermute x27, waiting for transfers between devices, exchange(): return lambda value: lax.ppermute(value, AXES, pairs)  51.4 us
    ppermute x27, starting transfers between devices, exchange(): return lambda value: lax.ppermute(value, AXES, pairs)  39.1 us
    dot_general x2, matrix products, tile_terms(): lax.dot_general(texts, images, (((1,), (1,)), ((), ())), preferred_elemen...  3.67 us
    dot_general x2, matrix products, tile_terms(): lax.dot_general(weights, texts, (((0,), (0,)), ((), ())), preferred_eleme...  3.14 us
    dot_general x2, matrix products, tile_terms(): text_part = jnp.dot(weights, images, preferred_element_type=jnp.float32)  3.04 us
  transfers between devices with their start and end apart: 27, of which 14 were waited for; matrix products, arithmetic and copies ran while one was open for 10% of the time, Pallas kernels for 0%

profile of v1, /device:TPU:8, one launch (start us, length us, event | category | flops | bytes accessed | tf_op | source)
XLA Modules:
  0.0 111.0 jit_solution(882607704099947276)
XLA Ops:
  2.7 2.3 %collective-permute-start.9 = (bf16[32,1152]{1,0:T(8,128)(2,1)S(1)}, bf16[32,1152]{1,0:T(8,128)(2,1)S(1)}, u32[]{:S(2)}, u32[]{:S(2)}) collective-permute-start(bf16[32,1152]{1,0:T(8,128)(2,1)S(1)} %get-tuple-element.8), channel_id=1, source_target_pairs={{0,4},{1,5},{2,6},{3,7},{4,0},{5,1},{6,2},{7,3},{8,140},{9,141},{1... | collective-permute-start | bytes 221192 | tf_op jit(solution)/shard_map/ppermute | solution.py:41
  7.1 1.8 %collective-permute-start = (bf16[64,1152]{1,0:T(8,128)(2,1)S(1)}, bf16[64,1152]{1,0:T(8,128)(2,1)S(1)}, u32[]{:S(2)}, u32[]{:S(2)}) collective-permute-start(bf16[64,1152]{1,0:T(8,128)(2,1)S(1)} %get-tuple-element.3), channel_id=1, source_target_pairs={{0,16},{1,17},{2,18},{3,19},{4,20},{5,21},{6,22},{7,23},{8,120},{9... | collective-permute-start | bytes 442376 | tf_op jit(solution)/shard_map/ppermute | solution.py:41
  10.2 2.5 %collective-permute-start.10 = (bf16[64,1152]{1,0:T(8,128)(2,1)S(1)}, bf16[64,1152]{1,0:T(8,128)(2,1)S(1)}, u32[]{:S(2)}, u32[]{:S(2)}) collective-permute-start(bf16[64,1152]{1,0:T(8,128)(2,1)S(1)} %pad_maximum_fusion.8), channel_id=1, source_target_pairs={{0,132},{1,133},{2,134},{3,135},{4,128},{5,129},{6,130},{7,131},{8... | collective-permute-start | bytes 442376 | tf_op jit(solution)/shard_map/ppermute | solution.py:41
  12.7 2.2 %collective-permute-start.7 = (bf16[64,1152]{1,0:T(8,128)(2,1)S(1)}, bf16[64,1152]{1,0:T(8,128)(2,1)S(1)}, u32[]{:S(2)}, u32[]{:S(2)}) collective-permute-start(bf16[64,1152]{1,0:T(8,128)(2,1)S(1)} %pad_maximum_fusion.7), channel_id=1, source_target_pairs={{0,3},{1,2},{2,1},{3,0},{4,7},{5,6},{6,5},{7,4},{8,9},{9,8},{10,11... | collective-permute-start | bytes 442376 | tf_op jit(solution)/shard_map/ppermute | solution.py:41
  14.9 5.0 %collective-permute-start.1 = (bf16[128,1152]{1,0:T(8,128)(2,1)S(1)}, bf16[128,1152]{1,0:T(8,128)(2,1)S(1)}, u32[]{:S(2)}, u32[]{:S(2)}) collective-permute-start(bf16[128,1152]{1,0:T(8,128)(2,1)S(1)} %pad_maximum_fusion.4), channel_id=1, source_target_pairs={{0,112},{1,113},{2,114},{3,115},{4,116},{5,117},{6,118},{7,119},{8... | collective-permute-start | bytes 884744 | tf_op jit(solution)/shard_map/ppermute | solution.py:41
  22.2 2.5 %collective-permute-done.1 = bf16[128,1152]{1,0:T(8,128)(2,1)S(1)} collective-permute-done((bf16[128,1152]{1,0:T(8,128)(2,1)S(1)}, bf16[128,1152]{1,0:T(8,128)(2,1)S(1)}, u32[]{:S(2)}, u32[]{:S(2)}) %collective-permute-start.1) | collective-permute-done | bytes 294944 | tf_op jit(solution)/shard_map/ppermute | solution.py:41
  24.9 2.6 %collective-permute-done.8 = bf16[128,1152]{1,0:T(8,128)(2,1)S(1)} collective-permute-done((bf16[128,1152]{1,0:T(8,128)(2,1)S(1)}, bf16[128,1152]{1,0:T(8,128)(2,1)S(1)}, u32[]{:S(2)}, u32[]{:S(2)}) %collective-permute-start.8) | collective-permute-done | bytes 294944 | tf_op jit(solution)/shard_map/ppermute | solution.py:41
  28.2 2.8 %collective-permute-start.13 = (bf16[256,1152]{1,0:T(8,128)(2,1)S(1)}, bf16[256,1152]{1,0:T(8,128)(2,1)S(1)}, u32[]{:S(2)}, u32[]{:S(2)}) collective-permute-start(bf16[256,1152]{1,0:T(8,128)(2,1)S(1)} %pad_maximum_fusion.3), channel_id=1, source_target_pairs={{0,3},{1,2},{2,1},{3,0},{4,7},{5,6},{6,5},{7,4},{8,9},{9,8},{10,11... | collective-permute-start | bytes 1769480 | tf_op jit(solution)/shard_map/ppermute | solution.py:41
  31.6 5.0 %collective-permute-start.3 = (bf16[128,1152]{1,0:T(8,128)(2,1)S(1)}, bf16[128,1152]{1,0:T(8,128)(2,1)S(1)}, u32[]{:S(2)}, u32[]{:S(2)}) collective-permute-start(bf16[128,1152]{1,0:T(8,128)(2,1)S(1)} %collective-permute-done.2), channel_id=1, source_target_pairs={{0,112},{1,113},{2,114},{3,115},{4,116},{5,117},{6,118},{7,119},{8... | collective-permute-start | bytes 884744 | tf_op jit(solution)/shard_map/ppermute | solution.py:41
  36.6 4.6 %collective-permute-done.3 = bf16[128,1152]{1,0:T(8,128)(2,1)S(1)} collective-permute-done((bf16[128,1152]{1,0:T(8,128)(2,1)S(1)}, bf16[128,1152]{1,0:T(8,128)(2,1)S(1)}, u32[]{:S(2)}, u32[]{:S(2)}) %collective-permute-start.3) | collective-permute-done | bytes 294944 | tf_op jit(solution)/shard_map/ppermute | solution.py:41
  43.5 1.8 %multiply_convert_fusion = bf16[1024,512]{1,0:T(8,128)(2,1)S(1)} fusion(bf16[1024,1152]{1,0:T(8,128)(2,1)S(1)} %constant_dynamic-update-slice_fusion, bf16[512,1152]{1,0:T(8,128)(2,1)S(1)} %constant_dynamic-update-slice_fusion.15, f32[]{:T(128)} %bitcast.21, f32[]{:T(128)} %bitcast.14), kind=kOutput, calls=%fused_computation.4 | convolution fusion | flops 1211629568 | bytes 4587528 | tf_op jit(solution)/shard_map/dot_general | solution.py:56
  47.0 2.3 %collective-permute-start.14 = (bf16[256,1152]{1,0:T(8,128)(2,1)S(1)}, bf16[256,1152]{1,0:T(8,128)(2,1)S(1)}, u32[]{:S(2)}, u32[]{:S(2)}) collective-permute-start(bf16[256,1152]{1,0:T(8,128)(2,1)S(1)} %get-tuple-element.6), channel_id=1, source_target_pairs={{0,132},{1,133},{2,134},{3,135},{4,128},{5,129},{6,130},{7,131},{8... | collective-permute-start | bytes 1769480 | tf_op jit(solution)/shard_map/ppermute | solution.py:41
  49.3 1.8 %multiply_convert_fusion.1 = bf16[1024,512]{1,0:T(8,128)(2,1)S(1)} fusion(bf16[1024,1152]{1,0:T(8,128)(2,1)S(1)} %constant_dynamic-update-slice_fusion, bf16[512,1152]{1,0:T(8,128)(2,1)S(1)} %constant_dynamic-update-slice_fusion.7, f32[]{:T(128)} %bitcast.20, f32[]{:T(128)} %bitcast.16), kind=kOutput, calls=%fused_computation.5 | convolution fusion | flops 1211629568 | bytes 4587528 | tf_op jit(solution)/shard_map/dot_general | solution.py:56
  54.2 2.9 %collective-permute-done.14 = bf16[256,1152]{1,0:T(8,128)(2,1)S(1)} collective-permute-done((bf16[256,1152]{1,0:T(8,128)(2,1)S(1)}, bf16[256,1152]{1,0:T(8,128)(2,1)S(1)}, u32[]{:S(2)}, u32[]{:S(2)}) %collective-permute-start.14) | collective-permute-done | bytes 589856 | tf_op jit(solution)/shard_map/ppermute | solution.py:41
  57.2 3.2 %collective-permute-done.18 = bf16[256,1152]{1,0:T(8,128)(2,1)S(1)} collective-permute-done((bf16[256,1152]{1,0:T(8,128)(2,1)S(1)}, bf16[256,1152]{1,0:T(8,128)(2,1)S(1)}, u32[]{:S(2)}, u32[]{:S(2)}) %collective-permute-start.18) | collective-permute-done | bytes 589856 | tf_op jit(solution)/shard_map/ppermute | solution.py:41
  64.1 3.3 %collective-permute-done.19 = bf16[128,1152]{1,0:T(8,128)(2,1)S(1)} collective-permute-done((bf16[128,1152]{1,0:T(8,128)(2,1)S(1)}, bf16[128,1152]{1,0:T(8,128)(2,1)S(1)}, u32[]{:S(2)}, u32[]{:S(2)}) %collective-permute-start.19) | collective-permute-done | bytes 294944 | tf_op jit(solution)/shard_map/ppermute | solution.py:41
  67.7 3.1 %collective-permute-done.15 = bf16[128,1152]{1,0:T(8,128)(2,1)S(1)} collective-permute-done((bf16[128,1152]{1,0:T(8,128)(2,1)S(1)}, bf16[128,1152]{1,0:T(8,128)(2,1)S(1)}, u32[]{:S(2)}, u32[]{:S(2)}) %collective-permute-start.15) | collective-permute-done | bytes 294944 | tf_op jit(solution)/shard_map/ppermute | solution.py:41
  72.8 2.8 %collective-permute-start.21 = (bf16[32,1152]{1,0:T(8,128)(2,1)S(1)}, bf16[32,1152]{1,0:T(8,128)(2,1)S(1)}, u32[]{:S(2)}, u32[]{:S(2)}) collective-permute-start(bf16[32,1152]{1,0:T(8,128)(2,1)S(1)} %slice.179), channel_id=1, source_target_pairs={{0,4},{1,5},{2,6},{3,7},{4,0},{5,1},{6,2},{7,3},{8,140},{9,141},{1... | collective-permute-start | bytes 221192 | tf_op jit(solution)/shard_map/ppermute | solution.py:41
  75.9 3.3 %collective-permute-start.23 = (bf16[128,1152]{1,0:T(8,128)(2,1)S(1)}, bf16[128,1152]{1,0:T(8,128)(2,1)S(1)}, u32[]{:S(2)}, u32[]{:S(2)}) collective-permute-start(bf16[128,1152]{1,0:T(8,128)(2,1)S(1)} %slice.173), channel_id=1, source_target_pairs={{0,112},{1,113},{2,114},{3,115},{4,116},{5,117},{6,118},{7,119},{8... | collective-permute-start | bytes 884744 | tf_op jit(solution)/shard_map/ppermute | solution.py:41
  79.3 6.8 %collective-permute-done.23 = bf16[128,1152]{1,0:T(8,128)(2,1)S(1)} collective-permute-done((bf16[128,1152]{1,0:T(8,128)(2,1)S(1)}, bf16[128,1152]{1,0:T(8,128)(2,1)S(1)}, u32[]{:S(2)}, u32[]{:S(2)}) %collective-permute-start.23) | collective-permute-done | bytes 294944 | tf_op jit(solution)/shard_map/ppermute | solution.py:41
  86.3 9.6 %collective-permute-done.24 = bf16[128,1152]{1,0:T(8,128)(2,1)S(1)} collective-permute-done((bf16[128,1152]{1,0:T(8,128)(2,1)S(1)}, bf16[128,1152]{1,0:T(8,128)(2,1)S(1)}, u32[]{:S(2)}, u32[]{:S(2)}) %collective-permute-start.24) | collective-permute-done | bytes 294944 | tf_op jit(solution)/shard_map/ppermute | solution.py:41
  96.0 3.3 %collective-permute-start.25 = (bf16[128,1152]{1,0:T(8,128)(2,1)S(1)}, bf16[128,1152]{1,0:T(8,128)(2,1)S(1)}, u32[]{:S(2)}, u32[]{:S(2)}) collective-permute-start(bf16[128,1152]{1,0:T(8,128)(2,1)S(1)} %fusion.1), channel_id=1, source_target_pairs={{0,112},{1,113},{2,114},{3,115},{4,116},{5,117},{6,118},{7,119},{8... | collective-permute-start | bytes 884744 | tf_op jit(solution)/shard_map/ppermute | solution.py:41
  99.6 5.0 %collective-permute-done.25 = bf16[128,1152]{1,0:T(8,128)(2,1)S(1)} collective-permute-done((bf16[128,1152]{1,0:T(8,128)(2,1)S(1)}, bf16[128,1152]{1,0:T(8,128)(2,1)S(1)}, u32[]{:S(2)}, u32[]{:S(2)}) %collective-permute-start.25) | collective-permute-done | bytes 294944 | tf_op jit(solution)/shard_map/ppermute | solution.py:41
  105.6 4.3 %collective-permute-done.26 = bf16[64,1152]{1,0:T(8,128)(2,1)S(1)} collective-permute-done((bf16[64,1152]{1,0:T(8,128)(2,1)S(1)}, bf16[64,1152]{1,0:T(8,128)(2,1)S(1)}, u32[]{:S(2)}, u32[]{:S(2)}) %collective-permute-start.26) | collective-permute-done | bytes 147488 | tf_op jit(solution)/shard_map/ppermute | solution.py:41
  (96 shorter events, 23.8 us)
Async XLA Ops:
  2.7 7.4 %collective-permute-start.9 = (bf16[32,1152]{1,0:T(8,128)(2,1)S(1)}, bf16[32,1152]{1,0:T(8,128)(2,1)S(1)}, u32[]{:S(2)}, u32[]{:S(2)}) collective-permute-start(bf16[32,1152]{1,0:T(8,128)(2,1)S(1)} %get-tuple-element.8), channel_id=1, source_target_pairs={{0,4},{1,5},{2,6},{3,7},{4,0},{5,1},{6,2},{7,3},{8,140},{9,141},{1... | collective-permute-start | bytes 221192 | tf_op jit(solution)/shard_map/ppermute | solution.py:41
  5.0 7.7 %collective-permute-start.6 = (bf16[32,1152]{1,0:T(8,128)(2,1)S(1)}, bf16[32,1152]{1,0:T(8,128)(2,1)S(1)}, u32[]{:S(2)}, u32[]{:S(2)}) collective-permute-start(bf16[32,1152]{1,0:T(8,128)(2,1)S(1)} %get-tuple-element.10), channel_id=1, source_target_pairs={{0,1},{1,0},{2,3},{3,2},{4,5},{5,4},{6,7},{7,6},{8,11},{9,10},{10,... | collective-permute-start | bytes 221192 | tf_op jit(solution)/shard_map/ppermute | solution.py:41
  7.1 7.8 %collective-permute-start = (bf16[64,1152]{1,0:T(8,128)(2,1)S(1)}, bf16[64,1152]{1,0:T(8,128)(2,1)S(1)}, u32[]{:S(2)}, u32[]{:S(2)}) collective-permute-start(bf16[64,1152]{1,0:T(8,128)(2,1)S(1)} %get-tuple-element.3), channel_id=1, source_target_pairs={{0,16},{1,17},{2,18},{3,19},{4,20},{5,21},{6,22},{7,23},{8,120},{9... | collective-permute-start | bytes 442376 | tf_op jit(solution)/shard_map/ppermute | solution.py:41
  10.2 9.8 %collective-permute-start.10 = (bf16[64,1152]{1,0:T(8,128)(2,1)S(1)}, bf16[64,1152]{1,0:T(8,128)(2,1)S(1)}, u32[]{:S(2)}, u32[]{:S(2)}) collective-permute-start(bf16[64,1152]{1,0:T(8,128)(2,1)S(1)} %pad_maximum_fusion.8), channel_id=1, source_target_pairs={{0,132},{1,133},{2,134},{3,135},{4,128},{5,129},{6,130},{7,131},{8... | collective-permute-start | bytes 442376 | tf_op jit(solution)/shard_map/ppermute | solution.py:41
  12.7 8.0 %collective-permute-start.7 = (bf16[64,1152]{1,0:T(8,128)(2,1)S(1)}, bf16[64,1152]{1,0:T(8,128)(2,1)S(1)}, u32[]{:S(2)}, u32[]{:S(2)}) collective-permute-start(bf16[64,1152]{1,0:T(8,128)(2,1)S(1)} %pad_maximum_fusion.7), channel_id=1, source_target_pairs={{0,3},{1,2},{2,1},{3,0},{4,7},{5,6},{6,5},{7,4},{8,9},{9,8},{10,11... | collective-permute-start | bytes 442376 | tf_op jit(solution)/shard_map/ppermute | solution.py:41
  14.9 9.7 %collective-permute-start.1 = (bf16[128,1152]{1,0:T(8,128)(2,1)S(1)}, bf16[128,1152]{1,0:T(8,128)(2,1)S(1)}, u32[]{:S(2)}, u32[]{:S(2)}) collective-permute-start(bf16[128,1152]{1,0:T(8,128)(2,1)S(1)} %pad_maximum_fusion.4), channel_id=1, source_target_pairs={{0,112},{1,113},{2,114},{3,115},{4,116},{5,117},{6,118},{7,119},{8... | collective-permute-start | bytes 884744 | tf_op jit(solution)/shard_map/ppermute | solution.py:41
  20.0 8.1 %collective-permute-start.11 = (bf16[128,1152]{1,0:T(8,128)(2,1)S(1)}, bf16[128,1152]{1,0:T(8,128)(2,1)S(1)}, u32[]{:S(2)}, u32[]{:S(2)}) collective-permute-start(bf16[128,1152]{1,0:T(8,128)(2,1)S(1)} %pad_maximum_fusion.6), channel_id=1, source_target_pairs={{0,1},{1,0},{2,3},{3,2},{4,5},{5,4},{6,7},{7,6},{8,11},{9,10},{10,... | collective-permute-start | bytes 884744 | tf_op jit(solution)/shard_map/ppermute | solution.py:41
  20.7 6.8 %collective-permute-start.8 = (bf16[128,1152]{1,0:T(8,128)(2,1)S(1)}, bf16[128,1152]{1,0:T(8,128)(2,1)S(1)}, u32[]{:S(2)}, u32[]{:S(2)}) collective-permute-start(bf16[128,1152]{1,0:T(8,128)(2,1)S(1)} %pad_maximum_fusion.5), channel_id=1, source_target_pairs={{0,4},{1,5},{2,6},{3,7},{4,0},{5,1},{6,2},{7,3},{8,140},{9,141},{1... | collective-permute-start | bytes 884744 | tf_op jit(solution)/shard_map/ppermute | solution.py:41
  24.7 16.8 %collective-permute-start.4 = (bf16[256,1152]{1,0:T(8,128)(2,1)S(1)}, bf16[256,1152]{1,0:T(8,128)(2,1)S(1)}, u32[]{:S(2)}, u32[]{:S(2)}) collective-permute-start(bf16[256,1152]{1,0:T(8,128)(2,1)S(1)} %pad_maximum_fusion), channel_id=1, source_target_pairs={{0,8},{1,9},{2,10},{3,11},{4,12},{5,13},{6,14},{7,15},{8,0},{9,1},... | collective-permute-start | bytes 1769480 | tf_op jit(solution)/shard_map/ppermute | solution.py:41
  24.8 6.8 %collective-permute-start.2 = (bf16[128,1152]{1,0:T(8,128)(2,1)S(1)}, bf16[128,1152]{1,0:T(8,128)(2,1)S(1)}, u32[]{:S(2)}, u32[]{:S(2)}) collective-permute-start(bf16[128,1152]{1,0:T(8,128)(2,1)S(1)} %collective-permute-done.1), channel_id=1, source_target_pairs={{0,16},{1,17},{2,18},{3,19},{4,20},{5,21},{6,22},{7,23},{8,120},{9... | collective-permute-start | bytes 884744 | tf_op jit(solution)/shard_map/ppermute | solution.py:41
  27.6 14.0 %collective-permute-start.12 = (bf16[256,1152]{1,0:T(8,128)(2,1)S(1)}, bf16[256,1152]{1,0:T(8,128)(2,1)S(1)}, u32[]{:S(2)}, u32[]{:S(2)}) collective-permute-start(bf16[256,1152]{1,0:T(8,128)(2,1)S(1)} %pad_maximum_fusion.2), channel_id=1, source_target_pairs={{0,132},{1,133},{2,134},{3,135},{4,128},{5,129},{6,130},{7,131},{8... | collective-permute-start | bytes 1769480 | tf_op jit(solution)/shard_map/ppermute | solution.py:41
  28.2 13.4 %collective-permute-start.13 = (bf16[256,1152]{1,0:T(8,128)(2,1)S(1)}, bf16[256,1152]{1,0:T(8,128)(2,1)S(1)}, u32[]{:S(2)}, u32[]{:S(2)}) collective-permute-start(bf16[256,1152]{1,0:T(8,128)(2,1)S(1)} %pad_maximum_fusion.3), channel_id=1, source_target_pairs={{0,3},{1,2},{2,1},{3,0},{4,7},{5,6},{6,5},{7,4},{8,9},{9,8},{10,11... | collective-permute-start | bytes 1769480 | tf_op jit(solution)/shard_map/ppermute | solution.py:41
  31.6 9.7 %collective-permute-start.3 = (bf16[128,1152]{1,0:T(8,128)(2,1)S(1)}, bf16[128,1152]{1,0:T(8,128)(2,1)S(1)}, u32[]{:S(2)}, u32[]{:S(2)}) collective-permute-start(bf16[128,1152]{1,0:T(8,128)(2,1)S(1)} %collective-permute-done.2), channel_id=1, source_target_pairs={{0,112},{1,113},{2,114},{3,115},{4,116},{5,117},{6,118},{7,119},{8... | collective-permute-start | bytes 884744 | tf_op jit(solution)/shard_map/ppermute | solution.py:41
  47.0 10.2 %collective-permute-start.14 = (bf16[256,1152]{1,0:T(8,128)(2,1)S(1)}, bf16[256,1152]{1,0:T(8,128)(2,1)S(1)}, u32[]{:S(2)}, u32[]{:S(2)}) collective-permute-start(bf16[256,1152]{1,0:T(8,128)(2,1)S(1)} %get-tuple-element.6), channel_id=1, source_target_pairs={{0,132},{1,133},{2,134},{3,135},{4,128},{5,129},{6,130},{7,131},{8... | collective-permute-start | bytes 1769480 | tf_op jit(solution)/shard_map/ppermute | solution.py:41
  49.3 11.1 %collective-permute-start.18 = (bf16[256,1152]{1,0:T(8,128)(2,1)S(1)}, bf16[256,1152]{1,0:T(8,128)(2,1)S(1)}, u32[]{:S(2)}, u32[]{:S(2)}) collective-permute-start(bf16[256,1152]{1,0:T(8,128)(2,1)S(1)} %get-tuple-element.7), channel_id=1, source_target_pairs={{0,3},{1,2},{2,1},{3,0},{4,7},{5,6},{6,5},{7,4},{8,9},{9,8},{10,11... | collective-permute-start | bytes 1769480 | tf_op jit(solution)/shard_map/ppermute | solution.py:41
  60.6 6.8 %collective-permute-start.19 = (bf16[128,1152]{1,0:T(8,128)(2,1)S(1)}, bf16[128,1152]{1,0:T(8,128)(2,1)S(1)}, u32[]{:S(2)}, u32[]{:S(2)}) collective-permute-start(bf16[128,1152]{1,0:T(8,128)(2,1)S(1)} %slice.174), channel_id=1, source_target_pairs={{0,1},{1,0},{2,3},{3,2},{4,5},{5,4},{6,7},{7,6},{8,11},{9,10},{10,... | collective-permute-start | bytes 884744 | tf_op jit(solution)/shard_map/ppermute | solution.py:41
  62.4 13.2 %collective-permute-start.22 = (bf16[512,1152]{1,0:T(8,128)(2,1)S(1)}, bf16[512,1152]{1,0:T(8,128)(2,1)S(1)}, u32[]{:S(2)}, u32[]{:S(2)}) collective-permute-start(bf16[512,1152]{1,0:T(8,128)(2,1)S(1)} %slice.172), channel_id=1, source_target_pairs={{0,8},{1,9},{2,10},{3,11},{4,12},{5,13},{6,14},{7,15},{8,0},{9,1},... | collective-permute-start | bytes 3538952 | tf_op jit(solution)/shard_map/ppermute | solution.py:41
  62.5 8.3 %collective-permute-start.15 = (bf16[128,1152]{1,0:T(8,128)(2,1)S(1)}, bf16[128,1152]{1,0:T(8,128)(2,1)S(1)}, u32[]{:S(2)}, u32[]{:S(2)}) collective-permute-start(bf16[128,1152]{1,0:T(8,128)(2,1)S(1)} %slice.175), channel_id=1, source_target_pairs={{0,4},{1,5},{2,6},{3,7},{4,0},{5,1},{6,2},{7,3},{8,140},{9,141},{1... | collective-permute-start | bytes 884744 | tf_op jit(solution)/shard_map/ppermute | solution.py:41
  70.9 8.3 %collective-permute-start.16 = (bf16[64,1152]{1,0:T(8,128)(2,1)S(1)}, bf16[64,1152]{1,0:T(8,128)(2,1)S(1)}, u32[]{:S(2)}, u32[]{:S(2)}) collective-permute-start(bf16[64,1152]{1,0:T(8,128)(2,1)S(1)} %slice.178), channel_id=1, source_target_pairs={{0,3},{1,2},{2,1},{3,0},{4,7},{5,6},{6,5},{7,4},{8,9},{9,8},{10,11... | collective-permute-start | bytes 442376 | tf_op jit(solution)/shard_map/ppermute | solution.py:41
  72.8 13.5 %collective-permute-start.21 = (bf16[32,1152]{1,0:T(8,128)(2,1)S(1)}, bf16[32,1152]{1,0:T(8,128)(2,1)S(1)}, u32[]{:S(2)}, u32[]{:S(2)}) collective-permute-start(bf16[32,1152]{1,0:T(8,128)(2,1)S(1)} %slice.179), channel_id=1, source_target_pairs={{0,4},{1,5},{2,6},{3,7},{4,0},{5,1},{6,2},{7,3},{8,140},{9,141},{1... | collective-permute-start | bytes 221192 | tf_op jit(solution)/shard_map/ppermute | solution.py:41
  75.9 10.2 %collective-permute-start.23 = (bf16[128,1152]{1,0:T(8,128)(2,1)S(1)}, bf16[128,1152]{1,0:T(8,128)(2,1)S(1)}, u32[]{:S(2)}, u32[]{:S(2)}) collective-permute-start(bf16[128,1152]{1,0:T(8,128)(2,1)S(1)} %slice.173), channel_id=1, source_target_pairs={{0,112},{1,113},{2,114},{3,115},{4,116},{5,117},{6,118},{7,119},{8... | collective-permute-start | bytes 884744 | tf_op jit(solution)/shard_map/ppermute | solution.py:41
  79.2 20.1 %collective-permute-start.17 = (bf16[32,1152]{1,0:T(8,128)(2,1)S(1)}, bf16[32,1152]{1,0:T(8,128)(2,1)S(1)}, u32[]{:S(2)}, u32[]{:S(2)}) collective-permute-start(bf16[32,1152]{1,0:T(8,128)(2,1)S(1)} %slice.180), channel_id=1, source_target_pairs={{0,1},{1,0},{2,3},{3,2},{4,5},{5,4},{6,7},{7,6},{8,11},{9,10},{10,... | collective-permute-start | bytes 221192 | tf_op jit(solution)/shard_map/ppermute | solution.py:41
  86.2 9.8 %collective-permute-start.24 = (bf16[128,1152]{1,0:T(8,128)(2,1)S(1)}, bf16[128,1152]{1,0:T(8,128)(2,1)S(1)}, u32[]{:S(2)}, u32[]{:S(2)}) collective-permute-start(bf16[128,1152]{1,0:T(8,128)(2,1)S(1)} %fusion), channel_id=1, source_target_pairs={{0,16},{1,17},{2,18},{3,19},{4,20},{5,21},{6,22},{7,23},{8,120},{9... | collective-permute-start | bytes 884744 | tf_op jit(solution)/shard_map/ppermute | solution.py:41
  96.0 8.6 %collective-permute-start.25 = (bf16[128,1152]{1,0:T(8,128)(2,1)S(1)}, bf16[128,1152]{1,0:T(8,128)(2,1)S(1)}, u32[]{:S(2)}, u32[]{:S(2)}) collective-permute-start(bf16[128,1152]{1,0:T(8,128)(2,1)S(1)} %fusion.1), channel_id=1, source_target_pairs={{0,112},{1,113},{2,114},{3,115},{4,116},{5,117},{6,118},{7,119},{8... | collective-permute-start | bytes 884744 | tf_op jit(solution)/shard_map/ppermute | solution.py:41
  (5 other events, 36.1 us)

commit v2 on v1

v2 whole, which is shorter than its diff:
```python
import functools

import jax
import jax.numpy as jnp
from jax import lax
from jax.experimental import pallas as pl
from jax.experimental.pallas import tpu as pltpu
from jax.sharding import PartitionSpec as P

epsilon = 1e-06
log2_e = 1.4426950408889634
AXES = ("blk", "grp")


def place(x, y, z, core):
    return ((((y >> 1) * 8 + z) * 2 + core) * 2 + (y & 1)) * 4 + x


def partner(position, size, first):
    step = 1 if (position % 2 == 0) == first else -1
    return (position + step) % size


def pairs_of(axis, first):
    pairs = []
    for x in range(4):
        for y in range(4):
            for z in range(8):
                for core in range(2):
                    side = first == (core == 0)
                    to = [x, y, z, core]
                    if axis == "x":
                        to[0] = partner(x, 4, side)
                    elif axis == "y":
                        to[1] = partner(y, 4, side)
                    elif axis == "z":
                        to[2] = partner(z, 8, side)
                    else:
                        to[3] = 1 - core
                    pairs.append((place(x, y, z, core), place(*to)))
    return sorted(pairs)


def exchange(axis, first=True):
    hops = [dict(pairs_of(one, first)) for one in ((axis,) if axis == "core" else axis)]
    pairs = []
    for source in sorted(hops[0]):
        target = source
        for hop in hops:
            target = hop[target]
        pairs.append((source, target))
    return lambda value: lax.ppermute(value, AXES, pairs)


def unit_rows(values):
    widened = values.astype(jnp.float32)
    inverse = lax.rsqrt(jnp.sum(widened * widened, axis=1, keepdims=True) + epsilon)
    return (widened * inverse, inverse)


def through_norm(unit_part, inverse, along_unit):
    projected = jnp.sum(unit_part * along_unit, axis=1, keepdims=True)
    return (along_unit - unit_part * projected) * inverse


def rounded(value):
    return value.astype(jnp.bfloat16)


def widened(value):
    return value.astype(jnp.float32)


def join(*parts):
    return jnp.concatenate(parts, axis=0)


def send_kernel(rows, *rest):
    rest[-1][...] = rounded(unit_rows(rows[...])[0])


def send_rows(rows, *earlier):
    whole = pl.BlockSpec(memory_space=pltpu.VMEM)
    return pl.pallas_call(
        send_kernel,
        out_shape=jax.ShapeDtypeStruct(rows.shape, jnp.bfloat16),
        in_specs=[whole] * (1 + len(earlier)),
        out_specs=whole,
        compiler_params=pltpu.CompilerParams(vmem_limit_bytes=4 * 2**20),
    )(rows, *earlier)


def grad_kernel(factor, rows, others, sums, *rest):
    *arrived, grad = rest
    unit, inverse = unit_rows(rows[...])
    other_send = widened(rounded(unit_rows(others[...])[0]))
    total = sums[...] - factor[0] * other_send
    for part in arrived:
        total = total + widened(part[...])
    grad[...] = through_norm(unit, inverse, total)


def grad_rows(factor, rows, others, sums, *arrived):
    whole = pl.BlockSpec(memory_space=pltpu.VMEM)
    return pl.pallas_call(
        grad_kernel,
        out_shape=jax.ShapeDtypeStruct(rows.shape, jnp.float32),
        in_specs=[pl.BlockSpec(memory_space=pltpu.SMEM)] + [whole] * (3 + len(arrived)),
        out_specs=whole,
        compiler_params=pltpu.CompilerParams(vmem_limit_bytes=4 * 2**20),
    )(factor, rows, others, sums, *arrived)


def weights_of(factor, offset, texts, images):
    logits = lax.dot_general(
        texts[...], images[...], (((1,), (1,)), ((), ())), preferred_element_type=jnp.float32
    )
    decay = jnp.exp2(logits * (factor * -log2_e) + offset * -log2_e)
    return rounded(factor / (1.0 + decay))


def for_images(weights, texts):
    return lax.dot_general(
        weights, texts[...], (((0,), (0,)), ((), ())), preferred_element_type=jnp.float32
    )


def for_texts(weights, images):
    return jnp.dot(weights, images[...], preferred_element_type=jnp.float32)


def rows_of(*refs):
    return jnp.concatenate([ref[...] for ref in refs], axis=0)


def columns_of(*parts):
    return jnp.concatenate(parts, axis=1)


def weight_kernel(count, scale, bias, *refs):
    *inputs, weights = refs
    weights[...] = weights_of(
        scale[0], bias[0], rows_of(*inputs[:count]), rows_of(*inputs[count:])
    )


def corner_kernel(scale, bias, own_a, sib_a, own_b, sib_b, quad, part_x, part_y, part_d,
                  w_aq, w_axy, w_bqxy, w_d, sums_own, sums_own_b, send):
    a, b = own_a.shape[0], own_b.shape[0]
    w_d[...] = weights_of(scale[0], bias[0], rows_of(own_a, sib_a, own_b, sib_b), part_d)
    images = rows_of(quad, part_x, part_y, part_d)
    late = w_d[pl.ds(2 * a, 2 * b)]
    total = for_texts(columns_of(w_bqxy[...], late), images)
    sums_own_b[...] = total[:b]
    send[pl.ds(0, b)] = rounded(total[b:])
    late = w_d[pl.ds(0, 2 * a)]
    total = for_texts(columns_of(w_aq[...], w_axy[...], late), images)
    sums_own[...] = total[:a]
    send[pl.ds(b, a)] = rounded(total[a:])


def sibling_kernel(scale, bias, sib_c, quad, part_x, part_y, part_d, weights, send):
    images = rows_of(quad, part_x, part_y, part_d)
    weights[...] = weights_of(scale[0], bias[0], sib_c, images)
    send[...] = rounded(for_texts(weights[...], images))


def text_kernel(weights, quad, part_x, part_y, part_d, sums):
    sums[...] = for_texts(weights[...], rows_of(quad, part_x, part_y, part_d))


def image_kernel(count, *refs):
    *inputs, sums = refs
    total = for_images(rows_of(*inputs[:count]), rows_of(*inputs[count:]))
    sums[...] = total.astype(sums.dtype)


def on_device(kernel, outputs, *operands, scalars=0, products=0):
    vmem = pl.BlockSpec(memory_space=pltpu.VMEM)
    smem = pl.BlockSpec(memory_space=pltpu.SMEM)
    width = operands[-1].shape[-1]
    return pl.pallas_call(
        kernel,
        out_shape=[jax.ShapeDtypeStruct(shape, kind) for shape, kind in outputs],
        in_specs=[smem] * scalars + [vmem] * (len(operands) - scalars),
        out_specs=[vmem] * len(outputs),
        compiler_params=pltpu.CompilerParams(vmem_limit_bytes=16 * 2**20),
        cost_estimate=pl.CostEstimate(
            flops=2 * width * products, bytes_accessed=0, transcendentals=0
        ),
    )(*operands)


def after(value, *others):
    return lax.optimization_barrier((value,) + others)[0]


def local(images, texts, logit_scale, logit_bias):
    x1, y1, d1 = exchange("x", True), exchange("y", True), exchange("xy", True)
    x2, y2, d2 = exchange("x", False), exchange("y", False), exchange("xy", False)
    z1, z2 = exchange("z", True), exchange("z", False)
    sibling = exchange("core")
    f32, bf16 = jnp.float32, jnp.bfloat16
    n, d = images.shape
    a, b, q = 4 * n, 2 * n, 4 * n
    scalars = (logit_scale, logit_bias)
    text_send = send_rows(texts)
    image_send = send_rows(images, text_send)

    def weigh(some_texts, some_images, share=1):
        m = sum(v.shape[0] for v in some_texts)
        k = sum(v.shape[0] for v in some_images)
        return on_device(
            functools.partial(weight_kernel, len(some_texts)), [((m, k), bf16)],
            *scalars, *some_texts, *some_images, scalars=2, products=share * m * k,
        )[0]

    r1 = z1(text_send)
    quad = join(image_send, x1(image_send), y1(image_send), d1(image_send))
    near = join(text_send, r1)
    r2 = z2(near)
    part_x, part_y, part_d = x2(quad), y2(quad), d2(quad)
    r3 = z1(r2)
    own_a = join(near, r2)
    sib_a = sibling(own_a)
    w_aq = weigh((own_a, sib_a), (quad,))
    w_axy = weigh((own_a, sib_a), (part_x, part_y), share=40)
    r3 = after(r3, w_aq, w_axy)
    r4 = z2(r3)
    sib_b = sibling(r3)
    w_bqxy = weigh((r3, sib_b), (quad, part_x, part_y))
    w_d, sums_own, sums_own_b, send_ab = on_device(
        corner_kernel,
        [((2 * a + 2 * b, q), bf16), ((a, d), f32), ((b, d), f32), ((a + b, d), bf16)],
        *scalars, own_a, sib_a, r3, sib_b, quad, part_x, part_y, part_d, w_aq, w_axy, w_bqxy,
        scalars=2, products=40 * 3 * q * (a + b),
    )
    r4 = after(r4, send_ab)
    back_ab = sibling(send_ab)
    all_images = (quad, part_x, part_y, part_d)
    sib_c = sibling(r4)
    w_own = weigh((r4,), all_images)
    w_sib, send_c = on_device(
        sibling_kernel, [((b, 4 * q), bf16), ((b, d), bf16)], *scalars, sib_c, *all_images,
        scalars=2, products=2 * b * 4 * q,
    )
    (sums_own_c,) = on_device(
        text_kernel, [((b, d), f32)], w_own, *all_images, products=b * 4 * q
    )
    s4 = rounded(sums_own_c + widened(sibling(send_c)))
    all_texts = (own_a, sib_a, r3, sib_b, r4, sib_c)

    def image_part(kind, *blocks):
        return on_device(
            functools.partial(image_kernel, len(blocks)), [((q, d), kind)],
            *blocks, *all_texts, products=q * 8 * q // 2,
        )[0]

    def late(index, *others):
        span = slice(index * q, (index + 1) * q)
        return after(w_own[:, span], *others), w_sib[:, span]

    back_d = d2(image_part(bf16, w_d, *late(3)))
    back_x = x2(image_part(bf16, w_axy[:, :q], w_bqxy[:, q : 2 * q], *late(1, s4)))
    back_y = y2(image_part(bf16, w_axy[:, q:], w_bqxy[:, 2 * q :], *late(2, s4)))
    s4 = z2(s4)
    quad_sums = image_part(f32, w_aq, w_bqxy[:, :q], *late(0, s4))
    s3 = sums_own_b + widened(back_ab[:b]) + widened(s4)
    near_sums = sums_own + widened(back_ab[b:])
    s2 = near_sums[2 * n :] + widened(z1(rounded(s3)))
    s01 = near_sums[: 2 * n] + widened(z2(rounded(s2)))
    quad_sums = quad_sums + widened(back_d) + widened(back_x) + widened(back_y)
    text_grad = grad_rows(logit_scale, texts, images, s01[:n], z1(rounded(s01[n:])))
    image_grad = grad_rows(
        logit_scale,
        images,
        texts,
        quad_sums[:n],
        d1(rounded(quad_sums[3 * n :])),
        x1(rounded(quad_sums[n : 2 * n])),
        y1(rounded(quad_sums[2 * n : 3 * n])),
    )
    return (image_grad, text_grad)


def solution(mesh):
    in_specs = (P(AXES, None), P(AXES, None), P(), P())
    out_specs = (P(AXES, None), P(AXES, None))
    return jax.shard_map(local, mesh=mesh, in_specs=in_specs, out_specs=out_specs, check_vma=False)
```

time: 111 us -> 86.9 us (0.78)
  the two profiles are of different devices: /device:TPU:8 before, /device:TPU:24 now
where the time goes in v2:
time: 86.9 us; the launch traced here: 86.8 us
  starting transfers between devices  41.5 us (48%)
  waiting for transfers between devices  26.3 us (30%)
  Pallas kernels  14 us (16%)
  between operations  2.21 us (3%)
  local copies, waits for them, and re-layouts  2.02 us (2%)
    ppermute x25, starting transfers between devices, exchange(): return lambda value: lax.ppermute(value, AXES, pairs)  41.5 us
    ppermute x25, waiting for transfers between devices, exchange(): return lambda value: lax.ppermute(value, AXES, pairs)  26.3 us
    pallas_call x11, Pallas kernels, on_device(): pl.pallas_call(kernel, out_shape=[jax.ShapeDtypeStruct(shape, kind) for s...  11.8 us
    pallas_call x2, Pallas kernels, grad_rows(): pl.pallas_call(grad_kernel, out_shape=jax.ShapeDtypeStruct(rows.shape, jn...  2.03 us
    unnamed x8, local copies, waits for them, and re-layouts  1.82 us
  transfers between devices with their start and end apart: 25, of which 12 were waited for; matrix products, arithmetic and copies ran while one was open for 1% of the time, Pallas kernels for 15%

profile of v2, /device:TPU:24, one launch (start us, length us, event | category | flops | bytes accessed | tf_op | source)
XLA Modules:
  0.0 86.8 jit_solution(5650332273094388281)
XLA Ops:
  1.7 2.0 %collective-permute-start = (bf16[64,1152]{1,0:T(8,128)(2,1)S(1)}, bf16[64,1152]{1,0:T(8,128)(2,1)S(1)}, u32[]{:S(2)}, u32[]{:S(2)}) collective-permute-start(bf16[64,1152]{1,0:T(8,128)(2,1)S(1)} %shard_map.59.rest_0_), channel_id=1, source_target_pairs={{0,16},{1,17},{2,18},{3,19},{4,20},{5,21},{6,22},{7,23},{8,120},{9... | collective-permute-start | bytes 442376 | tf_op jit(solution)/shard_map/ppermute | solution.py:52
  4.7 1.6 %collective-permute-start.3 = (bf16[64,1152]{1,0:T(8,128)(2,1)S(1)}, bf16[64,1152]{1,0:T(8,128)(2,1)S(1)}, u32[]{:S(2)}, u32[]{:S(2)}) collective-permute-start(bf16[64,1152]{1,0:T(8,128)(2,1)S(1)} %shard_map.60), channel_id=1, source_target_pairs={{0,1},{1,0},{2,3},{3,2},{4,5},{5,4},{6,7},{7,6},{8,11},{9,10},{10,... | collective-permute-start | bytes 442376 | tf_op jit(solution)/shard_map/ppermute | solution.py:52
  7.0 1.3 %collective-permute-start.5 = (bf16[64,1152]{1,0:T(8,128)(2,1)S(1)}, bf16[64,1152]{1,0:T(8,128)(2,1)S(1)}, u32[]{:S(2)}, u32[]{:S(2)}) collective-permute-start(bf16[64,1152]{1,0:T(8,128)(2,1)S(1)} %shard_map.60), channel_id=1, source_target_pairs={{0,5},{1,4},{2,7},{3,6},{4,1},{5,0},{6,3},{7,2},{8,143},{9,142},{1... | collective-permute-start | bytes 442376 | tf_op jit(solution)/shard_map/ppermute | solution.py:52
  8.3 5.0 %collective-permute-start.1 = (bf16[128,1152]{1,0:T(8,128)(2,1)S(1)}, bf16[128,1152]{1,0:T(8,128)(2,1)S(1)}, u32[]{:S(2)}, u32[]{:S(2)}) collective-permute-start(bf16[128,1152]{1,0:T(8,128)(2,1)S(1)} %pad_maximum_fusion.2), channel_id=1, source_target_pairs={{0,112},{1,113},{2,114},{3,115},{4,116},{5,117},{6,118},{7,119},{8... | collective-permute-start | bytes 884744 | tf_op jit(solution)/shard_map/ppermute | solution.py:52
  13.4 2.8 %collective-permute-start.7 = (bf16[256,1152]{1,0:T(8,128)(2,1)S(1)}, bf16[256,1152]{1,0:T(8,128)(2,1)S(1)}, u32[]{:S(2)}, u32[]{:S(2)}) collective-permute-start(bf16[256,1152]{1,0:T(8,128)(2,1)S(1)} %pad_maximum_fusion.1.refs_2_.quad.refs_1_), channel_id=1, source_target_pairs={{0,3},{1,2},{2,1},{3,0},{4,7},{5,6},{6,5},{7,4},{8,9},{9,8},{10,11... | collective-permute-start | bytes 1769480 | tf_op jit(solution)/shard_map/ppermute | solution.py:52
  16.5 1.6 %collective-permute-done.1 = bf16[128,1152]{1,0:T(8,128)(2,1)S(1)} collective-permute-done((bf16[128,1152]{1,0:T(8,128)(2,1)S(1)}, bf16[128,1152]{1,0:T(8,128)(2,1)S(1)}, u32[]{:S(2)}, u32[]{:S(2)}) %collective-permute-start.1) | collective-permute-done | bytes 294944 | tf_op jit(solution)/shard_map/ppermute | solution.py:52
  18.1 1.4 %collective-permute-start.2 = (bf16[256,1152]{1,0:T(8,128)(2,1)S(1)}, bf16[256,1152]{1,0:T(8,128)(2,1)S(1)}, u32[]{:S(2)}, u32[]{:S(2)}) collective-permute-start(bf16[256,1152]{1,0:T(8,128)(2,1)S(1)} %pad_maximum_fusion.refs_0_.own_a.refs_4_.refs_3_), channel_id=1, source_target_pairs={{0,8},{1,9},{2,10},{3,11},{4,12},{5,13},{6,14},{7,15},{8,0},{9,1},... | collective-permute-start | bytes 1769480 | tf_op jit(solution)/shard_map/ppermute | solution.py:52
  20.8 2.6 %collective-permute-start.11 = (bf16[256,1152]{1,0:T(8,128)(2,1)S(1)}, bf16[256,1152]{1,0:T(8,128)(2,1)S(1)}, u32[]{:S(2)}, u32[]{:S(2)}) collective-permute-start(bf16[256,1152]{1,0:T(8,128)(2,1)S(1)} %pad_maximum_fusion.1.refs_2_.quad.refs_1_), channel_id=1, source_target_pairs={{0,135},{1,134},{2,133},{3,132},{4,131},{5,130},{6,129},{7,128},{8... | collective-permute-start | bytes 1769480 | tf_op jit(solution)/shard_map/ppermute | solution.py:52
  23.6 1.2 %collective-permute-done.7.refs_2_.refs_3_.part_x = bf16[256,1152]{1,0:T(8,128)(2,1)S(1)} collective-permute-done((bf16[256,1152]{1,0:T(8,128)(2,1)S(1)}, bf16[256,1152]{1,0:T(8,128)(2,1)S(1)}, u32[]{:S(2)}, u32[]{:S(2)}) %collective-permute-start.7) | collective-permute-done | bytes 589856 | tf_op jit(solution)/shard_map/ppermute | solution.py:52
  24.9 2.5 %collective-permute-done.8.refs_3_.refs_4_.part_y = bf16[256,1152]{1,0:T(8,128)(2,1)S(1)} collective-permute-done((bf16[256,1152]{1,0:T(8,128)(2,1)S(1)}, bf16[256,1152]{1,0:T(8,128)(2,1)S(1)}, u32[]{:S(2)}, u32[]{:S(2)}) %collective-permute-start.8) | collective-permute-done | bytes 589856 | tf_op jit(solution)/shard_map/ppermute | solution.py:52
  28.9 1.1 %collective-permute-done.6.refs_0_.own_b.refs_6_.refs_5_ = bf16[128,1152]{1,0:T(8,128)(2,1)S(1)} collective-permute-done((bf16[128,1152]{1,0:T(8,128)(2,1)S(1)}, bf16[128,1152]{1,0:T(8,128)(2,1)S(1)}, u32[]{:S(2)}, u32[]{:S(2)}) %collective-permute-start.6) | collective-permute-done | bytes 294944 | tf_op jit(solution)/shard_map/ppermute | solution.py:52
  30.1 5.3 %collective-permute-start.9 = (bf16[128,1152]{1,0:T(8,128)(2,1)S(1)}, bf16[128,1152]{1,0:T(8,128)(2,1)S(1)}, u32[]{:S(2)}, u32[]{:S(2)}) collective-permute-start(bf16[128,1152]{1,0:T(8,128)(2,1)S(1)} %collective-permute-done.6.refs_0_.own_b.refs_6_.refs_5_), channel_id=1, source_target_pairs={{0,8},{1,9},{2,10},{3,11},{4,12},{5,13},{6,14},{7,15},{8,0},{9,1},... | collective-permute-start | bytes 884744 | tf_op jit(solution)/shard_map/ppermute | solution.py:52
  35.4 4.1 %collective-permute-start.10 = (bf16[128,1152]{1,0:T(8,128)(2,1)S(1)}, bf16[128,1152]{1,0:T(8,128)(2,1)S(1)}, u32[]{:S(2)}, u32[]{:S(2)}) collective-permute-start(bf16[128,1152]{1,0:T(8,128)(2,1)S(1)} %collective-permute-done.6.refs_0_.own_b.refs_6_.refs_5_), channel_id=1, source_target_pairs={{0,112},{1,113},{2,114},{3,115},{4,116},{5,117},{6,118},{7,119},{8... | collective-permute-start | bytes 884744 | tf_op jit(solution)/shard_map/ppermute | solution.py:52
  40.2 3.1 %shard_map.64 = (bf16[768,256]{1,0:T(8,128)(2,1)S(1)}, f32[256,1152]{1,0:T(8,128)S(1)}, f32[128,1152]{1,0:T(8,128)S(1)}, bf16[384,1152]{1,0:T(8,128)(2,1)S(1)}) custom-call(f32[1]{0:T(128)S(6)} %copy.6.scale.factor, f32[1]{0:T(128)S(6)} %copy.7.bias, bf16[256,1152]{1,0:T(8,128)(2,1)S(1)} %pad_maximum_fusion.refs_0_.own_a.refs_4_.refs_3_, ...), custom_call_target="tpu_custom_call" | custom-call | flops 18119393280 | tf_op jit(solution)/shard_map/pallas_call | solution.py:182
  45.9 1.3 %shard_map.67 = (bf16[128,1024]{1,0:T(8,128)(2,1)S(1)}, bf16[128,1152]{1,0:T(8,128)(2,1)S(1)}) custom-call(f32[1]{0:T(128)S(6)} %copy.6.scale.factor, f32[1]{0:T(128)S(6)} %copy.7.bias, bf16[128,1152]{1,0:T(8,128)(2,1)S(1)} %collective-permute-done.12.sib_c.refs_9_.refs_8_, bf16[256,1152]{1,0:T(8,128)(2,1)S(1)} %pad_maximum_fusion.1.refs_2_.quad.refs_1_, ...), custom_call_target="tpu_custom_call" | custom-call | flops 603979776 | tf_op jit(solution)/shard_map/pallas_call | solution.py:182
  49.0 3.3 %collective-permute-start.14 = (bf16[128,1152]{1,0:T(8,128)(2,1)S(1)}, bf16[128,1152]{1,0:T(8,128)(2,1)S(1)}, u32[]{:S(2)}, u32[]{:S(2)}) collective-permute-start(bf16[128,1152]{1,0:T(8,128)(2,1)S(1)} %add_convert_fusion.1), channel_id=1, source_target_pairs={{0,112},{1,113},{2,114},{3,115},{4,116},{5,117},{6,118},{7,119},{8... | collective-permute-start | bytes 884744 | tf_op jit(solution)/shard_map/ppermute | solution.py:52
  54.2 3.8 %collective-permute-start.16 = (bf16[256,1152]{1,0:T(8,128)(2,1)S(1)}, bf16[256,1152]{1,0:T(8,128)(2,1)S(1)}, u32[]{:S(2)}, u32[]{:S(2)}) collective-permute-start(bf16[256,1152]{1,0:T(8,128)(2,1)S(1)} %shard_map.70), channel_id=1, source_target_pairs={{0,3},{1,2},{2,1},{3,0},{4,7},{5,6},{6,5},{7,4},{8,9},{9,8},{10,11... | collective-permute-start | bytes 1769480 | tf_op jit(solution)/shard_map/ppermute | solution.py:52
  58.9 2.3 %collective-permute-start.17 = (bf16[256,1152]{1,0:T(8,128)(2,1)S(1)}, bf16[256,1152]{1,0:T(8,128)(2,1)S(1)}, u32[]{:S(2)}, u32[]{:S(2)}) collective-permute-start(bf16[256,1152]{1,0:T(8,128)(2,1)S(1)} %shard_map.71), channel_id=1, source_target_pairs={{0,132},{1,133},{2,134},{3,135},{4,128},{5,129},{6,130},{7,131},{8... | collective-permute-start | bytes 1769480 | tf_op jit(solution)/shard_map/ppermute | solution.py:52
  62.3 8.5 %collective-permute-done.22 = bf16[128,1152]{1,0:T(8,128)(2,1)S(1)} collective-permute-done((bf16[128,1152]{1,0:T(8,128)(2,1)S(1)}, bf16[128,1152]{1,0:T(8,128)(2,1)S(1)}, u32[]{:S(2)}, u32[]{:S(2)}) %collective-permute-start.22) | collective-permute-done | bytes 294944 | tf_op jit(solution)/shard_map/ppermute | solution.py:52
  71.2 1.6 %collective-permute-done.17 = bf16[256,1152]{1,0:T(8,128)(2,1)S(1)} collective-permute-done((bf16[256,1152]{1,0:T(8,128)(2,1)S(1)}, bf16[256,1152]{1,0:T(8,128)(2,1)S(1)}, u32[]{:S(2)}, u32[]{:S(2)}) %collective-permute-start.17) | collective-permute-done | bytes 589856 | tf_op jit(solution)/shard_map/ppermute | solution.py:52
  73.5 3.2 %collective-permute-start.20 = (bf16[64,1152]{1,0:T(8,128)(2,1)S(1)}, bf16[64,1152]{1,0:T(8,128)(2,1)S(1)}, u32[]{:S(2)}, u32[]{:S(2)}) collective-permute-start(bf16[64,1152]{1,0:T(8,128)(2,1)S(1)} %get-tuple-element.26), channel_id=1, source_target_pairs={{0,4},{1,5},{2,6},{3,7},{4,0},{5,1},{6,2},{7,3},{8,140},{9,141},{1... | collective-permute-start | bytes 442376 | tf_op jit(solution)/shard_map/ppermute | solution.py:52
  76.7 3.7 %collective-permute-done.23 = bf16[128,1152]{1,0:T(8,128)(2,1)S(1)} collective-permute-done((bf16[128,1152]{1,0:T(8,128)(2,1)S(1)}, bf16[128,1152]{1,0:T(8,128)(2,1)S(1)}, u32[]{:S(2)}, u32[]{:S(2)}) %collective-permute-start.23) | collective-permute-done | bytes 294944 | tf_op jit(solution)/shard_map/ppermute | solution.py:52
  80.8 1.0 %shard_map.72 = f32[64,1152]{1,0:T(8,128)} custom-call(f32[1]{0:T(128)S(6)} %copy.6.scale.factor, bf16[64,1152]{1,0:T(8,128)(2,1)S(1)} %copy-done.1, bf16[64,1152]{1,0:T(8,128)(2,1)S(1)} %copy-done.3, f32[64,1152]{1,0:T(8,128)S(1)} %slice.105.sums, bf16[64,1152]{1,0:T(8,128)(2,1)S(1)} %collective-permute-done.18.rest_0_, ...), custom_call_target="tpu_custom_call" | custom-call | tf_op jit(solution)/shard_map/pallas_call | solution.py:105
  81.9 3.9 %collective-permute-done.24.rest_0_ = bf16[64,1152]{1,0:T(8,128)(2,1)S(1)} collective-permute-done((bf16[64,1152]{1,0:T(8,128)(2,1)S(1)}, bf16[64,1152]{1,0:T(8,128)(2,1)S(1)}, u32[]{:S(2)}, u32[]{:S(2)}) %collective-permute-start.24) | collective-permute-done | bytes 147488 | tf_op jit(solution)/shard_map/ppermute | solution.py:52
  (66 shorter events, 16.3 us)
Async XLA Ops:
  1.7 6.6 %collective-permute-start = (bf16[64,1152]{1,0:T(8,128)(2,1)S(1)}, bf16[64,1152]{1,0:T(8,128)(2,1)S(1)}, u32[]{:S(2)}, u32[]{:S(2)}) collective-permute-start(bf16[64,1152]{1,0:T(8,128)(2,1)S(1)} %shard_map.59.rest_0_), channel_id=1, source_target_pairs={{0,16},{1,17},{2,18},{3,19},{4,20},{5,21},{6,22},{7,23},{8,120},{9... | collective-permute-start | bytes 442376 | tf_op jit(solution)/shard_map/ppermute | solution.py:52
  4.7 8.6 %collective-permute-start.3 = (bf16[64,1152]{1,0:T(8,128)(2,1)S(1)}, bf16[64,1152]{1,0:T(8,128)(2,1)S(1)}, u32[]{:S(2)}, u32[]{:S(2)}) collective-permute-start(bf16[64,1152]{1,0:T(8,128)(2,1)S(1)} %shard_map.60), channel_id=1, source_target_pairs={{0,1},{1,0},{2,3},{3,2},{4,5},{5,4},{6,7},{7,6},{8,11},{9,10},{10,... | collective-permute-start | bytes 442376 | tf_op jit(solution)/shard_map/ppermute | solution.py:52
  6.3 7.1 %collective-permute-start.4 = (bf16[64,1152]{1,0:T(8,128)(2,1)S(1)}, bf16[64,1152]{1,0:T(8,128)(2,1)S(1)}, u32[]{:S(2)}, u32[]{:S(2)}) collective-permute-start(bf16[64,1152]{1,0:T(8,128)(2,1)S(1)} %shard_map.60), channel_id=1, source_target_pairs={{0,4},{1,5},{2,6},{3,7},{4,0},{5,1},{6,2},{7,3},{8,140},{9,141},{1... | collective-permute-start | bytes 442376 | tf_op jit(solution)/shard_map/ppermute | solution.py:52
  7.0 6.3 %collective-permute-start.5 = (bf16[64,1152]{1,0:T(8,128)(2,1)S(1)}, bf16[64,1152]{1,0:T(8,128)(2,1)S(1)}, u32[]{:S(2)}, u32[]{:S(2)}) collective-permute-start(bf16[64,1152]{1,0:T(8,128)(2,1)S(1)} %shard_map.60), channel_id=1, source_target_pairs={{0,5},{1,4},{2,7},{3,6},{4,1},{5,0},{6,3},{7,2},{8,143},{9,142},{1... | collective-permute-start | bytes 442376 | tf_op jit(solution)/shard_map/ppermute | solution.py:52
  8.3 9.7 %collective-permute-start.1 = (bf16[128,1152]{1,0:T(8,128)(2,1)S(1)}, bf16[128,1152]{1,0:T(8,128)(2,1)S(1)}, u32[]{:S(2)}, u32[]{:S(2)}) collective-permute-start(bf16[128,1152]{1,0:T(8,128)(2,1)S(1)} %pad_maximum_fusion.2), channel_id=1, source_target_pairs={{0,112},{1,113},{2,114},{3,115},{4,116},{5,117},{6,118},{7,119},{8... | collective-permute-start | bytes 884744 | tf_op jit(solution)/shard_map/ppermute | solution.py:52
  13.4 11.4 %collective-permute-start.7 = (bf16[256,1152]{1,0:T(8,128)(2,1)S(1)}, bf16[256,1152]{1,0:T(8,128)(2,1)S(1)}, u32[]{:S(2)}, u32[]{:S(2)}) collective-permute-start(bf16[256,1152]{1,0:T(8,128)(2,1)S(1)} %pad_maximum_fusion.1.refs_2_.quad.refs_1_), channel_id=1, source_target_pairs={{0,3},{1,2},{2,1},{3,0},{4,7},{5,6},{6,5},{7,4},{8,9},{9,8},{10,11... | collective-permute-start | bytes 1769480 | tf_op jit(solution)/shard_map/ppermute | solution.py:52
  16.3 11.1 %collective-permute-start.8 = (bf16[256,1152]{1,0:T(8,128)(2,1)S(1)}, bf16[256,1152]{1,0:T(8,128)(2,1)S(1)}, u32[]{:S(2)}, u32[]{:S(2)}) collective-permute-start(bf16[256,1152]{1,0:T(8,128)(2,1)S(1)} %pad_maximum_fusion.1.refs_2_.quad.refs_1_), channel_id=1, source_target_pairs={{0,132},{1,133},{2,134},{3,135},{4,128},{5,129},{6,130},{7,131},{8... | collective-permute-start | bytes 1769480 | tf_op jit(solution)/shard_map/ppermute | solution.py:52
  18.1 9.3 %collective-permute-start.2 = (bf16[256,1152]{1,0:T(8,128)(2,1)S(1)}, bf16[256,1152]{1,0:T(8,128)(2,1)S(1)}, u32[]{:S(2)}, u32[]{:S(2)}) collective-permute-start(bf16[256,1152]{1,0:T(8,128)(2,1)S(1)} %pad_maximum_fusion.refs_0_.own_a.refs_4_.refs_3_), channel_id=1, source_target_pairs={{0,8},{1,9},{2,10},{3,11},{4,12},{5,13},{6,14},{7,15},{8,0},{9,1},... | collective-permute-start | bytes 1769480 | tf_op jit(solution)/shard_map/ppermute | solution.py:52
  20.8 19.4 %collective-permute-start.11 = (bf16[256,1152]{1,0:T(8,128)(2,1)S(1)}, bf16[256,1152]{1,0:T(8,128)(2,1)S(1)}, u32[]{:S(2)}, u32[]{:S(2)}) collective-permute-start(bf16[256,1152]{1,0:T(8,128)(2,1)S(1)} %pad_maximum_fusion.1.refs_2_.quad.refs_1_), channel_id=1, source_target_pairs={{0,135},{1,134},{2,133},{3,132},{4,131},{5,130},{6,129},{7,128},{8... | collective-permute-start | bytes 1769480 | tf_op jit(solution)/shard_map/ppermute | solution.py:52
  23.3 6.7 %collective-permute-start.6 = (bf16[128,1152]{1,0:T(8,128)(2,1)S(1)}, bf16[128,1152]{1,0:T(8,128)(2,1)S(1)}, u32[]{:S(2)}, u32[]{:S(2)}) collective-permute-start(bf16[128,1152]{1,0:T(8,128)(2,1)S(1)} %collective-permute-done.1), channel_id=1, source_target_pairs={{0,16},{1,17},{2,18},{3,19},{4,20},{5,21},{6,22},{7,23},{8,120},{9... | collective-permute-start | bytes 884744 | tf_op jit(solution)/shard_map/ppermute | solution.py:52
  30.1 9.4 %collective-permute-start.9 = (bf16[128,1152]{1,0:T(8,128)(2,1)S(1)}, bf16[128,1152]{1,0:T(8,128)(2,1)S(1)}, u32[]{:S(2)}, u32[]{:S(2)}) collective-permute-start(bf16[128,1152]{1,0:T(8,128)(2,1)S(1)} %collective-permute-done.6.refs_0_.own_b.refs_6_.refs_5_), channel_id=1, source_target_pairs={{0,8},{1,9},{2,10},{3,11},{4,12},{5,13},{6,14},{7,15},{8,0},{9,1},... | collective-permute-start | bytes 884744 | tf_op jit(solution)/shard_map/ppermute | solution.py:52
  35.4 8.8 %collective-permute-start.10 = (bf16[128,1152]{1,0:T(8,128)(2,1)S(1)}, bf16[128,1152]{1,0:T(8,128)(2,1)S(1)}, u32[]{:S(2)}, u32[]{:S(2)}) collective-permute-start(bf16[128,1152]{1,0:T(8,128)(2,1)S(1)} %collective-permute-done.6.refs_0_.own_b.refs_6_.refs_5_), channel_id=1, source_target_pairs={{0,112},{1,113},{2,114},{3,115},{4,116},{5,117},{6,118},{7,119},{8... | collective-permute-start | bytes 884744 | tf_op jit(solution)/shard_map/ppermute | solution.py:52
  44.2 1.8 %collective-permute-start.12 = (bf16[128,1152]{1,0:T(8,128)(2,1)S(1)}, bf16[128,1152]{1,0:T(8,128)(2,1)S(1)}, u32[]{:S(2)}, u32[]{:S(2)}) collective-permute-start(bf16[128,1152]{1,0:T(8,128)(2,1)S(1)} %collective-permute-done.10.refs_0_.refs_8_.refs_7_), channel_id=1, source_target_pairs={{0,8},{1,9},{2,10},{3,11},{4,12},{5,13},{6,14},{7,15},{8,0},{9,1},... | collective-permute-start | bytes 884744 | tf_op jit(solution)/shard_map/ppermute | solution.py:52
  44.2 16.9 %collective-permute-start.21 = (bf16[384,1152]{1,0:T(8,128)(2,1)S(1)}, bf16[384,1152]{1,0:T(8,128)(2,1)S(1)}, u32[]{:S(2)}, u32[]{:S(2)}) collective-permute-start(bf16[384,1152]{1,0:T(8,128)(2,1)S(1)} %get-tuple-element.14), channel_id=1, source_target_pairs={{0,8},{1,9},{2,10},{3,11},{4,12},{5,13},{6,14},{7,15},{8,0},{9,1},... | collective-permute-start | bytes 2654216 | tf_op jit(solution)/shard_map/ppermute | solution.py:52
  49.0 12.1 %collective-permute-start.14 = (bf16[128,1152]{1,0:T(8,128)(2,1)S(1)}, bf16[128,1152]{1,0:T(8,128)(2,1)S(1)}, u32[]{:S(2)}, u32[]{:S(2)}) collective-permute-start(bf16[128,1152]{1,0:T(8,128)(2,1)S(1)} %add_convert_fusion.1), channel_id=1, source_target_pairs={{0,112},{1,113},{2,114},{3,115},{4,116},{5,117},{6,118},{7,119},{8... | collective-permute-start | bytes 884744 | tf_op jit(solution)/shard_map/ppermute | solution.py:52
  53.2 17.7 %collective-permute-start.15 = (bf16[256,1152]{1,0:T(8,128)(2,1)S(1)}, bf16[256,1152]{1,0:T(8,128)(2,1)S(1)}, u32[]{:S(2)}, u32[]{:S(2)}) collective-permute-start(bf16[256,1152]{1,0:T(8,128)(2,1)S(1)} %shard_map.69), channel_id=1, source_target_pairs={{0,135},{1,134},{2,133},{3,132},{4,131},{5,130},{6,129},{7,128},{8... | collective-permute-start | bytes 1769480 | tf_op jit(solution)/shard_map/ppermute | solution.py:52
  54.2 17.0 %collective-permute-start.16 = (bf16[256,1152]{1,0:T(8,128)(2,1)S(1)}, bf16[256,1152]{1,0:T(8,128)(2,1)S(1)}, u32[]{:S(2)}, u32[]{:S(2)}) collective-permute-start(bf16[256,1152]{1,0:T(8,128)(2,1)S(1)} %shard_map.70), channel_id=1, source_target_pairs={{0,3},{1,2},{2,1},{3,0},{4,7},{5,6},{6,5},{7,4},{8,9},{9,8},{10,11... | collective-permute-start | bytes 1769480 | tf_op jit(solution)/shard_map/ppermute | solution.py:52
  58.9 14.0 %collective-permute-start.17 = (bf16[256,1152]{1,0:T(8,128)(2,1)S(1)}, bf16[256,1152]{1,0:T(8,128)(2,1)S(1)}, u32[]{:S(2)}, u32[]{:S(2)}) collective-permute-start(bf16[256,1152]{1,0:T(8,128)(2,1)S(1)} %shard_map.71), channel_id=1, source_target_pairs={{0,132},{1,133},{2,134},{3,135},{4,128},{5,129},{6,130},{7,131},{8... | collective-permute-start | bytes 1769480 | tf_op jit(solution)/shard_map/ppermute | solution.py:52
  61.2 9.6 %collective-permute-start.22 = (bf16[128,1152]{1,0:T(8,128)(2,1)S(1)}, bf16[128,1152]{1,0:T(8,128)(2,1)S(1)}, u32[]{:S(2)}, u32[]{:S(2)}) collective-permute-start(bf16[128,1152]{1,0:T(8,128)(2,1)S(1)} %add_convert_fusion), channel_id=1, source_target_pairs={{0,16},{1,17},{2,18},{3,19},{4,20},{5,21},{6,22},{7,23},{8,120},{9... | collective-permute-start | bytes 884744 | tf_op jit(solution)/shard_map/ppermute | solution.py:52
  70.8 9.6 %collective-permute-start.23 = (bf16[128,1152]{1,0:T(8,128)(2,1)S(1)}, bf16[128,1152]{1,0:T(8,128)(2,1)S(1)}, u32[]{:S(2)}, u32[]{:S(2)}) collective-permute-start(bf16[128,1152]{1,0:T(8,128)(2,1)S(1)} %fusion), channel_id=1, source_target_pairs={{0,112},{1,113},{2,114},{3,115},{4,116},{5,117},{6,118},{7,119},{8... | collective-permute-start | bytes 884744 | tf_op jit(solution)/shard_map/ppermute | solution.py:52
  73.1 7.5 %collective-permute-start.18 = (bf16[64,1152]{1,0:T(8,128)(2,1)S(1)}, bf16[64,1152]{1,0:T(8,128)(2,1)S(1)}, u32[]{:S(2)}, u32[]{:S(2)}) collective-permute-start(bf16[64,1152]{1,0:T(8,128)(2,1)S(1)} %get-tuple-element.28), channel_id=1, source_target_pairs={{0,5},{1,4},{2,7},{3,6},{4,1},{5,0},{6,3},{7,2},{8,143},{9,142},{1... | collective-permute-start | bytes 442376 | tf_op jit(solution)/shard_map/ppermute | solution.py:52
  73.2 7.4 %collective-permute-start.19 = (bf16[64,1152]{1,0:T(8,128)(2,1)S(1)}, bf16[64,1152]{1,0:T(8,128)(2,1)S(1)}, u32[]{:S(2)}, u32[]{:S(2)}) collective-permute-start(bf16[64,1152]{1,0:T(8,128)(2,1)S(1)} %get-tuple-element.27), channel_id=1, source_target_pairs={{0,1},{1,0},{2,3},{3,2},{4,5},{5,4},{6,7},{7,6},{8,11},{9,10},{10,... | collective-permute-start | bytes 442376 | tf_op jit(solution)/shard_map/ppermute | solution.py:52
  73.5 7.3 %collective-permute-start.20 = (bf16[64,1152]{1,0:T(8,128)(2,1)S(1)}, bf16[64,1152]{1,0:T(8,128)(2,1)S(1)}, u32[]{:S(2)}, u32[]{:S(2)}) collective-permute-start(bf16[64,1152]{1,0:T(8,128)(2,1)S(1)} %get-tuple-element.26), channel_id=1, source_target_pairs={{0,4},{1,5},{2,6},{3,7},{4,0},{5,1},{6,2},{7,3},{8,140},{9,141},{1... | collective-permute-start | bytes 442376 | tf_op jit(solution)/shard_map/ppermute | solution.py:52
  80.5 5.2 %collective-permute-start.24 = (bf16[64,1152]{1,0:T(8,128)(2,1)S(1)}, bf16[64,1152]{1,0:T(8,128)(2,1)S(1)}, u32[]{:S(2)}, u32[]{:S(2)}) collective-permute-start(bf16[64,1152]{1,0:T(8,128)(2,1)S(1)} %slice.122), channel_id=1, source_target_pairs={{0,16},{1,17},{2,18},{3,19},{4,20},{5,21},{6,22},{7,23},{8,120},{9... | collective-permute-start | bytes 442376 | tf_op jit(solution)/shard_map/ppermute | solution.py:52
  (5 other events, 18.1 us)

commit v3 on v2

--- a/solution.py
+++ b/solution.py
@@ -90,25 +90,25 @@
     )(rows, *earlier)
 
 
-def grad_kernel(factor, rows, others, sums, *rest):
+def grad_kernel(coefficients, rows, others, sums, *rest):
     *arrived, grad = rest
     unit, inverse = unit_rows(rows[...])
     other_send = widened(rounded(unit_rows(others[...])[0]))
-    total = sums[...] - factor[0] * other_send
+    total = sums[...] - scale_and_bias(coefficients)[0] * other_send
     for part in arrived:
         total = total + widened(part[...])
     grad[...] = through_norm(unit, inverse, total)
 
 
-def grad_rows(factor, rows, others, sums, *arrived):
+def grad_rows(coefficients, rows, others, sums, *arrived):
     whole = pl.BlockSpec(memory_space=pltpu.VMEM)
     return pl.pallas_call(
         grad_kernel,
         out_shape=jax.ShapeDtypeStruct(rows.shape, jnp.float32),
-        in_specs=[pl.BlockSpec(memory_space=pltpu.SMEM)] + [whole] * (3 + len(arrived)),
+        in_specs=[whole] * (4 + len(arrived)),
         out_specs=whole,
         compiler_params=pltpu.CompilerParams(vmem_limit_bytes=4 * 2**20),
-    )(factor, rows, others, sums, *arrived)
+    )(coefficients, rows, others, sums, *arrived)
 
 
 def weights_of(factor, offset, texts, images):
@@ -129,6 +129,10 @@
     return jnp.dot(weights, images[...], preferred_element_type=jnp.float32)
 
 
+def scale_and_bias(coefficients):
+    return coefficients[0:1, 0:1], coefficients[4:5, 0:1]
+
+
 def rows_of(*refs):
     return jnp.concatenate([ref[...] for ref in refs], axis=0)
 
@@ -137,36 +141,31 @@
     return jnp.concatenate(parts, axis=1)
 
 
-def weight_kernel(count, scale, bias, *refs):
+def weight_kernel(count, coefficients, *refs):
     *inputs, weights = refs
     weights[...] = weights_of(
-        scale[0], bias[0], rows_of(*inputs[:count]), rows_of(*inputs[count:])
-    )
-
-
-def corner_kernel(scale, bias, own_a, sib_a, own_b, sib_b, quad, part_x, part_y, part_d,
-                  w_aq, w_axy, w_bqxy, w_d, sums_own, sums_own_b, send):
-    a, b = own_a.shape[0], own_b.shape[0]
-    w_d[...] = weights_of(scale[0], bias[0], rows_of(own_a, sib_a, own_b, sib_b), part_d)
-    images = rows_of(quad, part_x, part_y, part_d)
-    late = w_d[pl.ds(2 * a, 2 * b)]
-    total = for_texts(columns_of(w_bqxy[...], late), images)
-    sums_own_b[...] = total[:b]
-    send[pl.ds(0, b)] = rounded(total[b:])
-    late = w_d[pl.ds(0, 2 * a)]
-    total = for_texts(columns_of(w_aq[...], w_axy[...], late), images)
-    sums_own[...] = total[:a]
-    send[pl.ds(b, a)] = rounded(total[a:])
-
-
-def sibling_kernel(scale, bias, sib_c, quad, part_x, part_y, part_d, weights, send):
-    images = rows_of(quad, part_x, part_y, part_d)
-    weights[...] = weights_of(scale[0], bias[0], sib_c, images)
+        *scale_and_bias(coefficients), rows_of(*inputs[:count]), rows_of(*inputs[count:])
+    )
+
+
+def near_kernel(count, *refs):
+    *inputs, sums_own, send = refs
+    weights = columns_of(*[ref[...] for ref in inputs[:count]])
+    total = for_texts(weights, rows_of(*inputs[count:]))
+    own = sums_own.shape[0]
+    sums_own[...] = total[:own]
+    send[...] = rounded(total[own:])
+
+
+def sibling_kernel(coefficients, sib_c, quad, part_x, part_y, top_d, low_d, weights, send):
+    images = rows_of(quad, part_x, part_y, top_d, low_d)
+    weights[...] = weights_of(*scale_and_bias(coefficients), sib_c, images)
     send[...] = rounded(for_texts(weights[...], images))
 
 
-def text_kernel(weights, quad, part_x, part_y, part_d, sums):
-    sums[...] = for_texts(weights[...], rows_of(quad, part_x, part_y, part_d))
+def text_kernel(weights, *refs):
+    *images, sums = refs
+    sums[...] = for_texts(weights[...], rows_of(*images))
 
 
 def image_kernel(count, *refs):
@@ -175,14 +174,13 @@
     sums[...] = total.astype(sums.dtype)
 
 
-def on_device(kernel, outputs, *operands, scalars=0, products=0):
+def on_device(kernel, outputs, *operands, products=0):
     vmem = pl.BlockSpec(memory_space=pltpu.VMEM)
-    smem = pl.BlockSpec(memory_space=pltpu.SMEM)
     width = operands[-1].shape[-1]
     return pl.pallas_call(
         kernel,
         out_shape=[jax.ShapeDtypeStruct(shape, kind) for shape, kind in outputs],
-        in_specs=[smem] * scalars + [vmem] * (len(operands) - scalars),
+        in_specs=[vmem] * len(operands),
         out_specs=[vmem] * len(outputs),
         compiler_params=pltpu.CompilerParams(vmem_limit_bytes=16 * 2**20),
         cost_estimate=pl.CostEstimate(
@@ -203,7 +201,7 @@
     f32, bf16 = jnp.float32, jnp.bfloat16
     n, d = images.shape
     a, b, q = 4 * n, 2 * n, 4 * n
-    scalars = (logit_scale, logit_bias)
+    coefficients = join(*[jnp.broadcast_to(v, (4, 128)) for v in (logit_scale, logit_bias)])
     text_send = send_rows(texts)
     image_send = send_rows(images, text_send)
 
@@ -212,37 +210,40 @@
         k = sum(v.shape[0] for v in some_images)
         return on_device(
             functools.partial(weight_kernel, len(some_texts)), [((m, k), bf16)],
-            *scalars, *some_texts, *some_images, scalars=2, products=share * m * k,
+            coefficients, *some_texts, *some_images, products=share * m * k,
         )[0]
 
     r1 = z1(text_send)
-    quad = join(image_send, x1(image_send), y1(image_send), d1(image_send))
-    near = join(text_send, r1)
-    r2 = z2(near)
-    part_x, part_y, part_d = x2(quad), y2(quad), d2(quad)
+    quad = join(image_send, after(x1(image_send), coefficients), y1(image_send), d1(image_send))
+    pair = join(text_send, r1)
+    r2 = z2(pair)
+    part_x, part_y = x2(quad), y2(quad)
     r3 = z1(r2)
-    own_a = join(near, r2)
+    top_d, low_d = y2(part_x[: q // 2]), x2(part_y[q // 2 :])
+    r4 = z2(r3)
+    own_a = join(pair, r2)
     sib_a = sibling(own_a)
     w_aq = weigh((own_a, sib_a), (quad,))
-    w_axy = weigh((own_a, sib_a), (part_x, part_y), share=40)
-    r3 = after(r3, w_aq, w_axy)
-    r4 = z2(r3)
+    w_axy = weigh((own_a, sib_a), (part_x, part_y))
     sib_b = sibling(r3)
     w_bqxy = weigh((r3, sib_b), (quad, part_x, part_y))
-    w_d, sums_own, sums_own_b, send_ab = on_device(
-        corner_kernel,
-        [((2 * a + 2 * b, q), bf16), ((a, d), f32), ((b, d), f32), ((a + b, d), bf16)],
-        *scalars, own_a, sib_a, r3, sib_b, quad, part_x, part_y, part_d, w_aq, w_axy, w_bqxy,
-        scalars=2, products=40 * 3 * q * (a + b),
-    )
-    r4 = after(r4, send_ab)
-    back_ab = sibling(send_ab)
-    all_images = (quad, part_x, part_y, part_d)
+    w_d = weigh((after(own_a, w_aq, w_axy, w_bqxy), sib_a, r3, sib_b), (top_d, low_d), share=40)
+    all_images = (quad, part_x, part_y, top_d, low_d)
+
+    def near(rows, *blocks, products=0):
+        return on_device(
+            functools.partial(near_kernel, len(blocks)), [((rows, d), f32), ((rows, d), bf16)],
+            *blocks, *all_images, products=products,
+        )
+
+    sums_own_b, send_b = near(b, w_bqxy, w_d[2 * a :], products=40 * 2 * b * 4 * q)
+    r4 = after(r4, send_b)
+    back_b = sibling(send_b)
     sib_c = sibling(r4)
     w_own = weigh((r4,), all_images)
     w_sib, send_c = on_device(
-        sibling_kernel, [((b, 4 * q), bf16), ((b, d), bf16)], *scalars, sib_c, *all_images,
-        scalars=2, products=2 * b * 4 * q,
+        sibling_kernel, [((b, 4 * q), bf16), ((b, d), bf16)], coefficients, sib_c, *all_images,
+        products=2 * b * 4 * q,
     )
     (sums_own_c,) = on_device(
         text_kernel, [((b, d), f32)], w_own, *all_images, products=b * 4 * q
@@ -250,10 +251,10 @@
     s4 = rounded(sums_own_c + widened(sibling(send_c)))
     all_texts = (own_a, sib_a, r3, sib_b, r4, sib_c)
 
-    def image_part(kind, *blocks):
+    def image_part(kind, *blocks, share=1):
         return on_device(
             functools.partial(image_kernel, len(blocks)), [((q, d), kind)],
-            *blocks, *all_texts, products=q * 8 * q // 2,
+            *blocks, *all_texts, products=share * q * 4 * q,
         )[0]
 
     def late(index, *others):
@@ -261,18 +262,21 @@
         return after(w_own[:, span], *others), w_sib[:, span]
 
     back_d = d2(image_part(bf16, w_d, *late(3)))
-    back_x = x2(image_part(bf16, w_axy[:, :q], w_bqxy[:, q : 2 * q], *late(1, s4)))
-    back_y = y2(image_part(bf16, w_axy[:, q:], w_bqxy[:, 2 * q :], *late(2, s4)))
-    s4 = z2(s4)
-    quad_sums = image_part(f32, w_aq, w_bqxy[:, :q], *late(0, s4))
-    s3 = sums_own_b + widened(back_ab[:b]) + widened(s4)
-    near_sums = sums_own + widened(back_ab[b:])
+    send_x = image_part(bf16, w_axy[:, :q], w_bqxy[:, q : 2 * q], *late(1, s4))
+    send_y = image_part(bf16, w_axy[:, q:], w_bqxy[:, 2 * q :], *late(2, s4))
+    back_x, back_y = x2(send_x), y2(send_y)
+    sums_own, send_a = near(a, after(w_aq, s4), w_axy, w_d[: 2 * a], products=2 * a * 4 * q)
+    back_a = sibling(send_a)
+    s4 = after(z2(s4), send_a)
+    s3 = sums_own_b + widened(back_b) + widened(s4)
+    near_sums = sums_own + widened(back_a)
     s2 = near_sums[2 * n :] + widened(z1(rounded(s3)))
+    quad_sums = image_part(f32, w_aq, w_bqxy[:, :q], *late(0, s2), share=1)
     s01 = near_sums[: 2 * n] + widened(z2(rounded(s2)))
     quad_sums = quad_sums + widened(back_d) + widened(back_x) + widened(back_y)
-    text_grad = grad_rows(logit_scale, texts, images, s01[:n], z1(rounded(s01[n:])))
+    text_grad = grad_rows(coefficients, texts, images, s01[:n], z1(rounded(s01[n:])))
     image_grad = grad_rows(
-        logit_scale,
+        coefficients,
         images,
         texts,
         quad_sums[:n],

time: 86.9 us -> 78.8 us (0.907)
  the two profiles are of different devices: /device:TPU:24 before, /device:TPU:8 now
where the time goes in v3:
time: 78.8 us; the launch traced here: 77.9 us
  starting transfers between devices  36.7 us (47%)
  waiting for transfers between devices  22 us (28%)
  Pallas kernels  14 us (18%)
  between operations  2.27 us (3%)
  local copies, waits for them, and re-layouts  2.17 us (3%)
    ppermute x27, starting transfers between devices, exchange(): return lambda value: lax.ppermute(value, AXES, pairs)  36.7 us
    ppermute x27, waiting for transfers between devices, exchange(): return lambda value: lax.ppermute(value, AXES, pairs)  22 us
    pallas_call x13, Pallas kernels, on_device(): pl.pallas_call(kernel, out_shape=[jax.ShapeDtypeStruct(shape, kind) for s...  11.8 us
    pallas_call x2, Pallas kernels, grad_rows(): pl.pallas_call(grad_kernel, out_shape=jax.ShapeDtypeStruct(rows.shape, jn...  2.03 us
    unnamed x8, local copies, waits for them, and re-layouts  1.82 us
  transfers between devices with their start and end apart: 27, of which 11 were waited for; matrix products, arithmetic and copies ran while one was open for 1% of the time, Pallas kernels for 17%

profile of v3, /device:TPU:8, one launch (start us, length us, event | category | flops | bytes accessed | tf_op | source)
XLA Modules:
  0.0 77.9 jit_solution(6073442354144763518)
XLA Ops:
  1.7 2.0 %collective-permute-start = (bf16[64,1152]{1,0:T(8,128)(2,1)S(1)}, bf16[64,1152]{1,0:T(8,128)(2,1)S(1)}, u32[]{:S(2)}, u32[]{:S(2)}) collective-permute-start(bf16[64,1152]{1,0:T(8,128)(2,1)S(1)} %shard_map.65.rest_0_), channel_id=1, source_target_pairs={{0,16},{1,17},{2,18},{3,19},{4,20},{5,21},{6,22},{7,23},{8,120},{9... | collective-permute-start | bytes 442376 | tf_op jit(solution)/shard_map/ppermute | solution.py:52
  4.7 1.6 %collective-permute-start.3 = (bf16[64,1152]{1,0:T(8,128)(2,1)S(1)}, bf16[64,1152]{1,0:T(8,128)(2,1)S(1)}, u32[]{:S(2)}, u32[]{:S(2)}) collective-permute-start(bf16[64,1152]{1,0:T(8,128)(2,1)S(1)} %shard_map.66), channel_id=1, source_target_pairs={{0,1},{1,0},{2,3},{3,2},{4,5},{5,4},{6,7},{7,6},{8,11},{9,10},{10,... | collective-permute-start | bytes 442376 | tf_op jit(solution)/shard_map/ppermute | solution.py:52
  6.7 1.5 %collective-permute-start.5 = (bf16[64,1152]{1,0:T(8,128)(2,1)S(1)}, bf16[64,1152]{1,0:T(8,128)(2,1)S(1)}, u32[]{:S(2)}, u32[]{:S(2)}) collective-permute-start(bf16[64,1152]{1,0:T(8,128)(2,1)S(1)} %shard_map.66), channel_id=1, source_target_pairs={{0,5},{1,4},{2,7},{3,6},{4,1},{5,0},{6,3},{7,2},{8,143},{9,142},{1... | collective-permute-start | bytes 442376 | tf_op jit(solution)/shard_map/ppermute | solution.py:52
  8.3 5.0 %collective-permute-start.1 = (bf16[128,1152]{1,0:T(8,128)(2,1)S(1)}, bf16[128,1152]{1,0:T(8,128)(2,1)S(1)}, u32[]{:S(2)}, u32[]{:S(2)}) collective-permute-start(bf16[128,1152]{1,0:T(8,128)(2,1)S(1)} %pad_maximum_fusion.2), channel_id=1, source_target_pairs={{0,112},{1,113},{2,114},{3,115},{4,116},{5,117},{6,118},{7,119},{8... | collective-permute-start | bytes 884744 | tf_op jit(solution)/shard_map/ppermute | solution.py:52
  14.8 2.8 %collective-permute-start.8 = (bf16[256,1152]{1,0:T(8,128)(2,1)S(1)}, bf16[256,1152]{1,0:T(8,128)(2,1)S(1)}, u32[]{:S(2)}, u32[]{:S(2)}) collective-permute-start(bf16[256,1152]{1,0:T(8,128)(2,1)S(1)} %pad_maximum_fusion.1.refs_2_.refs_1_.refs_0_.quad.refs_3_), channel_id=1, source_target_pairs={{0,3},{1,2},{2,1},{3,0},{4,7},{5,6},{6,5},{7,4},{8,9},{9,8},{10,11... | collective-permute-start | bytes 1769480 | tf_op jit(solution)/shard_map/ppermute | solution.py:52
  17.6 1.6 %collective-permute-start.9 = (bf16[256,1152]{1,0:T(8,128)(2,1)S(1)}, bf16[256,1152]{1,0:T(8,128)(2,1)S(1)}, u32[]{:S(2)}, u32[]{:S(2)}) collective-permute-start(bf16[256,1152]{1,0:T(8,128)(2,1)S(1)} %pad_maximum_fusion.1.refs_2_.refs_1_.refs_0_.quad.refs_3_), channel_id=1, source_target_pairs={{0,132},{1,133},{2,134},{3,135},{4,128},{5,129},{6,130},{7,131},{8... | collective-permute-start | bytes 1769480 | tf_op jit(solution)/shard_map/ppermute | solution.py:52
  19.3 2.1 %collective-permute-start.2 = (bf16[256,1152]{1,0:T(8,128)(2,1)S(1)}, bf16[256,1152]{1,0:T(8,128)(2,1)S(1)}, u32[]{:S(2)}, u32[]{:S(2)}) collective-permute-start(bf16[256,1152]{1,0:T(8,128)(2,1)S(1)} %pad_maximum_fusion.refs_0_.refs_4_.refs_3_), channel_id=1, source_target_pairs={{0,8},{1,9},{2,10},{3,11},{4,12},{5,13},{6,14},{7,15},{8,0},{9,1},... | collective-permute-start | bytes 1769480 | tf_op jit(solution)/shard_map/ppermute | solution.py:52
  21.4 6.7 %collective-permute-done.6.refs_0_.refs_2_.refs_6_.refs_5_ = bf16[128,1152]{1,0:T(8,128)(2,1)S(1)} collective-permute-done((bf16[128,1152]{1,0:T(8,128)(2,1)S(1)}, bf16[128,1152]{1,0:T(8,128)(2,1)S(1)}, u32[]{:S(2)}, u32[]{:S(2)}) %collective-permute-start.6) | collective-permute-done | bytes 294944 | tf_op jit(solution)/shard_map/ppermute | solution.py:52
  28.4 2.2 %collective-permute-start.12 = (bf16[128,1152]{1,0:T(8,128)(2,1)S(1)}, bf16[128,1152]{1,0:T(8,128)(2,1)S(1)}, u32[]{:S(2)}, u32[]{:S(2)}) collective-permute-start(bf16[128,1152]{1,0:T(8,128)(2,1)S(1)} %slice.106), channel_id=1, source_target_pairs={{0,3},{1,2},{2,1},{3,0},{4,7},{5,6},{6,5},{7,4},{8,9},{9,8},{10,11... | collective-permute-start | bytes 884744 | tf_op jit(solution)/shard_map/ppermute | solution.py:52
  30.6 3.1 %collective-permute-start.10 = (bf16[128,1152]{1,0:T(8,128)(2,1)S(1)}, bf16[128,1152]{1,0:T(8,128)(2,1)S(1)}, u32[]{:S(2)}, u32[]{:S(2)}) collective-permute-start(bf16[128,1152]{1,0:T(8,128)(2,1)S(1)} %collective-permute-done.6.refs_0_.refs_2_.refs_6_.refs_5_), channel_id=1, source_target_pairs={{0,112},{1,113},{2,114},{3,115},{4,116},{5,117},{6,118},{7,119},{8... | collective-permute-start | bytes 884744 | tf_op jit(solution)/shard_map/ppermute | solution.py:52
  35.1 1.0 %shard_map.69.refs_1_ = bf16[512,512]{1,0:T(8,128)(2,1)S(1)} custom-call(f32[8,128]{1,0:T(8,128)S(1)} %concatenate.16.coefficients, bf16[256,1152]{1,0:T(8,128)(2,1)S(1)} %pad_maximum_fusion.refs_0_.refs_4_.refs_3_, bf16[256,1152]{1,0:T(8,128)(2,1)S(1)} %collective-permute-done.2.refs_1_.refs_5_.refs_4_, ...), custom_call_target="tpu_custom_call" | custom-call | flops 603979776 | tf_op jit(solution)/shard_map/pallas_call | solution.py:180
  40.4 1.3 %shard_map.74 = (bf16[128,1024]{1,0:T(8,128)(2,1)S(1)}, bf16[128,1152]{1,0:T(8,128)(2,1)S(1)}) custom-call(f32[8,128]{1,0:T(8,128)S(1)} %concatenate.16.coefficients, bf16[128,1152]{1,0:T(8,128)(2,1)S(1)} %collective-permute-done.13.sib_c.refs_9_.refs_8_, bf16[256,1152]{1,0:T(8,128)(2,1)S(1)} %pad_maximum_fusion.1.refs_2_.refs_1_.refs_0_.quad.refs_3_, ...), custom_call_target="tpu_custom_call" | custom-call | flops 603979776 | tf_op jit(solution)/shard_map/pallas_call | solution.py:180
  43.4 3.1 %collective-permute-start.17 = (bf16[128,1152]{1,0:T(8,128)(2,1)S(1)}, bf16[128,1152]{1,0:T(8,128)(2,1)S(1)}, u32[]{:S(2)}, u32[]{:S(2)}) collective-permute-start(bf16[128,1152]{1,0:T(8,128)(2,1)S(1)} %add_convert_fusion.1), channel_id=1, source_target_pairs={{0,112},{1,113},{2,114},{3,115},{4,116},{5,117},{6,118},{7,119},{8... | collective-permute-start | bytes 884744 | tf_op jit(solution)/shard_map/ppermute | solution.py:52
  47.5 1.4 %collective-permute-start.19 = (bf16[256,1152]{1,0:T(8,128)(2,1)S(1)}, bf16[256,1152]{1,0:T(8,128)(2,1)S(1)}, u32[]{:S(2)}, u32[]{:S(2)}) collective-permute-start(bf16[256,1152]{1,0:T(8,128)(2,1)S(1)} %shard_map.77), channel_id=1, source_target_pairs={{0,135},{1,134},{2,133},{3,132},{4,131},{5,130},{6,129},{7,128},{8... | collective-permute-start | bytes 1769480 | tf_op jit(solution)/shard_map/ppermute | solution.py:52
  48.9 1.5 %shard_map.75 = (f32[256,1152]{1,0:T(8,128)S(1)}, bf16[256,1152]{1,0:T(8,128)(2,1)S(1)}) custom-call(bf16[512,256]{1,0:T(8,128)(2,1)S(1)} %shard_map.67.refs_0_, bf16[512,512]{1,0:T(8,128)(2,1)S(1)} %shard_map.69.refs_1_, bf16[512,256]{1,0:T(8,128)(2,1)S(1)} %slice.109.refs_2_, bf16[256,1152]{1,0:T(8,128)(2,1)S(1)} %pad_maximum_fusion.1.refs_2_.refs_1_.refs_0_.quad.refs_3_, ...), custom_call_target="tpu_custom_call" | custom-call | flops 1207959552 | tf_op jit(solution)/shard_map/pallas_call | solution.py:180
  51.4 1.8 %collective-permute-start.20 = (bf16[256,1152]{1,0:T(8,128)(2,1)S(1)}, bf16[256,1152]{1,0:T(8,128)(2,1)S(1)}, u32[]{:S(2)}, u32[]{:S(2)}) collective-permute-start(bf16[256,1152]{1,0:T(8,128)(2,1)S(1)} %shard_map.78), channel_id=1, source_target_pairs={{0,3},{1,2},{2,1},{3,0},{4,7},{5,6},{6,5},{7,4},{8,9},{9,8},{10,11... | collective-permute-start | bytes 1769480 | tf_op jit(solution)/shard_map/ppermute | solution.py:52
  54.1 1.7 %collective-permute-start.21 = (bf16[256,1152]{1,0:T(8,128)(2,1)S(1)}, bf16[256,1152]{1,0:T(8,128)(2,1)S(1)}, u32[]{:S(2)}, u32[]{:S(2)}) collective-permute-start(bf16[256,1152]{1,0:T(8,128)(2,1)S(1)} %shard_map.79), channel_id=1, source_target_pairs={{0,132},{1,133},{2,134},{3,135},{4,128},{5,129},{6,130},{7,131},{8... | collective-permute-start | bytes 1769480 | tf_op jit(solution)/shard_map/ppermute | solution.py:52
  56.2 6.6 %collective-permute-done.18 = bf16[128,1152]{1,0:T(8,128)(2,1)S(1)} collective-permute-done((bf16[128,1152]{1,0:T(8,128)(2,1)S(1)}, bf16[128,1152]{1,0:T(8,128)(2,1)S(1)}, u32[]{:S(2)}, u32[]{:S(2)}) %collective-permute-start.18) | collective-permute-done | bytes 294944 | tf_op jit(solution)/shard_map/ppermute | solution.py:52
  64.8 1.1 %collective-permute-done.21 = bf16[256,1152]{1,0:T(8,128)(2,1)S(1)} collective-permute-done((bf16[256,1152]{1,0:T(8,128)(2,1)S(1)}, bf16[256,1152]{1,0:T(8,128)(2,1)S(1)}, u32[]{:S(2)}, u32[]{:S(2)}) %collective-permute-start.21) | collective-permute-done | bytes 589856 | tf_op jit(solution)/shard_map/ppermute | solution.py:52
  66.2 1.5 %collective-permute-start.22 = (bf16[64,1152]{1,0:T(8,128)(2,1)S(1)}, bf16[64,1152]{1,0:T(8,128)(2,1)S(1)}, u32[]{:S(2)}, u32[]{:S(2)}) collective-permute-start(bf16[64,1152]{1,0:T(8,128)(2,1)S(1)} %get-tuple-element.34), channel_id=1, source_target_pairs={{0,5},{1,4},{2,7},{3,6},{4,1},{5,0},{6,3},{7,2},{8,143},{9,142},{1... | collective-permute-start | bytes 442376 | tf_op jit(solution)/shard_map/ppermute | solution.py:52
  67.7 3.0 %collective-permute-start.23 = (bf16[64,1152]{1,0:T(8,128)(2,1)S(1)}, bf16[64,1152]{1,0:T(8,128)(2,1)S(1)}, u32[]{:S(2)}, u32[]{:S(2)}) collective-permute-start(bf16[64,1152]{1,0:T(8,128)(2,1)S(1)} %get-tuple-element.33), channel_id=1, source_target_pairs={{0,1},{1,0},{2,3},{3,2},{4,5},{5,4},{6,7},{7,6},{8,11},{9,10},{10,... | collective-permute-start | bytes 442376 | tf_op jit(solution)/shard_map/ppermute | solution.py:52
  71.0 1.3 %collective-permute-done.22.rest_0_ = bf16[64,1152]{1,0:T(8,128)(2,1)S(1)} collective-permute-done((bf16[64,1152]{1,0:T(8,128)(2,1)S(1)}, bf16[64,1152]{1,0:T(8,128)(2,1)S(1)}, u32[]{:S(2)}, u32[]{:S(2)}) %collective-permute-start.22) | collective-permute-done | bytes 147488 | tf_op jit(solution)/shard_map/ppermute | solution.py:52
  72.3 3.1 %collective-permute-done.23.rest_1_ = bf16[64,1152]{1,0:T(8,128)(2,1)S(1)} collective-permute-done((bf16[64,1152]{1,0:T(8,128)(2,1)S(1)}, bf16[64,1152]{1,0:T(8,128)(2,1)S(1)}, u32[]{:S(2)}, u32[]{:S(2)}) %collective-permute-start.23) | collective-permute-done | bytes 147488 | tf_op jit(solution)/shard_map/ppermute | solution.py:52
  75.9 1.0 %shard_map.80 = f32[64,1152]{1,0:T(8,128)} custom-call(f32[8,128]{1,0:T(8,128)S(1)} %concatenate.16.coefficients, bf16[64,1152]{1,0:T(8,128)(2,1)S(1)} %copy-done.1, bf16[64,1152]{1,0:T(8,128)(2,1)S(1)} %copy-done.3, f32[64,1152]{1,0:T(8,128)S(1)} %slice.118.sums, bf16[64,1152]{1,0:T(8,128)(2,1)S(1)} %collective-permute-done.22.rest_0_, ...), custom_call_target="tpu_custom_call" | custom-call | tf_op jit(solution)/shard_map/pallas_call | solution.py:105
  (79 shorter events, 17.5 us)
Async XLA Ops:
  1.7 6.6 %collective-permute-start = (bf16[64,1152]{1,0:T(8,128)(2,1)S(1)}, bf16[64,1152]{1,0:T(8,128)(2,1)S(1)}, u32[]{:S(2)}, u32[]{:S(2)}) collective-permute-start(bf16[64,1152]{1,0:T(8,128)(2,1)S(1)} %shard_map.65.rest_0_), channel_id=1, source_target_pairs={{0,16},{1,17},{2,18},{3,19},{4,20},{5,21},{6,22},{7,23},{8,120},{9... | collective-permute-start | bytes 442376 | tf_op jit(solution)/shard_map/ppermute | solution.py:52
  4.7 10.0 %collective-permute-start.3 = (bf16[64,1152]{1,0:T(8,128)(2,1)S(1)}, bf16[64,1152]{1,0:T(8,128)(2,1)S(1)}, u32[]{:S(2)}, u32[]{:S(2)}) collective-permute-start(bf16[64,1152]{1,0:T(8,128)(2,1)S(1)} %shard_map.66), channel_id=1, source_target_pairs={{0,1},{1,0},{2,3},{3,2},{4,5},{5,4},{6,7},{7,6},{8,11},{9,10},{10,... | collective-permute-start | bytes 442376 | tf_op jit(solution)/shard_map/ppermute | solution.py:52
  6.3 8.5 %collective-permute-start.4 = (bf16[64,1152]{1,0:T(8,128)(2,1)S(1)}, bf16[64,1152]{1,0:T(8,128)(2,1)S(1)}, u32[]{:S(2)}, u32[]{:S(2)}) collective-permute-start(bf16[64,1152]{1,0:T(8,128)(2,1)S(1)} %shard_map.66), channel_id=1, source_target_pairs={{0,4},{1,5},{2,6},{3,7},{4,0},{5,1},{6,2},{7,3},{8,140},{9,141},{1... | collective-permute-start | bytes 442376 | tf_op jit(solution)/shard_map/ppermute | solution.py:52
  6.7 8.0 %collective-permute-start.5 = (bf16[64,1152]{1,0:T(8,128)(2,1)S(1)}, bf16[64,1152]{1,0:T(8,128)(2,1)S(1)}, u32[]{:S(2)}, u32[]{:S(2)}) collective-permute-start(bf16[64,1152]{1,0:T(8,128)(2,1)S(1)} %shard_map.66), channel_id=1, source_target_pairs={{0,5},{1,4},{2,7},{3,6},{4,1},{5,0},{6,3},{7,2},{8,143},{9,142},{1... | collective-permute-start | bytes 442376 | tf_op jit(solution)/shard_map/ppermute | solution.py:52
  8.3 10.9 %collective-permute-start.1 = (bf16[128,1152]{1,0:T(8,128)(2,1)S(1)}, bf16[128,1152]{1,0:T(8,128)(2,1)S(1)}, u32[]{:S(2)}, u32[]{:S(2)}) collective-permute-start(bf16[128,1152]{1,0:T(8,128)(2,1)S(1)} %pad_maximum_fusion.2), channel_id=1, source_target_pairs={{0,112},{1,113},{2,114},{3,115},{4,116},{5,117},{6,118},{7,119},{8... | collective-permute-start | bytes 884744 | tf_op jit(solution)/shard_map/ppermute | solution.py:52
  14.8 13.4 %collective-permute-start.8 = (bf16[256,1152]{1,0:T(8,128)(2,1)S(1)}, bf16[256,1152]{1,0:T(8,128)(2,1)S(1)}, u32[]{:S(2)}, u32[]{:S(2)}) collective-permute-start(bf16[256,1152]{1,0:T(8,128)(2,1)S(1)} %pad_maximum_fusion.1.refs_2_.refs_1_.refs_0_.quad.refs_3_), channel_id=1, source_target_pairs={{0,3},{1,2},{2,1},{3,0},{4,7},{5,6},{6,5},{7,4},{8,9},{9,8},{10,11... | collective-permute-start | bytes 1769480 | tf_op jit(solution)/shard_map/ppermute | solution.py:52
  17.6 10.7 %collective-permute-start.9 = (bf16[256,1152]{1,0:T(8,128)(2,1)S(1)}, bf16[256,1152]{1,0:T(8,128)(2,1)S(1)}, u32[]{:S(2)}, u32[]{:S(2)}) collective-permute-start(bf16[256,1152]{1,0:T(8,128)(2,1)S(1)} %pad_maximum_fusion.1.refs_2_.refs_1_.refs_0_.quad.refs_3_), channel_id=1, source_target_pairs={{0,132},{1,133},{2,134},{3,135},{4,128},{5,129},{6,130},{7,131},{8... | collective-permute-start | bytes 1769480 | tf_op jit(solution)/shard_map/ppermute | solution.py:52
  19.3 14.4 %collective-permute-start.2 = (bf16[256,1152]{1,0:T(8,128)(2,1)S(1)}, bf16[256,1152]{1,0:T(8,128)(2,1)S(1)}, u32[]{:S(2)}, u32[]{:S(2)}) collective-permute-start(bf16[256,1152]{1,0:T(8,128)(2,1)S(1)} %pad_maximum_fusion.refs_0_.refs_4_.refs_3_), channel_id=1, source_target_pairs={{0,8},{1,9},{2,10},{3,11},{4,12},{5,13},{6,14},{7,15},{8,0},{9,1},... | collective-permute-start | bytes 1769480 | tf_op jit(solution)/shard_map/ppermute | solution.py:52
  21.4 6.7 %collective-permute-start.6 = (bf16[128,1152]{1,0:T(8,128)(2,1)S(1)}, bf16[128,1152]{1,0:T(8,128)(2,1)S(1)}, u32[]{:S(2)}, u32[]{:S(2)}) collective-permute-start(bf16[128,1152]{1,0:T(8,128)(2,1)S(1)} %collective-permute-done.1), channel_id=1, source_target_pairs={{0,16},{1,17},{2,18},{3,19},{4,20},{5,21},{6,22},{7,23},{8,120},{9... | collective-permute-start | bytes 884744 | tf_op jit(solution)/shard_map/ppermute | solution.py:52
  28.1 6.2 %collective-permute-start.7 = (bf16[128,1152]{1,0:T(8,128)(2,1)S(1)}, bf16[128,1152]{1,0:T(8,128)(2,1)S(1)}, u32[]{:S(2)}, u32[]{:S(2)}) collective-permute-start(bf16[128,1152]{1,0:T(8,128)(2,1)S(1)} %collective-permute-done.6.refs_0_.refs_2_.refs_6_.refs_5_), channel_id=1, source_target_pairs={{0,8},{1,9},{2,10},{3,11},{4,12},{5,13},{6,14},{7,15},{8,0},{9,1},... | collective-permute-start | bytes 884744 | tf_op jit(solution)/shard_map/ppermute | solution.py:52
  28.3 7.8 %collective-permute-start.11 = (bf16[128,1152]{1,0:T(8,128)(2,1)S(1)}, bf16[128,1152]{1,0:T(8,128)(2,1)S(1)}, u32[]{:S(2)}, u32[]{:S(2)}) collective-permute-start(bf16[128,1152]{1,0:T(8,128)(2,1)S(1)} %slice.105), channel_id=1, source_target_pairs={{0,132},{1,133},{2,134},{3,135},{4,128},{5,129},{6,130},{7,131},{8... | collective-permute-start | bytes 884744 | tf_op jit(solution)/shard_map/ppermute | solution.py:52
  28.4 8.0 %collective-permute-start.12 = (bf16[128,1152]{1,0:T(8,128)(2,1)S(1)}, bf16[128,1152]{1,0:T(8,128)(2,1)S(1)}, u32[]{:S(2)}, u32[]{:S(2)}) collective-permute-start(bf16[128,1152]{1,0:T(8,128)(2,1)S(1)} %slice.106), channel_id=1, source_target_pairs={{0,3},{1,2},{2,1},{3,0},{4,7},{5,6},{6,5},{7,4},{8,9},{9,8},{10,11... | collective-permute-start | bytes 884744 | tf_op jit(solution)/shard_map/ppermute | solution.py:52
  30.6 7.9 %collective-permute-start.10 = (bf16[128,1152]{1,0:T(8,128)(2,1)S(1)}, bf16[128,1152]{1,0:T(8,128)(2,1)S(1)}, u32[]{:S(2)}, u32[]{:S(2)}) collective-permute-start(bf16[128,1152]{1,0:T(8,128)(2,1)S(1)} %collective-permute-done.6.refs_0_.refs_2_.refs_6_.refs_5_), channel_id=1, source_target_pairs={{0,112},{1,113},{2,114},{3,115},{4,116},{5,117},{6,118},{7,119},{8... | collective-permute-start | bytes 884744 | tf_op jit(solution)/shard_map/ppermute | solution.py:52
  38.6 17.3 %collective-permute-start.16 = (bf16[128,1152]{1,0:T(8,128)(2,1)S(1)}, bf16[128,1152]{1,0:T(8,128)(2,1)S(1)}, u32[]{:S(2)}, u32[]{:S(2)}) collective-permute-start(bf16[128,1152]{1,0:T(8,128)(2,1)S(1)} %get-tuple-element.18), channel_id=1, source_target_pairs={{0,8},{1,9},{2,10},{3,11},{4,12},{5,13},{6,14},{7,15},{8,0},{9,1},... | collective-permute-start | bytes 884744 | tf_op jit(solution)/shard_map/ppermute | solution.py:52
  43.4 10.7 %collective-permute-start.17 = (bf16[128,1152]{1,0:T(8,128)(2,1)S(1)}, bf16[128,1152]{1,0:T(8,128)(2,1)S(1)}, u32[]{:S(2)}, u32[]{:S(2)}) collective-permute-start(bf16[128,1152]{1,0:T(8,128)(2,1)S(1)} %add_convert_fusion.1), channel_id=1, source_target_pairs={{0,112},{1,113},{2,114},{3,115},{4,116},{5,117},{6,118},{7,119},{8... | collective-permute-start | bytes 884744 | tf_op jit(solution)/shard_map/ppermute | solution.py:52
  47.5 16.5 %collective-permute-start.19 = (bf16[256,1152]{1,0:T(8,128)(2,1)S(1)}, bf16[256,1152]{1,0:T(8,128)(2,1)S(1)}, u32[]{:S(2)}, u32[]{:S(2)}) collective-permute-start(bf16[256,1152]{1,0:T(8,128)(2,1)S(1)} %shard_map.77), channel_id=1, source_target_pairs={{0,135},{1,134},{2,133},{3,132},{4,131},{5,130},{6,129},{7,128},{8... | collective-permute-start | bytes 1769480 | tf_op jit(solution)/shard_map/ppermute | solution.py:52
  50.5 5.6 %collective-permute-start.15 = (bf16[256,1152]{1,0:T(8,128)(2,1)S(1)}, bf16[256,1152]{1,0:T(8,128)(2,1)S(1)}, u32[]{:S(2)}, u32[]{:S(2)}) collective-permute-start(bf16[256,1152]{1,0:T(8,128)(2,1)S(1)} %get-tuple-element.23), channel_id=1, source_target_pairs={{0,8},{1,9},{2,10},{3,11},{4,12},{5,13},{6,14},{7,15},{8,0},{9,1},... | collective-permute-start | bytes 1769480 | tf_op jit(solution)/shard_map/ppermute | solution.py:52
  51.4 13.4 %collective-permute-start.20 = (bf16[256,1152]{1,0:T(8,128)(2,1)S(1)}, bf16[256,1152]{1,0:T(8,128)(2,1)S(1)}, u32[]{:S(2)}, u32[]{:S(2)}) collective-permute-start(bf16[256,1152]{1,0:T(8,128)(2,1)S(1)} %shard_map.78), channel_id=1, source_target_pairs={{0,3},{1,2},{2,1},{3,0},{4,7},{5,6},{6,5},{7,4},{8,9},{9,8},{10,11... | collective-permute-start | bytes 1769480 | tf_op jit(solution)/shard_map/ppermute | solution.py:52
  54.1 11.8 %collective-permute-start.21 = (bf16[256,1152]{1,0:T(8,128)(2,1)S(1)}, bf16[256,1152]{1,0:T(8,128)(2,1)S(1)}, u32[]{:S(2)}, u32[]{:S(2)}) collective-permute-start(bf16[256,1152]{1,0:T(8,128)(2,1)S(1)} %shard_map.79), channel_id=1, source_target_pairs={{0,132},{1,133},{2,134},{3,135},{4,128},{5,129},{6,130},{7,131},{8... | collective-permute-start | bytes 1769480 | tf_op jit(solution)/shard_map/ppermute | solution.py:52
  55.9 6.8 %collective-permute-start.18 = (bf16[128,1152]{1,0:T(8,128)(2,1)S(1)}, bf16[128,1152]{1,0:T(8,128)(2,1)S(1)}, u32[]{:S(2)}, u32[]{:S(2)}) collective-permute-start(bf16[128,1152]{1,0:T(8,128)(2,1)S(1)} %add_convert_fusion), channel_id=1, source_target_pairs={{0,16},{1,17},{2,18},{3,19},{4,20},{5,21},{6,22},{7,23},{8,120},{9... | collective-permute-start | bytes 884744 | tf_op jit(solution)/shard_map/ppermute | solution.py:52
  62.8 8.0 %collective-permute-start.25 = (bf16[128,1152]{1,0:T(8,128)(2,1)S(1)}, bf16[128,1152]{1,0:T(8,128)(2,1)S(1)}, u32[]{:S(2)}, u32[]{:S(2)}) collective-permute-start(bf16[128,1152]{1,0:T(8,128)(2,1)S(1)} %slice_add_fusion.1), channel_id=1, source_target_pairs={{0,112},{1,113},{2,114},{3,115},{4,116},{5,117},{6,118},{7,119},{8... | collective-permute-start | bytes 884744 | tf_op jit(solution)/shard_map/ppermute | solution.py:52
  66.2 6.1 %collective-permute-start.22 = (bf16[64,1152]{1,0:T(8,128)(2,1)S(1)}, bf16[64,1152]{1,0:T(8,128)(2,1)S(1)}, u32[]{:S(2)}, u32[]{:S(2)}) collective-permute-start(bf16[64,1152]{1,0:T(8,128)(2,1)S(1)} %get-tuple-element.34), channel_id=1, source_target_pairs={{0,5},{1,4},{2,7},{3,6},{4,1},{5,0},{6,3},{7,2},{8,143},{9,142},{1... | collective-permute-start | bytes 442376 | tf_op jit(solution)/shard_map/ppermute | solution.py:52
  67.7 7.7 %collective-permute-start.23 = (bf16[64,1152]{1,0:T(8,128)(2,1)S(1)}, bf16[64,1152]{1,0:T(8,128)(2,1)S(1)}, u32[]{:S(2)}, u32[]{:S(2)}) collective-permute-start(bf16[64,1152]{1,0:T(8,128)(2,1)S(1)} %get-tuple-element.33), channel_id=1, source_target_pairs={{0,1},{1,0},{2,3},{3,2},{4,5},{5,4},{6,7},{7,6},{8,11},{9,10},{10,... | collective-permute-start | bytes 442376 | tf_op jit(solution)/shard_map/ppermute | solution.py:52
  70.9 6.0 %collective-permute-start.26 = (bf16[64,1152]{1,0:T(8,128)(2,1)S(1)}, bf16[64,1152]{1,0:T(8,128)(2,1)S(1)}, u32[]{:S(2)}, u32[]{:S(2)}) collective-permute-start(bf16[64,1152]{1,0:T(8,128)(2,1)S(1)} %slice.128), channel_id=1, source_target_pairs={{0,16},{1,17},{2,18},{3,19},{4,20},{5,21},{6,22},{7,23},{8,120},{9... | collective-permute-start | bytes 442376 | tf_op jit(solution)/shard_map/ppermute | solution.py:52
  (7 other events, 20.7 us)

commit v4 on v3

--- a/solution.py
+++ b/solution.py
@@ -75,19 +75,16 @@
     return jnp.concatenate(parts, axis=0)
 
 
-def send_kernel(rows, *rest):
-    rest[-1][...] = rounded(unit_rows(rows[...])[0])
-
-
-def send_rows(rows, *earlier):
-    whole = pl.BlockSpec(memory_space=pltpu.VMEM)
-    return pl.pallas_call(
-        send_kernel,
-        out_shape=jax.ShapeDtypeStruct(rows.shape, jnp.bfloat16),
-        in_specs=[whole] * (1 + len(earlier)),
-        out_specs=whole,
-        compiler_params=pltpu.CompilerParams(vmem_limit_bytes=4 * 2**20),
-    )(rows, *earlier)
+def unit_kernel(rows, units):
+    units[...] = rounded(unit_rows(rows[...])[0])
+
+
+def block_kernel(own, *refs):
+    *arrived, block = refs
+    n = own.shape[0]
+    block[pl.ds(0, n)] = own[...]
+    for index, rows in enumerate(arrived):
+        block[pl.ds((index + 1) * n, n)] = rounded(unit_rows(rows[...])[0])
 
 
 def grad_kernel(coefficients, rows, others, sums, *rest):
@@ -202,8 +199,13 @@
     n, d = images.shape
     a, b, q = 4 * n, 2 * n, 4 * n
     coefficients = join(*[jnp.broadcast_to(v, (4, 128)) for v in (logit_scale, logit_bias)])
-    text_send = send_rows(texts)
-    image_send = send_rows(images, text_send)
+    coefficients = join(*[jnp.broadcast_to(v, (4, 128)) for v in (logit_scale, logit_bias)])
+
+    def units_of(rows):
+        return on_device(unit_kernel, [((n, d), bf16)], rows)[0]
+
+    def block_of(own, *arrived):
+        return on_device(block_kernel, [(((1 + len(arrived)) * n, d), bf16)], own, *arrived)[0]
 
     def weigh(some_texts, some_images, share=1):
         m = sum(v.shape[0] for v in some_texts)
@@ -213,9 +215,10 @@
             coefficients, *some_texts, *some_images, products=share * m * k,
         )[0]
 
-    r1 = z1(text_send)
-    quad = join(image_send, after(x1(image_send), coefficients), y1(image_send), d1(image_send))
-    pair = join(text_send, r1)
+    raw = (d1(images), x1(images), y1(images), z1(texts), units_of(texts), units_of(images), coefficients)
+    raw_d, raw_x, raw_y, raw_t, own_text, own_image, coefficients = lax.optimization_barrier(raw)
+    pair = block_of(own_text, raw_t)
+    quad = block_of(own_image, raw_x, raw_y, raw_d)
     r2 = z2(pair)
     part_x, part_y = x2(quad), y2(quad)
     r3 = z1(r2)
@@ -223,11 +226,10 @@
     r4 = z2(r3)
     own_a = join(pair, r2)
     sib_a = sibling(own_a)
-    w_aq = weigh((own_a, sib_a), (quad,))
-    w_axy = weigh((own_a, sib_a), (part_x, part_y))
+    w_aq = weigh((own_a, sib_a), (quad,), share=0)
+    w_axy = weigh((own_a, sib_a), (part_x, part_y), share=0)
+    w_ad = weigh((after(own_a, w_aq, w_axy), sib_a), (top_d, low_d), share=40)
     sib_b = sibling(r3)
-    w_bqxy = weigh((r3, sib_b), (quad, part_x, part_y))
-    w_d = weigh((after(own_a, w_aq, w_axy, w_bqxy), sib_a, r3, sib_b), (top_d, low_d), share=40)
     all_images = (quad, part_x, part_y, top_d, low_d)
 
     def near(rows, *blocks, products=0):
@@ -236,7 +238,8 @@
             *blocks, *all_images, products=products,
         )
 
-    sums_own_b, send_b = near(b, w_bqxy, w_d[2 * a :], products=40 * 2 * b * 4 * q)
+    w_b = weigh((after(r3, w_ad), sib_b), all_images)
+    sums_own_b, send_b = near(b, w_b, products=2 * b * 4 * q)
     r4 = after(r4, send_b)
     back_b = sibling(send_b)
     sib_c = sibling(r4)
@@ -248,7 +251,7 @@
     (sums_own_c,) = on_device(
         text_kernel, [((b, d), f32)], w_own, *all_images, products=b * 4 * q
     )
-    s4 = rounded(sums_own_c + widened(sibling(send_c)))
+    back_c = sibling(send_c)
     all_texts = (own_a, sib_a, r3, sib_b, r4, sib_c)
 
     def image_part(kind, *blocks, share=1):
@@ -259,19 +262,21 @@
 
     def late(index, *others):
         span = slice(index * q, (index + 1) * q)
-        return after(w_own[:, span], *others), w_sib[:, span]
-
-    back_d = d2(image_part(bf16, w_d, *late(3)))
-    send_x = image_part(bf16, w_axy[:, :q], w_bqxy[:, q : 2 * q], *late(1, s4))
-    send_y = image_part(bf16, w_axy[:, q:], w_bqxy[:, 2 * q :], *late(2, s4))
+        return after(w_b[:, span], *others), w_own[:, span], w_sib[:, span]
+
+    send_d = image_part(bf16, w_ad, *late(3))
+    back_d = d2(send_d)
+    s4 = rounded(after(sums_own_c, send_d) + widened(back_c))
+    send_x = image_part(bf16, w_axy[:, :q], *late(1, s4))
+    send_y = image_part(bf16, w_axy[:, q:], *late(2, s4))
     back_x, back_y = x2(send_x), y2(send_y)
-    sums_own, send_a = near(a, after(w_aq, s4), w_axy, w_d[: 2 * a], products=2 * a * 4 * q)
+    sums_own, send_a = near(a, after(w_aq, s4), w_axy, w_ad, products=2 * a * 4 * q)
     back_a = sibling(send_a)
     s4 = after(z2(s4), send_a)
     s3 = sums_own_b + widened(back_b) + widened(s4)
     near_sums = sums_own + widened(back_a)
     s2 = near_sums[2 * n :] + widened(z1(rounded(s3)))
-    quad_sums = image_part(f32, w_aq, w_bqxy[:, :q], *late(0, s2), share=1)
+    quad_sums = image_part(f32, w_aq, *late(0, s2))
     s01 = near_sums[: 2 * n] + widened(z2(rounded(s2)))
     quad_sums = quad_sums + widened(back_d) + widened(back_x) + widened(back_y)
     text_grad = grad_rows(coefficients, texts, images, s01[:n], z1(rounded(s01[n:])))

time: 78.8 us -> 77 us (0.977)
  waiting for transfers between devices: 22 us -> 18.6 us
  starting transfers between devices: 36.7 us -> 38 us
    ppermute x27, waiting for transfers between devices: 22 us -> 18.6 us  [exchange(): return lambda value: lax.ppermute(value, AXES, pairs)]
    ppermute x27, starting transfers between devices: 36.7 us -> 38 us  [exchange(): return lambda value: lax.ppermute(value, AXES, pairs)]
    pallas_call x13 -> x17, Pallas kernels: 11.8 us -> 12.4 us  [on_device(): pl.pallas_call(kernel, out_shape=[jax.ShapeDtypeStruct(shape, kind) for s...]
where the time goes in v4:
time: 77 us; the launch traced here: 76.2 us
  starting transfers between devices  38 us (49%)
  waiting for transfers between devices  18.6 us (24%)
  Pallas kernels  14.4 us (19%)
  between operations  2.27 us (3%)
  local copies, waits for them, and re-layouts  2.19 us (3%)
    ppermute x27, starting transfers between devices, exchange(): return lambda value: lax.ppermute(value, AXES, pairs)  38 us
    ppermute x27, waiting for transfers between devices, exchange(): return lambda value: lax.ppermute(value, AXES, pairs)  18.6 us
    pallas_call x17, Pallas kernels, on_device(): pl.pallas_call(kernel, out_shape=[jax.ShapeDtypeStruct(shape, kind) for s...  12.4 us
    pallas_call x2, Pallas kernels, grad_rows(): pl.pallas_call(grad_kernel, out_shape=jax.ShapeDtypeStruct(rows.shape, jn...  2.03 us
    unnamed x8, local copies, waits for them, and re-layouts  1.86 us
  transfers between devices with their start and end apart: 27, of which 11 were waited for; matrix products, arithmetic and copies ran while one was open for 1% of the time, Pallas kernels for 17%

profile of v4, /device:TPU:8, one launch (start us, length us, event | category | flops | bytes accessed | tf_op | source)
XLA Modules:
  0.0 76.2 jit_solution(17792075509744393591)
XLA Ops:
  0.6 1.5 %collective-permute-start = (bf16[64,1152]{1,0:T(8,128)(2,1)}, bf16[64,1152]{1,0:T(8,128)(2,1)S(1)}, u32[]{:S(2)}, u32[]{:S(2)}) collective-permute-start(bf16[64,1152]{1,0:T(8,128)(2,1)} %others.3), channel_id=1, source_target_pairs={{0,5},{1,4},{2,7},{3,6},{4,1},{5,0},{6,3},{7,2},{8,143},{9,142},{1... | collective-permute-start | bytes 442376 | tf_op jit(solution)/shard_map/ppermute | solution.py:52
  2.1 2.3 %collective-permute-start.1 = (bf16[64,1152]{1,0:T(8,128)(2,1)}, bf16[64,1152]{1,0:T(8,128)(2,1)S(1)}, u32[]{:S(2)}, u32[]{:S(2)}) collective-permute-start(bf16[64,1152]{1,0:T(8,128)(2,1)} %others.3), channel_id=1, source_target_pairs={{0,1},{1,0},{2,3},{3,2},{4,5},{5,4},{6,7},{7,6},{8,11},{9,10},{10,... | collective-permute-start | bytes 442376 | tf_op jit(solution)/shard_map/ppermute | solution.py:52
  4.4 1.8 %collective-permute-start.3 = (bf16[64,1152]{1,0:T(8,128)(2,1)}, bf16[64,1152]{1,0:T(8,128)(2,1)S(1)}, u32[]{:S(2)}, u32[]{:S(2)}) collective-permute-start(bf16[64,1152]{1,0:T(8,128)(2,1)} %rows.7), channel_id=1, source_target_pairs={{0,16},{1,17},{2,18},{3,19},{4,20},{5,21},{6,22},{7,23},{8,120},{9... | collective-permute-start | bytes 442376 | tf_op jit(solution)/shard_map/ppermute | solution.py:52
  9.9 5.8 %collective-permute-start.4 = (bf16[128,1152]{1,0:T(8,128)(2,1)S(1)}, bf16[128,1152]{1,0:T(8,128)(2,1)S(1)}, u32[]{:S(2)}, u32[]{:S(2)}) collective-permute-start(bf16[128,1152]{1,0:T(8,128)(2,1)S(1)} %shard_map.67), channel_id=1, source_target_pairs={{0,112},{1,113},{2,114},{3,115},{4,116},{5,117},{6,118},{7,119},{8... | collective-permute-start | bytes 884744 | tf_op jit(solution)/shard_map/ppermute | solution.py:52
  15.9 1.7 %collective-permute-start.8 = (bf16[256,1152]{1,0:T(8,128)(2,1)S(1)}, bf16[256,1152]{1,0:T(8,128)(2,1)S(1)}, u32[]{:S(2)}, u32[]{:S(2)}) collective-permute-start(bf16[256,1152]{1,0:T(8,128)(2,1)S(1)} %shard_map.68.refs_2_.refs_1_.refs_0_.quad.refs_3_), channel_id=1, source_target_pairs={{0,132},{1,133},{2,134},{3,135},{4,128},{5,129},{6,130},{7,131},{8... | collective-permute-start | bytes 1769480 | tf_op jit(solution)/shard_map/ppermute | solution.py:52
  17.5 2.8 %collective-permute-start.7 = (bf16[256,1152]{1,0:T(8,128)(2,1)S(1)}, bf16[256,1152]{1,0:T(8,128)(2,1)S(1)}, u32[]{:S(2)}, u32[]{:S(2)}) collective-permute-start(bf16[256,1152]{1,0:T(8,128)(2,1)S(1)} %shard_map.68.refs_2_.refs_1_.refs_0_.quad.refs_3_), channel_id=1, source_target_pairs={{0,3},{1,2},{2,1},{3,0},{4,7},{5,6},{6,5},{7,4},{8,9},{9,8},{10,11... | collective-permute-start | bytes 1769480 | tf_op jit(solution)/shard_map/ppermute | solution.py:52
  20.6 5.2 %collective-permute-done.8.refs_3_.refs_4_.refs_2_.part_y.refs_5_ = bf16[256,1152]{1,0:T(8,128)(2,1)S(1)} collective-permute-done((bf16[256,1152]{1,0:T(8,128)(2,1)S(1)}, bf16[256,1152]{1,0:T(8,128)(2,1)S(1)}, u32[]{:S(2)}, u32[]{:S(2)}) %collective-permute-start.8) | collective-permute-done | bytes 589856 | tf_op jit(solution)/shard_map/ppermute | solution.py:52
  25.9 2.8 %collective-permute-start.10 = (bf16[128,1152]{1,0:T(8,128)(2,1)S(1)}, bf16[128,1152]{1,0:T(8,128)(2,1)S(1)}, u32[]{:S(2)}, u32[]{:S(2)}) collective-permute-start(bf16[128,1152]{1,0:T(8,128)(2,1)S(1)} %slice.101), channel_id=1, source_target_pairs={{0,3},{1,2},{2,1},{3,0},{4,7},{5,6},{6,5},{7,4},{8,9},{9,8},{10,11... | collective-permute-start | bytes 884744 | tf_op jit(solution)/shard_map/ppermute | solution.py:52
  28.7 1.7 %collective-permute-start.9 = (bf16[128,1152]{1,0:T(8,128)(2,1)S(1)}, bf16[128,1152]{1,0:T(8,128)(2,1)S(1)}, u32[]{:S(2)}, u32[]{:S(2)}) collective-permute-start(bf16[128,1152]{1,0:T(8,128)(2,1)S(1)} %slice.100), channel_id=1, source_target_pairs={{0,132},{1,133},{2,134},{3,135},{4,128},{5,129},{6,130},{7,131},{8... | collective-permute-start | bytes 884744 | tf_op jit(solution)/shard_map/ppermute | solution.py:52
  31.4 1.0 %shard_map.70.refs_1_ = bf16[512,512]{1,0:T(8,128)(2,1)S(1)} custom-call(f32[8,128]{1,0:T(8,128)S(1)} %concatenate.9.coefficients, bf16[256,1152]{1,0:T(8,128)(2,1)S(1)} %pad_maximum_fusion.refs_0_.refs_4_, bf16[256,1152]{1,0:T(8,128)(2,1)S(1)} %collective-permute-done.5.refs_1_.refs_5_, ...), custom_call_target="tpu_custom_call" | custom-call | tf_op jit(solution)/shard_map/pallas_call | solution.py:177
  33.9 1.7 %collective-permute-done.9.refs_2_.refs_5_.refs_4_.refs_3_.top_d.refs_6_ = bf16[128,1152]{1,0:T(8,128)(2,1)S(1)} collective-permute-done((bf16[128,1152]{1,0:T(8,128)(2,1)S(1)}, bf16[128,1152]{1,0:T(8,128)(2,1)S(1)}, u32[]{:S(2)}, u32[]{:S(2)}) %collective-permute-start.9) | collective-permute-done | bytes 294944 | tf_op jit(solution)/shard_map/ppermute | solution.py:52
  36.1 1.0 %shard_map.72.refs_0_ = bf16[256,1024]{1,0:T(8,128)(2,1)S(1)} custom-call(f32[8,128]{1,0:T(8,128)S(1)} %concatenate.9.coefficients, bf16[128,1152]{1,0:T(8,128)(2,1)S(1)} %collective-permute-done.6.refs_0_.refs_6_, bf16[128,1152]{1,0:T(8,128)(2,1)S(1)} %collective-permute-done.11.refs_1_.refs_7_, ...), custom_call_target="tpu_custom_call" | custom-call | flops 603979776 | tf_op jit(solution)/shard_map/pallas_call | solution.py:177
  40.1 1.4 %shard_map.76 = (bf16[128,1024]{1,0:T(8,128)(2,1)S(1)}, bf16[128,1152]{1,0:T(8,128)(2,1)S(1)}) custom-call(f32[8,128]{1,0:T(8,128)S(1)} %concatenate.9.coefficients, bf16[128,1152]{1,0:T(8,128)(2,1)S(1)} %collective-permute-done.13.sib_c.refs_9_, bf16[256,1152]{1,0:T(8,128)(2,1)S(1)} %shard_map.68.refs_2_.refs_1_.refs_0_.quad.refs_3_, ...), custom_call_target="tpu_custom_call" | custom-call | flops 603979776 | tf_op jit(solution)/shard_map/pallas_call | solution.py:177
  44.1 3.9 %collective-permute-start.19 = (bf16[256,1152]{1,0:T(8,128)(2,1)S(1)}, bf16[256,1152]{1,0:T(8,128)(2,1)S(1)}, u32[]{:S(2)}, u32[]{:S(2)}) collective-permute-start(bf16[256,1152]{1,0:T(8,128)(2,1)S(1)} %shard_map.77), channel_id=1, source_target_pairs={{0,135},{1,134},{2,133},{3,132},{4,131},{5,130},{6,129},{7,128},{8... | collective-permute-start | bytes 1769480 | tf_op jit(solution)/shard_map/ppermute | solution.py:52
  48.0 1.5 %shard_map.78 = (f32[256,1152]{1,0:T(8,128)S(1)}, bf16[256,1152]{1,0:T(8,128)(2,1)S(1)}) custom-call(bf16[512,256]{1,0:T(8,128)(2,1)S(1)} %shard_map.69.refs_0_, bf16[512,512]{1,0:T(8,128)(2,1)S(1)} %shard_map.70.refs_1_, bf16[512,256]{1,0:T(8,128)(2,1)S(1)} %shard_map.71.refs_0_.refs_2_, ...), custom_call_target="tpu_custom_call" | custom-call | flops 1207959552 | tf_op jit(solution)/shard_map/pallas_call | solution.py:177
  51.9 1.2 %collective-permute-start.21 = (bf16[256,1152]{1,0:T(8,128)(2,1)S(1)}, bf16[256,1152]{1,0:T(8,128)(2,1)S(1)}, u32[]{:S(2)}, u32[]{:S(2)}) collective-permute-start(bf16[256,1152]{1,0:T(8,128)(2,1)S(1)} %shard_map.81), channel_id=1, source_target_pairs={{0,132},{1,133},{2,134},{3,135},{4,128},{5,129},{6,130},{7,131},{8... | collective-permute-start | bytes 1769480 | tf_op jit(solution)/shard_map/ppermute | solution.py:52
  53.2 1.8 %collective-permute-start.18 = (bf16[128,1152]{1,0:T(8,128)(2,1)S(1)}, bf16[128,1152]{1,0:T(8,128)(2,1)S(1)}, u32[]{:S(2)}, u32[]{:S(2)}) collective-permute-start(bf16[128,1152]{1,0:T(8,128)(2,1)S(1)} %add_convert_fusion), channel_id=1, source_target_pairs={{0,16},{1,17},{2,18},{3,19},{4,20},{5,21},{6,22},{7,23},{8,120},{9... | collective-permute-start | bytes 884744 | tf_op jit(solution)/shard_map/ppermute | solution.py:52
  55.2 4.9 %collective-permute-done.18 = bf16[128,1152]{1,0:T(8,128)(2,1)S(1)} collective-permute-done((bf16[128,1152]{1,0:T(8,128)(2,1)S(1)}, bf16[128,1152]{1,0:T(8,128)(2,1)S(1)}, u32[]{:S(2)}, u32[]{:S(2)}) %collective-permute-start.18) | collective-permute-done | bytes 294944 | tf_op jit(solution)/shard_map/ppermute | solution.py:52
  60.1 1.9 %collective-permute-start.25 = (bf16[128,1152]{1,0:T(8,128)(2,1)S(1)}, bf16[128,1152]{1,0:T(8,128)(2,1)S(1)}, u32[]{:S(2)}, u32[]{:S(2)}) collective-permute-start(bf16[128,1152]{1,0:T(8,128)(2,1)S(1)} %slice_add_fusion.1), channel_id=1, source_target_pairs={{0,112},{1,113},{2,114},{3,115},{4,116},{5,117},{6,118},{7,119},{8... | collective-permute-start | bytes 884744 | tf_op jit(solution)/shard_map/ppermute | solution.py:52
  63.2 2.8 %collective-permute-start.22 = (bf16[64,1152]{1,0:T(8,128)(2,1)S(1)}, bf16[64,1152]{1,0:T(8,128)(2,1)S(1)}, u32[]{:S(2)}, u32[]{:S(2)}) collective-permute-start(bf16[64,1152]{1,0:T(8,128)(2,1)S(1)} %get-tuple-element.50), channel_id=1, source_target_pairs={{0,5},{1,4},{2,7},{3,6},{4,1},{5,0},{6,3},{7,2},{8,143},{9,142},{1... | collective-permute-start | bytes 442376 | tf_op jit(solution)/shard_map/ppermute | solution.py:52
  66.0 3.0 %collective-permute-start.23 = (bf16[64,1152]{1,0:T(8,128)(2,1)S(1)}, bf16[64,1152]{1,0:T(8,128)(2,1)S(1)}, u32[]{:S(2)}, u32[]{:S(2)}) collective-permute-start(bf16[64,1152]{1,0:T(8,128)(2,1)S(1)} %get-tuple-element.49), channel_id=1, source_target_pairs={{0,1},{1,0},{2,3},{3,2},{4,5},{5,4},{6,7},{7,6},{8,11},{9,10},{10,... | collective-permute-start | bytes 442376 | tf_op jit(solution)/shard_map/ppermute | solution.py:52
  69.3 4.3 %collective-permute-done.23.rest_1_ = bf16[64,1152]{1,0:T(8,128)(2,1)S(1)} collective-permute-done((bf16[64,1152]{1,0:T(8,128)(2,1)S(1)}, bf16[64,1152]{1,0:T(8,128)(2,1)S(1)}, u32[]{:S(2)}, u32[]{:S(2)}) %collective-permute-start.23) | collective-permute-done | bytes 147488 | tf_op jit(solution)/shard_map/ppermute | solution.py:52
  74.1 1.0 %shard_map.82 = f32[64,1152]{1,0:T(8,128)} custom-call(f32[8,128]{1,0:T(8,128)S(1)} %concatenate.9.coefficients, bf16[64,1152]{1,0:T(8,128)(2,1)S(1)} %copy-done.1, bf16[64,1152]{1,0:T(8,128)(2,1)S(1)} %copy-done.3, f32[64,1152]{1,0:T(8,128)S(1)} %slice.113.sums, bf16[64,1152]{1,0:T(8,128)(2,1)S(1)} %collective-permute-done.22.rest_0_, ...), custom_call_target="tpu_custom_call" | custom-call | tf_op jit(solution)/shard_map/pallas_call | solution.py:102
  75.2 1.0 %shard_map.83 = f32[64,1152]{1,0:T(8,128)} custom-call(f32[8,128]{1,0:T(8,128)S(1)} %concatenate.9.coefficients, bf16[64,1152]{1,0:T(8,128)(2,1)S(1)} %copy-done.3, bf16[64,1152]{1,0:T(8,128)(2,1)S(1)} %copy-done.1, f32[64,1152]{1,0:T(8,128)S(1)} %slice.118.sums, bf16[64,1152]{1,0:T(8,128)(2,1)S(1)} %collective-permute-done.26.rest_0_), custom_call_target="tpu_custom_call" | custom-call | tf_op jit(solution)/shard_map/pallas_call | solution.py:102
  (77 shorter events, 16.2 us)
Async XLA Ops:
  0.6 8.9 %collective-permute-start = (bf16[64,1152]{1,0:T(8,128)(2,1)}, bf16[64,1152]{1,0:T(8,128)(2,1)S(1)}, u32[]{:S(2)}, u32[]{:S(2)}) collective-permute-start(bf16[64,1152]{1,0:T(8,128)(2,1)} %others.3), channel_id=1, source_target_pairs={{0,5},{1,4},{2,7},{3,6},{4,1},{5,0},{6,3},{7,2},{8,143},{9,142},{1... | collective-permute-start | bytes 442376 | tf_op jit(solution)/shard_map/ppermute | solution.py:52
  2.1 7.5 %collective-permute-start.1 = (bf16[64,1152]{1,0:T(8,128)(2,1)}, bf16[64,1152]{1,0:T(8,128)(2,1)S(1)}, u32[]{:S(2)}, u32[]{:S(2)}) collective-permute-start(bf16[64,1152]{1,0:T(8,128)(2,1)} %others.3), channel_id=1, source_target_pairs={{0,1},{1,0},{2,3},{3,2},{4,5},{5,4},{6,7},{7,6},{8,11},{9,10},{10,... | collective-permute-start | bytes 442376 | tf_op jit(solution)/shard_map/ppermute | solution.py:52
  4.4 5.4 %collective-permute-start.2 = (bf16[64,1152]{1,0:T(8,128)(2,1)}, bf16[64,1152]{1,0:T(8,128)(2,1)S(1)}, u32[]{:S(2)}, u32[]{:S(2)}) collective-permute-start(bf16[64,1152]{1,0:T(8,128)(2,1)} %others.3), channel_id=1, source_target_pairs={{0,4},{1,5},{2,6},{3,7},{4,0},{5,1},{6,2},{7,3},{8,140},{9,141},{1... | collective-permute-start | bytes 442376 | tf_op jit(solution)/shard_map/ppermute | solution.py:52
  4.4 5.4 %collective-permute-start.3 = (bf16[64,1152]{1,0:T(8,128)(2,1)}, bf16[64,1152]{1,0:T(8,128)(2,1)S(1)}, u32[]{:S(2)}, u32[]{:S(2)}) collective-permute-start(bf16[64,1152]{1,0:T(8,128)(2,1)} %rows.7), channel_id=1, source_target_pairs={{0,16},{1,17},{2,18},{3,19},{4,20},{5,21},{6,22},{7,23},{8,120},{9... | collective-permute-start | bytes 442376 | tf_op jit(solution)/shard_map/ppermute | solution.py:52
  9.9 10.5 %collective-permute-start.4 = (bf16[128,1152]{1,0:T(8,128)(2,1)S(1)}, bf16[128,1152]{1,0:T(8,128)(2,1)S(1)}, u32[]{:S(2)}, u32[]{:S(2)}) collective-permute-start(bf16[128,1152]{1,0:T(8,128)(2,1)S(1)} %shard_map.67), channel_id=1, source_target_pairs={{0,112},{1,113},{2,114},{3,115},{4,116},{5,117},{6,118},{7,119},{8... | collective-permute-start | bytes 884744 | tf_op jit(solution)/shard_map/ppermute | solution.py:52
  15.9 10.0 %collective-permute-start.8 = (bf16[256,1152]{1,0:T(8,128)(2,1)S(1)}, bf16[256,1152]{1,0:T(8,128)(2,1)S(1)}, u32[]{:S(2)}, u32[]{:S(2)}) collective-permute-start(bf16[256,1152]{1,0:T(8,128)(2,1)S(1)} %shard_map.68.refs_2_.refs_1_.refs_0_.quad.refs_3_), channel_id=1, source_target_pairs={{0,132},{1,133},{2,134},{3,135},{4,128},{5,129},{6,130},{7,131},{8... | collective-permute-start | bytes 1769480 | tf_op jit(solution)/shard_map/ppermute | solution.py:52
  17.5 11.2 %collective-permute-start.7 = (bf16[256,1152]{1,0:T(8,128)(2,1)S(1)}, bf16[256,1152]{1,0:T(8,128)(2,1)S(1)}, u32[]{:S(2)}, u32[]{:S(2)}) collective-permute-start(bf16[256,1152]{1,0:T(8,128)(2,1)S(1)} %shard_map.68.refs_2_.refs_1_.refs_0_.quad.refs_3_), channel_id=1, source_target_pairs={{0,3},{1,2},{2,1},{3,0},{4,7},{5,6},{6,5},{7,4},{8,9},{9,8},{10,11... | collective-permute-start | bytes 1769480 | tf_op jit(solution)/shard_map/ppermute | solution.py:52
  20.4 10.9 %collective-permute-start.5 = (bf16[256,1152]{1,0:T(8,128)(2,1)S(1)}, bf16[256,1152]{1,0:T(8,128)(2,1)S(1)}, u32[]{:S(2)}, u32[]{:S(2)}) collective-permute-start(bf16[256,1152]{1,0:T(8,128)(2,1)S(1)} %pad_maximum_fusion.refs_0_.refs_4_), channel_id=1, source_target_pairs={{0,8},{1,9},{2,10},{3,11},{4,12},{5,13},{6,14},{7,15},{8,0},{9,1},... | collective-permute-start | bytes 1769480 | tf_op jit(solution)/shard_map/ppermute | solution.py:52
  20.5 9.9 %collective-permute-start.6 = (bf16[128,1152]{1,0:T(8,128)(2,1)S(1)}, bf16[128,1152]{1,0:T(8,128)(2,1)S(1)}, u32[]{:S(2)}, u32[]{:S(2)}) collective-permute-start(bf16[128,1152]{1,0:T(8,128)(2,1)S(1)} %collective-permute-done.4), channel_id=1, source_target_pairs={{0,16},{1,17},{2,18},{3,19},{4,20},{5,21},{6,22},{7,23},{8,120},{9... | collective-permute-start | bytes 884744 | tf_op jit(solution)/shard_map/ppermute | solution.py:52
  25.9 8.0 %collective-permute-start.10 = (bf16[128,1152]{1,0:T(8,128)(2,1)S(1)}, bf16[128,1152]{1,0:T(8,128)(2,1)S(1)}, u32[]{:S(2)}, u32[]{:S(2)}) collective-permute-start(bf16[128,1152]{1,0:T(8,128)(2,1)S(1)} %slice.101), channel_id=1, source_target_pairs={{0,3},{1,2},{2,1},{3,0},{4,7},{5,6},{6,5},{7,4},{8,9},{9,8},{10,11... | collective-permute-start | bytes 884744 | tf_op jit(solution)/shard_map/ppermute | solution.py:52
  28.7 6.8 %collective-permute-start.9 = (bf16[128,1152]{1,0:T(8,128)(2,1)S(1)}, bf16[128,1152]{1,0:T(8,128)(2,1)S(1)}, u32[]{:S(2)}, u32[]{:S(2)}) collective-permute-start(bf16[128,1152]{1,0:T(8,128)(2,1)S(1)} %slice.100), channel_id=1, source_target_pairs={{0,132},{1,133},{2,134},{3,135},{4,128},{5,129},{6,130},{7,131},{8... | collective-permute-start | bytes 884744 | tf_op jit(solution)/shard_map/ppermute | solution.py:52
  30.4 5.7 %collective-permute-start.11 = (bf16[128,1152]{1,0:T(8,128)(2,1)S(1)}, bf16[128,1152]{1,0:T(8,128)(2,1)S(1)}, u32[]{:S(2)}, u32[]{:S(2)}) collective-permute-start(bf16[128,1152]{1,0:T(8,128)(2,1)S(1)} %collective-permute-done.6.refs_0_.refs_6_), channel_id=1, source_target_pairs={{0,8},{1,9},{2,10},{3,11},{4,12},{5,13},{6,14},{7,15},{8,0},{9,1},... | collective-permute-start | bytes 884744 | tf_op jit(solution)/shard_map/ppermute | solution.py:52
  30.4 7.9 %collective-permute-start.12 = (bf16[128,1152]{1,0:T(8,128)(2,1)S(1)}, bf16[128,1152]{1,0:T(8,128)(2,1)S(1)}, u32[]{:S(2)}, u32[]{:S(2)}) collective-permute-start(bf16[128,1152]{1,0:T(8,128)(2,1)S(1)} %collective-permute-done.6.refs_0_.refs_6_), channel_id=1, source_target_pairs={{0,112},{1,113},{2,114},{3,115},{4,116},{5,117},{6,118},{7,119},{8... | collective-permute-start | bytes 884744 | tf_op jit(solution)/shard_map/ppermute | solution.py:52
  38.0 15.2 %collective-permute-start.16 = (bf16[128,1152]{1,0:T(8,128)(2,1)S(1)}, bf16[128,1152]{1,0:T(8,128)(2,1)S(1)}, u32[]{:S(2)}, u32[]{:S(2)}) collective-permute-start(bf16[128,1152]{1,0:T(8,128)(2,1)S(1)} %get-tuple-element.33), channel_id=1, source_target_pairs={{0,8},{1,9},{2,10},{3,11},{4,12},{5,13},{6,14},{7,15},{8,0},{9,1},... | collective-permute-start | bytes 884744 | tf_op jit(solution)/shard_map/ppermute | solution.py:52
  43.2 8.8 %collective-permute-start.17 = (bf16[128,1152]{1,0:T(8,128)(2,1)S(1)}, bf16[128,1152]{1,0:T(8,128)(2,1)S(1)}, u32[]{:S(2)}, u32[]{:S(2)}) collective-permute-start(bf16[128,1152]{1,0:T(8,128)(2,1)S(1)} %add_convert_fusion.1), channel_id=1, source_target_pairs={{0,112},{1,113},{2,114},{3,115},{4,116},{5,117},{6,118},{7,119},{8... | collective-permute-start | bytes 884744 | tf_op jit(solution)/shard_map/ppermute | solution.py:52
  44.1 18.8 %collective-permute-start.19 = (bf16[256,1152]{1,0:T(8,128)(2,1)S(1)}, bf16[256,1152]{1,0:T(8,128)(2,1)S(1)}, u32[]{:S(2)}, u32[]{:S(2)}) collective-permute-start(bf16[256,1152]{1,0:T(8,128)(2,1)S(1)} %shard_map.77), channel_id=1, source_target_pairs={{0,135},{1,134},{2,133},{3,132},{4,131},{5,130},{6,129},{7,128},{8... | collective-permute-start | bytes 1769480 | tf_op jit(solution)/shard_map/ppermute | solution.py:52
  49.5 5.6 %collective-permute-start.15 = (bf16[256,1152]{1,0:T(8,128)(2,1)S(1)}, bf16[256,1152]{1,0:T(8,128)(2,1)S(1)}, u32[]{:S(2)}, u32[]{:S(2)}) collective-permute-start(bf16[256,1152]{1,0:T(8,128)(2,1)S(1)} %get-tuple-element.40), channel_id=1, source_target_pairs={{0,8},{1,9},{2,10},{3,11},{4,12},{5,13},{6,14},{7,15},{8,0},{9,1},... | collective-permute-start | bytes 1769480 | tf_op jit(solution)/shard_map/ppermute | solution.py:52
  50.5 12.4 %collective-permute-start.20 = (bf16[256,1152]{1,0:T(8,128)(2,1)S(1)}, bf16[256,1152]{1,0:T(8,128)(2,1)S(1)}, u32[]{:S(2)}, u32[]{:S(2)}) collective-permute-start(bf16[256,1152]{1,0:T(8,128)(2,1)S(1)} %shard_map.80), channel_id=1, source_target_pairs={{0,3},{1,2},{2,1},{3,0},{4,7},{5,6},{6,5},{7,4},{8,9},{9,8},{10,11... | collective-permute-start | bytes 1769480 | tf_op jit(solution)/shard_map/ppermute | solution.py:52
  51.9 10.9 %collective-permute-start.21 = (bf16[256,1152]{1,0:T(8,128)(2,1)S(1)}, bf16[256,1152]{1,0:T(8,128)(2,1)S(1)}, u32[]{:S(2)}, u32[]{:S(2)}) collective-permute-start(bf16[256,1152]{1,0:T(8,128)(2,1)S(1)} %shard_map.81), channel_id=1, source_target_pairs={{0,132},{1,133},{2,134},{3,135},{4,128},{5,129},{6,130},{7,131},{8... | collective-permute-start | bytes 1769480 | tf_op jit(solution)/shard_map/ppermute | solution.py:52
  53.2 6.8 %collective-permute-start.18 = (bf16[128,1152]{1,0:T(8,128)(2,1)S(1)}, bf16[128,1152]{1,0:T(8,128)(2,1)S(1)}, u32[]{:S(2)}, u32[]{:S(2)}) collective-permute-start(bf16[128,1152]{1,0:T(8,128)(2,1)S(1)} %add_convert_fusion), channel_id=1, source_target_pairs={{0,16},{1,17},{2,18},{3,19},{4,20},{5,21},{6,22},{7,23},{8,120},{9... | collective-permute-start | bytes 884744 | tf_op jit(solution)/shard_map/ppermute | solution.py:52
  60.1 8.9 %collective-permute-start.25 = (bf16[128,1152]{1,0:T(8,128)(2,1)S(1)}, bf16[128,1152]{1,0:T(8,128)(2,1)S(1)}, u32[]{:S(2)}, u32[]{:S(2)}) collective-permute-start(bf16[128,1152]{1,0:T(8,128)(2,1)S(1)} %slice_add_fusion.1), channel_id=1, source_target_pairs={{0,112},{1,113},{2,114},{3,115},{4,116},{5,117},{6,118},{7,119},{8... | collective-permute-start | bytes 884744 | tf_op jit(solution)/shard_map/ppermute | solution.py:52
  63.2 6.1 %collective-permute-start.22 = (bf16[64,1152]{1,0:T(8,128)(2,1)S(1)}, bf16[64,1152]{1,0:T(8,128)(2,1)S(1)}, u32[]{:S(2)}, u32[]{:S(2)}) collective-permute-start(bf16[64,1152]{1,0:T(8,128)(2,1)S(1)} %get-tuple-element.50), channel_id=1, source_target_pairs={{0,5},{1,4},{2,7},{3,6},{4,1},{5,0},{6,3},{7,2},{8,143},{9,142},{1... | collective-permute-start | bytes 442376 | tf_op jit(solution)/shard_map/ppermute | solution.py:52
  66.0 7.7 %collective-permute-start.23 = (bf16[64,1152]{1,0:T(8,128)(2,1)S(1)}, bf16[64,1152]{1,0:T(8,128)(2,1)S(1)}, u32[]{:S(2)}, u32[]{:S(2)}) collective-permute-start(bf16[64,1152]{1,0:T(8,128)(2,1)S(1)} %get-tuple-element.49), channel_id=1, source_target_pairs={{0,1},{1,0},{2,3},{3,2},{4,5},{5,4},{6,7},{7,6},{8,11},{9,10},{10,... | collective-permute-start | bytes 442376 | tf_op jit(solution)/shard_map/ppermute | solution.py:52
  69.1 6.1 %collective-permute-start.26 = (bf16[64,1152]{1,0:T(8,128)(2,1)S(1)}, bf16[64,1152]{1,0:T(8,128)(2,1)S(1)}, u32[]{:S(2)}, u32[]{:S(2)}) collective-permute-start(bf16[64,1152]{1,0:T(8,128)(2,1)S(1)} %slice.123), channel_id=1, source_target_pairs={{0,16},{1,17},{2,18},{3,19},{4,20},{5,21},{6,22},{7,23},{8,120},{9... | collective-permute-start | bytes 442376 | tf_op jit(solution)/shard_map/ppermute | solution.py:52
  (7 other events, 20.7 us)

commit v5 on v4

--- a/solution.py
+++ b/solution.py
@@ -41,12 +41,12 @@
     return sorted(pairs)
 
 
-def exchange(axis, first=True):
-    hops = [dict(pairs_of(one, first)) for one in ((axis,) if axis == "core" else axis)]
+def permute(*hops):
+    maps = [dict(pairs_of(axis, first)) for axis, first in hops]
     pairs = []
-    for source in sorted(hops[0]):
+    for source in sorted(maps[0]):
         target = source
-        for hop in hops:
+        for hop in maps:
             target = hop[target]
         pairs.append((source, target))
     return lambda value: lax.ppermute(value, AXES, pairs)
@@ -145,10 +145,12 @@
     )
 
 
-def near_kernel(count, *refs):
-    *inputs, sums_own, send = refs
-    weights = columns_of(*[ref[...] for ref in inputs[:count]])
-    total = for_texts(weights, rows_of(*inputs[count:]))
+def part_kernel(w_aq, w_axy, quad, part_x, part_y, sums):
+    sums[...] = for_texts(columns_of(w_aq[...], w_axy[...]), rows_of(quad, part_x, part_y))
+
+
+def near_kernel(part, w_ad, top_d, low_d, sums_own, send):
+    total = part[...] + for_texts(w_ad[...], rows_of(top_d, low_d))
     own = sums_own.shape[0]
     sums_own[...] = total[:own]
     send[...] = rounded(total[own:])
@@ -191,10 +193,11 @@
 
 
 def local(images, texts, logit_scale, logit_bias):
-    x1, y1, d1 = exchange("x", True), exchange("y", True), exchange("xy", True)
-    x2, y2, d2 = exchange("x", False), exchange("y", False), exchange("xy", False)
-    z1, z2 = exchange("z", True), exchange("z", False)
-    sibling = exchange("core")
+    x1, y1, d1 = permute(("x", True)), permute(("y", True)), permute(("x", True), ("y", True))
+    x2, y2, d2 = permute(("x", False)), permute(("y", False)), permute(("x", False), ("y", False))
+    z1, z2 = permute(("z", True)), permute(("z", False))
+    z_out, z_home = permute(("z", True), ("z", False)), permute(("z", False), ("z", True))
+    sibling = permute(("core", True))
     f32, bf16 = jnp.float32, jnp.bfloat16
     n, d = images.shape
     a, b, q = 4 * n, 2 * n, 4 * n
@@ -215,44 +218,35 @@
             coefficients, *some_texts, *some_images, products=share * m * k,
         )[0]
 
-    raw = (d1(images), x1(images), y1(images), z1(texts), units_of(texts), units_of(images), coefficients)
-    raw_d, raw_x, raw_y, raw_t, own_text, own_image, coefficients = lax.optimization_barrier(raw)
+    raw = (z1(texts), y1(images), x1(images), d1(images), units_of(texts), units_of(images), coefficients)
+    raw_t, raw_y, raw_x, raw_d, own_text, own_image, coefficients = lax.optimization_barrier(raw)
     pair = block_of(own_text, raw_t)
     quad = block_of(own_image, raw_x, raw_y, raw_d)
     r2 = z2(pair)
     part_x, part_y = x2(quad), y2(quad)
-    r3 = z1(r2)
+    r3, r4 = z1(r2), z_out(r2)
     top_d, low_d = y2(part_x[: q // 2]), x2(part_y[q // 2 :])
-    r4 = z2(r3)
     own_a = join(pair, r2)
     sib_a = sibling(own_a)
     w_aq = weigh((own_a, sib_a), (quad,), share=0)
     w_axy = weigh((own_a, sib_a), (part_x, part_y), share=0)
-    w_ad = weigh((after(own_a, w_aq, w_axy), sib_a), (top_d, low_d), share=40)
-    sib_b = sibling(r3)
+    w_ad = weigh((after(own_a, w_aq, w_axy), sib_a), (top_d, low_d))
     all_images = (quad, part_x, part_y, top_d, low_d)
 
-    def near(rows, *blocks, products=0):
-        return on_device(
-            functools.partial(near_kernel, len(blocks)), [((rows, d), f32), ((rows, d), bf16)],
-            *blocks, *all_images, products=products,
-        )
-
-    w_b = weigh((after(r3, w_ad), sib_b), all_images)
-    sums_own_b, send_b = near(b, w_b, products=2 * b * 4 * q)
-    r4 = after(r4, send_b)
-    back_b = sibling(send_b)
-    sib_c = sibling(r4)
-    w_own = weigh((r4,), all_images)
+    (near_part,) = on_device(part_kernel, [((2 * a, d), f32)], w_aq, w_axy, quad, part_x, part_y)
+    r3, r4, w_aq, w_axy, near_part = lax.optimization_barrier((r3, r4, w_aq, w_axy, near_part))
+    own_c = join(r3, r4)
+    sib_c = sibling(own_c)
+    w_own = weigh((own_c,), all_images)
     w_sib, send_c = on_device(
-        sibling_kernel, [((b, 4 * q), bf16), ((b, d), bf16)], coefficients, sib_c, *all_images,
-        products=2 * b * 4 * q,
+        sibling_kernel, [((a, 4 * q), bf16), ((a, d), bf16)], coefficients, sib_c, *all_images,
+        products=2 * a * 4 * q,
     )
     (sums_own_c,) = on_device(
-        text_kernel, [((b, d), f32)], w_own, *all_images, products=b * 4 * q
+        text_kernel, [((a, d), f32)], w_own, *all_images, products=a * 4 * q
     )
     back_c = sibling(send_c)
-    all_texts = (own_a, sib_a, r3, sib_b, r4, sib_c)
+    all_texts = (own_a, sib_a, own_c, sib_c)
 
     def image_part(kind, *blocks, share=1):
         return on_device(
@@ -262,7 +256,7 @@
 
     def late(index, *others):
         span = slice(index * q, (index + 1) * q)
-        return after(w_b[:, span], *others), w_own[:, span], w_sib[:, span]
+        return after(w_own[:, span], *others), w_sib[:, span]
 
     send_d = image_part(bf16, w_ad, *late(3))
     back_d = d2(send_d)
@@ -270,12 +264,14 @@
     send_x = image_part(bf16, w_axy[:, :q], *late(1, s4))
     send_y = image_part(bf16, w_axy[:, q:], *late(2, s4))
     back_x, back_y = x2(send_x), y2(send_y)
-    sums_own, send_a = near(a, after(w_aq, s4), w_axy, w_ad, products=2 * a * 4 * q)
+    sums_own, send_a = on_device(
+        near_kernel, [((a, d), f32), ((a, d), bf16)], near_part, after(w_ad, s4), top_d, low_d,
+        products=2 * a * 4 * q,
+    )
     back_a = sibling(send_a)
-    s4 = after(z2(s4), send_a)
-    s3 = sums_own_b + widened(back_b) + widened(s4)
+    back_3, back_4 = z1(s4[:b]), z_home(s4[b:])
     near_sums = sums_own + widened(back_a)
-    s2 = near_sums[2 * n :] + widened(z1(rounded(s3)))
+    s2 = near_sums[2 * n :] + widened(back_3) + widened(back_4)
     quad_sums = image_part(f32, w_aq, *late(0, s2))
     s01 = near_sums[: 2 * n] + widened(z2(rounded(s2)))
     quad_sums = quad_sums + widened(back_d) + widened(back_x) + widened(back_y)

time: 77 us -> 75.8 us (0.984)
  the two profiles are of different devices: /device:TPU:8 before, /device:TPU:1 now
where the time goes in v5:
time: 75.8 us; the launch traced here: 75.7 us
  starting transfers between devices  30.4 us (40%)
  waiting for transfers between devices  26.8 us (35%)
  Pallas kernels  13.3 us (18%)
  between operations  2.28 us (3%)
  local copies, waits for them, and re-layouts  2.25 us (3%)
    ppermute x25, starting transfers between devices, permute(): return lambda value: lax.ppermute(value, AXES, pairs)  30.4 us
    ppermute x25, waiting for transfers between devices, permute(): return lambda value: lax.ppermute(value, AXES, pairs)  26.8 us
    pallas_call x16, Pallas kernels, on_device(): pl.pallas_call(kernel, out_shape=[jax.ShapeDtypeStruct(shape, kind) for s...  11.3 us
    pallas_call x2, Pallas kernels, grad_rows(): pl.pallas_call(grad_kernel, out_shape=jax.ShapeDtypeStruct(rows.shape, jn...  2.03 us
    unnamed x9, local copies, waits for them, and re-layouts  1.85 us
  transfers between devices with their start and end apart: 25, of which 10 were waited for; matrix products, arithmetic and copies ran while one was open for 1% of the time, Pallas kernels for 14%

profile of v5, /device:TPU:1, one launch (start us, length us, event | category | flops | bytes accessed | tf_op | source)
XLA Modules:
  0.0 75.7 jit_solution(12589767703385838113)
XLA Ops:
  0.6 6.5 %collective-permute-start = (bf16[64,1152]{1,0:T(8,128)(2,1)}, bf16[64,1152]{1,0:T(8,128)(2,1)S(1)}, u32[]{:S(2)}, u32[]{:S(2)}) collective-permute-start(bf16[64,1152]{1,0:T(8,128)(2,1)} %rows.7), channel_id=1, source_target_pairs={{0,16},{1,17},{2,18},{3,19},{4,20},{5,21},{6,22},{7,23},{8,120},{9... | collective-permute-start | bytes 442376 | tf_op jit(solution)/shard_map/ppermute | solution.py:52
  7.1 4.9 %collective-permute-start.3 = (bf16[64,1152]{1,0:T(8,128)(2,1)}, bf16[64,1152]{1,0:T(8,128)(2,1)S(1)}, u32[]{:S(2)}, u32[]{:S(2)}) collective-permute-start(bf16[64,1152]{1,0:T(8,128)(2,1)} %others.3), channel_id=1, source_target_pairs={{0,5},{1,4},{2,7},{3,6},{4,1},{5,0},{6,3},{7,2},{8,143},{9,142},{1... | collective-permute-start | bytes 442376 | tf_op jit(solution)/shard_map/ppermute | solution.py:52
  12.3 0.9 %copy-done.2 = bf16[64,1152]{1,0:T(8,128)(2,1)S(1)} copy-done((bf16[64,1152]{1,0:T(8,128)(2,1)S(1)}, bf16[64,1152]{1,0:T(8,128)(2,1)}, u32[]{:S(2)}) %copy-start.2) | copy-done | bytes 147480
  13.4 0.9 %copy-done = bf16[64,1152]{1,0:T(8,128)(2,1)S(1)} copy-done((bf16[64,1152]{1,0:T(8,128)(2,1)S(1)}, bf16[64,1152]{1,0:T(8,128)(2,1)}, u32[]{:S(2)}) %copy-start) | copy-done | bytes 147480
  15.7 1.7 %collective-permute-done.2.refs_0_ = bf16[64,1152]{1,0:T(8,128)(2,1)S(1)} collective-permute-done((bf16[64,1152]{1,0:T(8,128)(2,1)}, bf16[64,1152]{1,0:T(8,128)(2,1)S(1)}, u32[]{:S(2)}, u32[]{:S(2)}) %collective-permute-start.2) | collective-permute-done | bytes 147488 | tf_op jit(solution)/shard_map/ppermute | solution.py:52
  18.3 5.5 %collective-permute-done.4 = bf16[128,1152]{1,0:T(8,128)(2,1)S(1)} collective-permute-done((bf16[128,1152]{1,0:T(8,128)(2,1)S(1)}, bf16[128,1152]{1,0:T(8,128)(2,1)S(1)}, u32[]{:S(2)}, u32[]{:S(2)}) %collective-permute-start.4) | collective-permute-done | bytes 294944 | tf_op jit(solution)/shard_map/ppermute | solution.py:52
  24.0 1.2 %collective-permute-start.6 = (bf16[128,1152]{1,0:T(8,128)(2,1)S(1)}, bf16[128,1152]{1,0:T(8,128)(2,1)S(1)}, u32[]{:S(2)}, u32[]{:S(2)}) collective-permute-start(bf16[128,1152]{1,0:T(8,128)(2,1)S(1)} %collective-permute-done.4), channel_id=1, source_target_pairs={{0,32},{1,33},{2,34},{3,35},{4,36},{5,37},{6,38},{7,39},{8,104},{9... | collective-permute-start | bytes 884744 | tf_op jit(solution)/shard_map/ppermute | solution.py:52
  25.2 1.2 %collective-permute-start.5 = (bf16[128,1152]{1,0:T(8,128)(2,1)S(1)}, bf16[128,1152]{1,0:T(8,128)(2,1)S(1)}, u32[]{:S(2)}, u32[]{:S(2)}) collective-permute-start(bf16[128,1152]{1,0:T(8,128)(2,1)S(1)} %collective-permute-done.4), channel_id=1, source_target_pairs={{0,16},{1,17},{2,18},{3,19},{4,20},{5,21},{6,22},{7,23},{8,120},{9... | collective-permute-start | bytes 884744 | tf_op jit(solution)/shard_map/ppermute | solution.py:52
  27.4 1.4 %collective-permute-start.10 = (bf16[128,1152]{1,0:T(8,128)(2,1)S(1)}, bf16[128,1152]{1,0:T(8,128)(2,1)S(1)}, u32[]{:S(2)}, u32[]{:S(2)}) collective-permute-start(bf16[128,1152]{1,0:T(8,128)(2,1)S(1)} %slice.92), channel_id=1, source_target_pairs={{0,132},{1,133},{2,134},{3,135},{4,128},{5,129},{6,130},{7,131},{8... | collective-permute-start | bytes 884744 | tf_op jit(solution)/shard_map/ppermute | solution.py:52
  29.4 1.0 %shard_map.70.w_axy = bf16[512,512]{1,0:T(8,128)(2,1)S(1)} custom-call(f32[8,128]{1,0:T(8,128)S(1)} %concatenate.12.coefficients, bf16[256,1152]{1,0:T(8,128)(2,1)S(1)} %pad_maximum_fusion.refs_0_.refs_3_, bf16[256,1152]{1,0:T(8,128)(2,1)S(1)} %collective-permute-done.7.refs_1_.refs_4_, bf16[256,1152]{1,0:T(8,128)(2,1)S(1)} %collective-permute-done.8.refs_2_.part_x.refs_1_, ...), custom_call_target="tpu_custom_call" | custom-call | tf_op jit(solution)/shard_map/pallas_call | solution.py:179
  30.4 1.2 %shard_map.71.part = f32[512,1152]{1,0:T(8,128)S(1)} custom-call(bf16[512,256]{1,0:T(8,128)(2,1)S(1)} %shard_map.69.w_aq.refs_0_, bf16[512,512]{1,0:T(8,128)(2,1)S(1)} %shard_map.70.w_axy, bf16[256,1152]{1,0:T(8,128)(2,1)S(1)} %shard_map.68.refs_2_.quad.refs_1_.refs_0_, bf16[256,1152]{1,0:T(8,128)(2,1)S(1)} %collective-permute-done.8.refs_2_.part_x.refs_1_, ...), custom_call_target="tpu_custom_call" | custom-call | tf_op jit(solution)/shard_map/pallas_call | solution.py:179
  32.5 4.7 %collective-permute-done.5 = bf16[128,1152]{1,0:T(8,128)(2,1)S(1)} collective-permute-done((bf16[128,1152]{1,0:T(8,128)(2,1)S(1)}, bf16[128,1152]{1,0:T(8,128)(2,1)S(1)}, u32[]{:S(2)}, u32[]{:S(2)}) %collective-permute-start.5) | collective-permute-done | bytes 294944 | tf_op jit(solution)/shard_map/ppermute | solution.py:52
  38.0 1.0 %shard_map.72.weights = bf16[256,1024]{1,0:T(8,128)(2,1)S(1)} custom-call(f32[8,128]{1,0:T(8,128)S(1)} %concatenate.12.coefficients, bf16[256,1152]{1,0:T(8,128)(2,1)S(1)} %constant_dynamic-update-slice_fusion.refs_0_.refs_5_, bf16[256,1152]{1,0:T(8,128)(2,1)S(1)} %shard_map.68.refs_2_.quad.refs_1_.refs_0_, ...), custom_call_target="tpu_custom_call" | custom-call | flops 603979776 | tf_op jit(solution)/shard_map/pallas_call | solution.py:179
  39.7 1.6 %shard_map.75 = (bf16[256,1024]{1,0:T(8,128)(2,1)S(1)}, bf16[256,1152]{1,0:T(8,128)(2,1)S(1)}) custom-call(f32[8,128]{1,0:T(8,128)S(1)} %concatenate.12.coefficients, bf16[256,1152]{1,0:T(8,128)(2,1)S(1)} %collective-permute-done.12.sib_c.refs_6_, bf16[256,1152]{1,0:T(8,128)(2,1)S(1)} %shard_map.68.refs_2_.quad.refs_1_.refs_0_, ...), custom_call_target="tpu_custom_call" | custom-call | flops 1207959552 | tf_op jit(solution)/shard_map/pallas_call | solution.py:179
  41.2 2.1 %collective-permute-start.13 = (bf16[256,1152]{1,0:T(8,128)(2,1)S(1)}, bf16[256,1152]{1,0:T(8,128)(2,1)S(1)}, u32[]{:S(2)}, u32[]{:S(2)}) collective-permute-start(bf16[256,1152]{1,0:T(8,128)(2,1)S(1)} %get-tuple-element.38), channel_id=1, source_target_pairs={{0,8},{1,9},{2,10},{3,11},{4,12},{5,13},{6,14},{7,15},{8,0},{9,1},... | collective-permute-start | bytes 1769480 | tf_op jit(solution)/shard_map/ppermute | solution.py:52
  46.4 2.6 %collective-permute-start.14 = (bf16[256,1152]{1,0:T(8,128)(2,1)S(1)}, bf16[256,1152]{1,0:T(8,128)(2,1)S(1)}, u32[]{:S(2)}, u32[]{:S(2)}) collective-permute-start(bf16[256,1152]{1,0:T(8,128)(2,1)S(1)} %get-tuple-element.41), channel_id=1, source_target_pairs={{0,8},{1,9},{2,10},{3,11},{4,12},{5,13},{6,14},{7,15},{8,0},{9,1},... | collective-permute-start | bytes 1769480 | tf_op jit(solution)/shard_map/ppermute | solution.py:52
  49.0 1.6 %collective-permute-start.15 = (bf16[128,1152]{1,0:T(8,128)(2,1)S(1)}, bf16[128,1152]{1,0:T(8,128)(2,1)S(1)}, u32[]{:S(2)}, u32[]{:S(2)}) collective-permute-start(bf16[128,1152]{1,0:T(8,128)(2,1)S(1)} %get-tuple-element.51), channel_id=1, source_target_pairs={{0,16},{1,17},{2,18},{3,19},{4,20},{5,21},{6,22},{7,23},{8,120},{9... | collective-permute-start | bytes 884744 | tf_op jit(solution)/shard_map/ppermute | solution.py:52
  52.7 5.6 %collective-permute-done.15 = bf16[128,1152]{1,0:T(8,128)(2,1)S(1)} collective-permute-done((bf16[128,1152]{1,0:T(8,128)(2,1)S(1)}, bf16[128,1152]{1,0:T(8,128)(2,1)S(1)}, u32[]{:S(2)}, u32[]{:S(2)}) %collective-permute-start.15) | collective-permute-done | bytes 294944 | tf_op jit(solution)/shard_map/ppermute | solution.py:52
  58.3 4.4 %collective-permute-done.16 = bf16[128,1152]{1,0:T(8,128)(2,1)S(1)} collective-permute-done((bf16[128,1152]{1,0:T(8,128)(2,1)S(1)}, bf16[128,1152]{1,0:T(8,128)(2,1)S(1)}, u32[]{:S(2)}, u32[]{:S(2)}) %collective-permute-start.16) | collective-permute-done | bytes 294944 | tf_op jit(solution)/shard_map/ppermute | solution.py:52
  65.1 4.2 %collective-permute-start.20 = (bf16[64,1152]{1,0:T(8,128)(2,1)S(1)}, bf16[64,1152]{1,0:T(8,128)(2,1)S(1)}, u32[]{:S(2)}, u32[]{:S(2)}) collective-permute-start(bf16[64,1152]{1,0:T(8,128)(2,1)S(1)} %get-tuple-element.50), channel_id=1, source_target_pairs={{0,5},{1,4},{2,7},{3,6},{4,1},{5,0},{6,3},{7,2},{8,143},{9,142},{1... | collective-permute-start | bytes 442376 | tf_op jit(solution)/shard_map/ppermute | solution.py:52
  69.4 1.2 %collective-permute-start.24 = (bf16[64,1152]{1,0:T(8,128)(2,1)S(1)}, bf16[64,1152]{1,0:T(8,128)(2,1)S(1)}, u32[]{:S(2)}, u32[]{:S(2)}) collective-permute-start(bf16[64,1152]{1,0:T(8,128)(2,1)S(1)} %slice.113), channel_id=1, source_target_pairs={{0,16},{1,17},{2,18},{3,19},{4,20},{5,21},{6,22},{7,23},{8,120},{9... | collective-permute-start | bytes 442376 | tf_op jit(solution)/shard_map/ppermute | solution.py:52
  70.7 2.7 %collective-permute-done.20.rest_0_ = bf16[64,1152]{1,0:T(8,128)(2,1)S(1)} collective-permute-done((bf16[64,1152]{1,0:T(8,128)(2,1)S(1)}, bf16[64,1152]{1,0:T(8,128)(2,1)S(1)}, u32[]{:S(2)}, u32[]{:S(2)}) %collective-permute-start.20) | collective-permute-done | bytes 147488 | tf_op jit(solution)/shard_map/ppermute | solution.py:52
  73.4 1.0 %shard_map.81 = f32[64,1152]{1,0:T(8,128)} custom-call(f32[8,128]{1,0:T(8,128)S(1)} %concatenate.12.coefficients, bf16[64,1152]{1,0:T(8,128)(2,1)S(1)} %copy-done.1, bf16[64,1152]{1,0:T(8,128)(2,1)S(1)} %copy-done.3, f32[64,1152]{1,0:T(8,128)S(1)} %slice.101.sums, bf16[64,1152]{1,0:T(8,128)(2,1)S(1)} %collective-permute-done.20.rest_0_, ...), custom_call_target="tpu_custom_call" | custom-call | tf_op jit(solution)/shard_map/pallas_call | solution.py:102
  74.7 1.0 %shard_map.82 = f32[64,1152]{1,0:T(8,128)} custom-call(f32[8,128]{1,0:T(8,128)S(1)} %concatenate.12.coefficients, bf16[64,1152]{1,0:T(8,128)(2,1)S(1)} %copy-done.3, bf16[64,1152]{1,0:T(8,128)(2,1)S(1)} %copy-done.1, f32[64,1152]{1,0:T(8,128)S(1)} %slice.106.sums, bf16[64,1152]{1,0:T(8,128)(2,1)S(1)} %collective-permute-done.24.rest_0_), custom_call_target="tpu_custom_call" | custom-call | tf_op jit(solution)/shard_map/pallas_call | solution.py:102
  (73 shorter events, 13.2 us)
Async XLA Ops:
  0.6 15.1 %collective-permute-start = (bf16[64,1152]{1,0:T(8,128)(2,1)}, bf16[64,1152]{1,0:T(8,128)(2,1)S(1)}, u32[]{:S(2)}, u32[]{:S(2)}) collective-permute-start(bf16[64,1152]{1,0:T(8,128)(2,1)} %rows.7), channel_id=1, source_target_pairs={{0,16},{1,17},{2,18},{3,19},{4,20},{5,21},{6,22},{7,23},{8,120},{9... | collective-permute-start | bytes 442376 | tf_op jit(solution)/shard_map/ppermute | solution.py:52
  7.1 8.6 %collective-permute-start.3 = (bf16[64,1152]{1,0:T(8,128)(2,1)}, bf16[64,1152]{1,0:T(8,128)(2,1)S(1)}, u32[]{:S(2)}, u32[]{:S(2)}) collective-permute-start(bf16[64,1152]{1,0:T(8,128)(2,1)} %others.3), channel_id=1, source_target_pairs={{0,5},{1,4},{2,7},{3,6},{4,1},{5,0},{6,3},{7,2},{8,143},{9,142},{1... | collective-permute-start | bytes 442376 | tf_op jit(solution)/shard_map/ppermute | solution.py:52
  12.1 5.4 %collective-permute-start.2 = (bf16[64,1152]{1,0:T(8,128)(2,1)}, bf16[64,1152]{1,0:T(8,128)(2,1)S(1)}, u32[]{:S(2)}, u32[]{:S(2)}) collective-permute-start(bf16[64,1152]{1,0:T(8,128)(2,1)} %others.3), channel_id=1, source_target_pairs={{0,1},{1,0},{2,3},{3,2},{4,5},{5,4},{6,7},{7,6},{8,11},{9,10},{10,... | collective-permute-start | bytes 442376 | tf_op jit(solution)/shard_map/ppermute | solution.py:52
  12.2 5.4 %collective-permute-start.1 = (bf16[64,1152]{1,0:T(8,128)(2,1)}, bf16[64,1152]{1,0:T(8,128)(2,1)S(1)}, u32[]{:S(2)}, u32[]{:S(2)}) collective-permute-start(bf16[64,1152]{1,0:T(8,128)(2,1)} %others.3), channel_id=1, source_target_pairs={{0,4},{1,5},{2,6},{3,7},{4,0},{5,1},{6,2},{7,3},{8,140},{9,141},{1... | collective-permute-start | bytes 442376 | tf_op jit(solution)/shard_map/ppermute | solution.py:52
  17.9 6.0 %collective-permute-start.4 = (bf16[128,1152]{1,0:T(8,128)(2,1)S(1)}, bf16[128,1152]{1,0:T(8,128)(2,1)S(1)}, u32[]{:S(2)}, u32[]{:S(2)}) collective-permute-start(bf16[128,1152]{1,0:T(8,128)(2,1)S(1)} %shard_map.67), channel_id=1, source_target_pairs={{0,112},{1,113},{2,114},{3,115},{4,116},{5,117},{6,118},{7,119},{8... | collective-permute-start | bytes 884744 | tf_op jit(solution)/shard_map/ppermute | solution.py:52
  18.1 9.1 %collective-permute-start.9 = (bf16[256,1152]{1,0:T(8,128)(2,1)S(1)}, bf16[256,1152]{1,0:T(8,128)(2,1)S(1)}, u32[]{:S(2)}, u32[]{:S(2)}) collective-permute-start(bf16[256,1152]{1,0:T(8,128)(2,1)S(1)} %shard_map.68.refs_2_.quad.refs_1_.refs_0_), channel_id=1, source_target_pairs={{0,132},{1,133},{2,134},{3,135},{4,128},{5,129},{6,130},{7,131},{8... | collective-permute-start | bytes 1769480 | tf_op jit(solution)/shard_map/ppermute | solution.py:52
  18.2 9.1 %collective-permute-start.8 = (bf16[256,1152]{1,0:T(8,128)(2,1)S(1)}, bf16[256,1152]{1,0:T(8,128)(2,1)S(1)}, u32[]{:S(2)}, u32[]{:S(2)}) collective-permute-start(bf16[256,1152]{1,0:T(8,128)(2,1)S(1)} %shard_map.68.refs_2_.quad.refs_1_.refs_0_), channel_id=1, source_target_pairs={{0,3},{1,2},{2,1},{3,0},{4,7},{5,6},{6,5},{7,4},{8,9},{9,8},{10,11... | collective-permute-start | bytes 1769480 | tf_op jit(solution)/shard_map/ppermute | solution.py:52
  23.9 5.0 %collective-permute-start.7 = (bf16[256,1152]{1,0:T(8,128)(2,1)S(1)}, bf16[256,1152]{1,0:T(8,128)(2,1)S(1)}, u32[]{:S(2)}, u32[]{:S(2)}) collective-permute-start(bf16[256,1152]{1,0:T(8,128)(2,1)S(1)} %pad_maximum_fusion.refs_0_.refs_3_), channel_id=1, source_target_pairs={{0,8},{1,9},{2,10},{3,11},{4,12},{5,13},{6,14},{7,15},{8,0},{9,1},... | collective-permute-start | bytes 1769480 | tf_op jit(solution)/shard_map/ppermute | solution.py:52
  24.0 8.5 %collective-permute-start.6 = (bf16[128,1152]{1,0:T(8,128)(2,1)S(1)}, bf16[128,1152]{1,0:T(8,128)(2,1)S(1)}, u32[]{:S(2)}, u32[]{:S(2)}) collective-permute-start(bf16[128,1152]{1,0:T(8,128)(2,1)S(1)} %collective-permute-done.4), channel_id=1, source_target_pairs={{0,32},{1,33},{2,34},{3,35},{4,36},{5,37},{6,38},{7,39},{8,104},{9... | collective-permute-start | bytes 884744 | tf_op jit(solution)/shard_map/ppermute | solution.py:52
  25.2 11.9 %collective-permute-start.5 = (bf16[128,1152]{1,0:T(8,128)(2,1)S(1)}, bf16[128,1152]{1,0:T(8,128)(2,1)S(1)}, u32[]{:S(2)}, u32[]{:S(2)}) collective-permute-start(bf16[128,1152]{1,0:T(8,128)(2,1)S(1)} %collective-permute-done.4), channel_id=1, source_target_pairs={{0,16},{1,17},{2,18},{3,19},{4,20},{5,21},{6,22},{7,23},{8,120},{9... | collective-permute-start | bytes 884744 | tf_op jit(solution)/shard_map/ppermute | solution.py:52
  27.3 10.8 %collective-permute-start.11 = (bf16[128,1152]{1,0:T(8,128)(2,1)S(1)}, bf16[128,1152]{1,0:T(8,128)(2,1)S(1)}, u32[]{:S(2)}, u32[]{:S(2)}) collective-permute-start(bf16[128,1152]{1,0:T(8,128)(2,1)S(1)} %slice.93), channel_id=1, source_target_pairs={{0,3},{1,2},{2,1},{3,0},{4,7},{5,6},{6,5},{7,4},{8,9},{9,8},{10,11... | collective-permute-start | bytes 884744 | tf_op jit(solution)/shard_map/ppermute | solution.py:52
  27.4 10.6 %collective-permute-start.10 = (bf16[128,1152]{1,0:T(8,128)(2,1)S(1)}, bf16[128,1152]{1,0:T(8,128)(2,1)S(1)}, u32[]{:S(2)}, u32[]{:S(2)}) collective-permute-start(bf16[128,1152]{1,0:T(8,128)(2,1)S(1)} %slice.92), channel_id=1, source_target_pairs={{0,132},{1,133},{2,134},{3,135},{4,128},{5,129},{6,130},{7,131},{8... | collective-permute-start | bytes 884744 | tf_op jit(solution)/shard_map/ppermute | solution.py:52
  41.2 4.5 %collective-permute-start.13 = (bf16[256,1152]{1,0:T(8,128)(2,1)S(1)}, bf16[256,1152]{1,0:T(8,128)(2,1)S(1)}, u32[]{:S(2)}, u32[]{:S(2)}) collective-permute-start(bf16[256,1152]{1,0:T(8,128)(2,1)S(1)} %get-tuple-element.38), channel_id=1, source_target_pairs={{0,8},{1,9},{2,10},{3,11},{4,12},{5,13},{6,14},{7,15},{8,0},{9,1},... | collective-permute-start | bytes 1769480 | tf_op jit(solution)/shard_map/ppermute | solution.py:52
  45.1 18.7 %collective-permute-start.17 = (bf16[256,1152]{1,0:T(8,128)(2,1)S(1)}, bf16[256,1152]{1,0:T(8,128)(2,1)S(1)}, u32[]{:S(2)}, u32[]{:S(2)}) collective-permute-start(bf16[256,1152]{1,0:T(8,128)(2,1)S(1)} %shard_map.76), channel_id=1, source_target_pairs={{0,135},{1,134},{2,133},{3,132},{4,131},{5,130},{6,129},{7,128},{8... | collective-permute-start | bytes 1769480 | tf_op jit(solution)/shard_map/ppermute | solution.py:52
  46.4 6.2 %collective-permute-start.14 = (bf16[256,1152]{1,0:T(8,128)(2,1)S(1)}, bf16[256,1152]{1,0:T(8,128)(2,1)S(1)}, u32[]{:S(2)}, u32[]{:S(2)}) collective-permute-start(bf16[256,1152]{1,0:T(8,128)(2,1)S(1)} %get-tuple-element.41), channel_id=1, source_target_pairs={{0,8},{1,9},{2,10},{3,11},{4,12},{5,13},{6,14},{7,15},{8,0},{9,1},... | collective-permute-start | bytes 1769480 | tf_op jit(solution)/shard_map/ppermute | solution.py:52
  49.0 9.3 %collective-permute-start.15 = (bf16[128,1152]{1,0:T(8,128)(2,1)S(1)}, bf16[128,1152]{1,0:T(8,128)(2,1)S(1)}, u32[]{:S(2)}, u32[]{:S(2)}) collective-permute-start(bf16[128,1152]{1,0:T(8,128)(2,1)S(1)} %get-tuple-element.51), channel_id=1, source_target_pairs={{0,16},{1,17},{2,18},{3,19},{4,20},{5,21},{6,22},{7,23},{8,120},{9... | collective-permute-start | bytes 884744 | tf_op jit(solution)/shard_map/ppermute | solution.py:52
  50.6 12.1 %collective-permute-start.16 = (bf16[128,1152]{1,0:T(8,128)(2,1)S(1)}, bf16[128,1152]{1,0:T(8,128)(2,1)S(1)}, u32[]{:S(2)}, u32[]{:S(2)}) collective-permute-start(bf16[128,1152]{1,0:T(8,128)(2,1)S(1)} %get-tuple-element.52), channel_id=1, source_target_pairs={{0,96},{1,97},{2,98},{3,99},{4,100},{5,101},{6,102},{7,103},{8,40}... | collective-permute-start | bytes 884744 | tf_op jit(solution)/shard_map/ppermute | solution.py:52
  51.5 12.3 %collective-permute-start.18 = (bf16[256,1152]{1,0:T(8,128)(2,1)S(1)}, bf16[256,1152]{1,0:T(8,128)(2,1)S(1)}, u32[]{:S(2)}, u32[]{:S(2)}) collective-permute-start(bf16[256,1152]{1,0:T(8,128)(2,1)S(1)} %shard_map.79), channel_id=1, source_target_pairs={{0,3},{1,2},{2,1},{3,0},{4,7},{5,6},{6,5},{7,4},{8,9},{9,8},{10,11... | collective-permute-start | bytes 1769480 | tf_op jit(solution)/shard_map/ppermute | solution.py:52
  52.5 11.3 %collective-permute-start.19 = (bf16[256,1152]{1,0:T(8,128)(2,1)S(1)}, bf16[256,1152]{1,0:T(8,128)(2,1)S(1)}, u32[]{:S(2)}, u32[]{:S(2)}) collective-permute-start(bf16[256,1152]{1,0:T(8,128)(2,1)S(1)} %shard_map.80), channel_id=1, source_target_pairs={{0,132},{1,133},{2,134},{3,135},{4,128},{5,129},{6,130},{7,131},{8... | collective-permute-start | bytes 1769480 | tf_op jit(solution)/shard_map/ppermute | solution.py:52
  62.8 6.5 %collective-permute-start.23 = (bf16[128,1152]{1,0:T(8,128)(2,1)S(1)}, bf16[128,1152]{1,0:T(8,128)(2,1)S(1)}, u32[]{:S(2)}, u32[]{:S(2)}) collective-permute-start(bf16[128,1152]{1,0:T(8,128)(2,1)S(1)} %fusion), channel_id=1, source_target_pairs={{0,112},{1,113},{2,114},{3,115},{4,116},{5,117},{6,118},{7,119},{8... | collective-permute-start | bytes 884744 | tf_op jit(solution)/shard_map/ppermute | solution.py:52
  64.2 6.5 %collective-permute-start.22 = (bf16[64,1152]{1,0:T(8,128)(2,1)S(1)}, bf16[64,1152]{1,0:T(8,128)(2,1)S(1)}, u32[]{:S(2)}, u32[]{:S(2)}) collective-permute-start(bf16[64,1152]{1,0:T(8,128)(2,1)S(1)} %get-tuple-element.48), channel_id=1, source_target_pairs={{0,4},{1,5},{2,6},{3,7},{4,0},{5,1},{6,2},{7,3},{8,140},{9,141},{1... | collective-permute-start | bytes 442376 | tf_op jit(solution)/shard_map/ppermute | solution.py:52
  64.9 5.7 %collective-permute-start.21 = (bf16[64,1152]{1,0:T(8,128)(2,1)S(1)}, bf16[64,1152]{1,0:T(8,128)(2,1)S(1)}, u32[]{:S(2)}, u32[]{:S(2)}) collective-permute-start(bf16[64,1152]{1,0:T(8,128)(2,1)S(1)} %get-tuple-element.49), channel_id=1, source_target_pairs={{0,1},{1,0},{2,3},{3,2},{4,5},{5,4},{6,7},{7,6},{8,11},{9,10},{10,... | collective-permute-start | bytes 442376 | tf_op jit(solution)/shard_map/ppermute | solution.py:52
  65.1 8.3 %collective-permute-start.20 = (bf16[64,1152]{1,0:T(8,128)(2,1)S(1)}, bf16[64,1152]{1,0:T(8,128)(2,1)S(1)}, u32[]{:S(2)}, u32[]{:S(2)}) collective-permute-start(bf16[64,1152]{1,0:T(8,128)(2,1)S(1)} %get-tuple-element.50), channel_id=1, source_target_pairs={{0,5},{1,4},{2,7},{3,6},{4,1},{5,0},{6,3},{7,2},{8,143},{9,142},{1... | collective-permute-start | bytes 442376 | tf_op jit(solution)/shard_map/ppermute | solution.py:52
  69.4 5.3 %collective-permute-start.24 = (bf16[64,1152]{1,0:T(8,128)(2,1)S(1)}, bf16[64,1152]{1,0:T(8,128)(2,1)S(1)}, u32[]{:S(2)}, u32[]{:S(2)}) collective-permute-start(bf16[64,1152]{1,0:T(8,128)(2,1)S(1)} %slice.113), channel_id=1, source_target_pairs={{0,16},{1,17},{2,18},{3,19},{4,20},{5,21},{6,22},{7,23},{8,120},{9... | collective-permute-start | bytes 442376 | tf_op jit(solution)/shard_map/ppermute | solution.py:52
  (5 other events, 20.8 us)

commit v6 on v5

--- a/solution.py
+++ b/solution.py
@@ -27,7 +27,7 @@
         for y in range(4):
             for z in range(8):
                 for core in range(2):
-                    side = first == (core == 0)
+                    side = first == (core == (1 if axis == "z" else 0))
                     to = [x, y, z, core]
                     if axis == "x":
                         to[0] = partner(x, 4, side)
@@ -281,9 +281,9 @@
         images,
         texts,
         quad_sums[:n],
+        y1(rounded(quad_sums[2 * n : 3 * n])),
+        x1(rounded(quad_sums[n : 2 * n])),
         d1(rounded(quad_sums[3 * n :])),
-        x1(rounded(quad_sums[n : 2 * n])),
-        y1(rounded(quad_sums[2 * n : 3 * n])),
     )
     return (image_grad, text_grad)
 

time: 75.8 us -> 75.4 us (level)
  the two profiles are of different devices: /device:TPU:1 before, /device:TPU:8 now
where the time goes in v6:
time: 75.4 us; the launch traced here: 75.1 us
  starting transfers between devices  38 us (50%)
  waiting for transfers between devices  18.6 us (25%)
  Pallas kernels  13.3 us (18%)
  between operations  2.28 us (3%)
  local copies, waits for them, and re-layouts  2.25 us (3%)
    ppermute x25, starting transfers between devices, permute(): return lambda value: lax.ppermute(value, AXES, pairs)  38 us
    ppermute x25, waiting for transfers between devices, permute(): return lambda value: lax.ppermute(value, AXES, pairs)  18.6 us
    pallas_call x16, Pallas kernels, on_device(): pl.pallas_call(kernel, out_shape=[jax.ShapeDtypeStruct(shape, kind) for s...  11.3 us
    pallas_call x2, Pallas kernels, grad_rows(): pl.pallas_call(grad_kernel, out_shape=jax.ShapeDtypeStruct(rows.shape, jn...  2.03 us
    unnamed x9, local copies, waits for them, and re-layouts  1.85 us
  transfers between devices with their start and end apart: 25, of which 10 were waited for; matrix products, arithmetic and copies ran while one was open for 1% of the time, Pallas kernels for 14%

profile of v6, /device:TPU:8, one launch (start us, length us, event | category | flops | bytes accessed | tf_op | source)
XLA Modules:
  0.0 75.1 jit_solution(3370643891865095015)
XLA Ops:
  0.6 5.9 %collective-permute-start = (bf16[64,1152]{1,0:T(8,128)(2,1)}, bf16[64,1152]{1,0:T(8,128)(2,1)S(1)}, u32[]{:S(2)}, u32[]{:S(2)}) collective-permute-start(bf16[64,1152]{1,0:T(8,128)(2,1)} %rows.7), channel_id=1, source_target_pairs={{0,112},{1,113},{2,114},{3,115},{4,116},{5,117},{6,118},{7,119},{8... | collective-permute-start | bytes 442376 | tf_op jit(solution)/shard_map/ppermute | solution.py:52
  6.6 1.4 %collective-permute-start.3 = (bf16[64,1152]{1,0:T(8,128)(2,1)}, bf16[64,1152]{1,0:T(8,128)(2,1)S(1)}, u32[]{:S(2)}, u32[]{:S(2)}) collective-permute-start(bf16[64,1152]{1,0:T(8,128)(2,1)} %others.3), channel_id=1, source_target_pairs={{0,5},{1,4},{2,7},{3,6},{4,1},{5,0},{6,3},{7,2},{8,143},{9,142},{1... | collective-permute-start | bytes 442376 | tf_op jit(solution)/shard_map/ppermute | solution.py:52
  8.5 1.6 %collective-permute-start.1 = (bf16[64,1152]{1,0:T(8,128)(2,1)}, bf16[64,1152]{1,0:T(8,128)(2,1)S(1)}, u32[]{:S(2)}, u32[]{:S(2)}) collective-permute-start(bf16[64,1152]{1,0:T(8,128)(2,1)} %others.3), channel_id=1, source_target_pairs={{0,4},{1,5},{2,6},{3,7},{4,0},{5,1},{6,2},{7,3},{8,140},{9,141},{1... | collective-permute-start | bytes 442376 | tf_op jit(solution)/shard_map/ppermute | solution.py:52
  14.9 1.9 %collective-permute-start.9 = (bf16[256,1152]{1,0:T(8,128)(2,1)S(1)}, bf16[256,1152]{1,0:T(8,128)(2,1)S(1)}, u32[]{:S(2)}, u32[]{:S(2)}) collective-permute-start(bf16[256,1152]{1,0:T(8,128)(2,1)S(1)} %shard_map.68.refs_2_.quad.refs_1_.refs_0_), channel_id=1, source_target_pairs={{0,132},{1,133},{2,134},{3,135},{4,128},{5,129},{6,130},{7,131},{8... | collective-permute-start | bytes 1769480 | tf_op jit(solution)/shard_map/ppermute | solution.py:52
  16.8 2.8 %collective-permute-start.8 = (bf16[256,1152]{1,0:T(8,128)(2,1)S(1)}, bf16[256,1152]{1,0:T(8,128)(2,1)S(1)}, u32[]{:S(2)}, u32[]{:S(2)}) collective-permute-start(bf16[256,1152]{1,0:T(8,128)(2,1)S(1)} %shard_map.68.refs_2_.quad.refs_1_.refs_0_), channel_id=1, source_target_pairs={{0,3},{1,2},{2,1},{3,0},{4,7},{5,6},{6,5},{7,4},{8,9},{9,8},{10,11... | collective-permute-start | bytes 1769480 | tf_op jit(solution)/shard_map/ppermute | solution.py:52
  19.6 1.8 %collective-permute-done.4 = bf16[128,1152]{1,0:T(8,128)(2,1)S(1)} collective-permute-done((bf16[128,1152]{1,0:T(8,128)(2,1)S(1)}, bf16[128,1152]{1,0:T(8,128)(2,1)S(1)}, u32[]{:S(2)}, u32[]{:S(2)}) %collective-permute-start.4) | collective-permute-done | bytes 294944 | tf_op jit(solution)/shard_map/ppermute | solution.py:52
  21.6 1.5 %collective-permute-start.6 = (bf16[128,1152]{1,0:T(8,128)(2,1)S(1)}, bf16[128,1152]{1,0:T(8,128)(2,1)S(1)}, u32[]{:S(2)}, u32[]{:S(2)}) collective-permute-start(bf16[128,1152]{1,0:T(8,128)(2,1)S(1)} %collective-permute-done.4), channel_id=1, source_target_pairs={{0,96},{1,97},{2,98},{3,99},{4,100},{5,101},{6,102},{7,103},{8,40}... | collective-permute-start | bytes 884744 | tf_op jit(solution)/shard_map/ppermute | solution.py:52
  23.1 1.4 %collective-permute-start.5 = (bf16[128,1152]{1,0:T(8,128)(2,1)S(1)}, bf16[128,1152]{1,0:T(8,128)(2,1)S(1)}, u32[]{:S(2)}, u32[]{:S(2)}) collective-permute-start(bf16[128,1152]{1,0:T(8,128)(2,1)S(1)} %collective-permute-done.4), channel_id=1, source_target_pairs={{0,112},{1,113},{2,114},{3,115},{4,116},{5,117},{6,118},{7,119},{8... | collective-permute-start | bytes 884744 | tf_op jit(solution)/shard_map/ppermute | solution.py:52
  24.9 2.8 %collective-permute-start.11 = (bf16[128,1152]{1,0:T(8,128)(2,1)S(1)}, bf16[128,1152]{1,0:T(8,128)(2,1)S(1)}, u32[]{:S(2)}, u32[]{:S(2)}) collective-permute-start(bf16[128,1152]{1,0:T(8,128)(2,1)S(1)} %slice.93), channel_id=1, source_target_pairs={{0,3},{1,2},{2,1},{3,0},{4,7},{5,6},{6,5},{7,4},{8,9},{9,8},{10,11... | collective-permute-start | bytes 884744 | tf_op jit(solution)/shard_map/ppermute | solution.py:52
  27.9 1.8 %collective-permute-start.10 = (bf16[128,1152]{1,0:T(8,128)(2,1)S(1)}, bf16[128,1152]{1,0:T(8,128)(2,1)S(1)}, u32[]{:S(2)}, u32[]{:S(2)}) collective-permute-start(bf16[128,1152]{1,0:T(8,128)(2,1)S(1)} %slice.92), channel_id=1, source_target_pairs={{0,132},{1,133},{2,134},{3,135},{4,128},{5,129},{6,130},{7,131},{8... | collective-permute-start | bytes 884744 | tf_op jit(solution)/shard_map/ppermute | solution.py:52
  30.3 1.0 %shard_map.70.w_axy = bf16[512,512]{1,0:T(8,128)(2,1)S(1)} custom-call(f32[8,128]{1,0:T(8,128)S(1)} %concatenate.12.coefficients, bf16[256,1152]{1,0:T(8,128)(2,1)S(1)} %pad_maximum_fusion.refs_0_.refs_3_, bf16[256,1152]{1,0:T(8,128)(2,1)S(1)} %collective-permute-done.7.refs_1_.refs_4_, bf16[256,1152]{1,0:T(8,128)(2,1)S(1)} %collective-permute-done.8.refs_2_.part_x.refs_1_, ...), custom_call_target="tpu_custom_call" | custom-call | tf_op jit(solution)/shard_map/pallas_call | solution.py:179
  31.3 1.2 %shard_map.71.part = f32[512,1152]{1,0:T(8,128)S(1)} custom-call(bf16[512,256]{1,0:T(8,128)(2,1)S(1)} %shard_map.69.w_aq.refs_0_, bf16[512,512]{1,0:T(8,128)(2,1)S(1)} %shard_map.70.w_axy, bf16[256,1152]{1,0:T(8,128)(2,1)S(1)} %shard_map.68.refs_2_.quad.refs_1_.refs_0_, bf16[256,1152]{1,0:T(8,128)(2,1)S(1)} %collective-permute-done.8.refs_2_.part_x.refs_1_, ...), custom_call_target="tpu_custom_call" | custom-call | tf_op jit(solution)/shard_map/pallas_call | solution.py:179
  32.5 3.0 %collective-permute-done.5 = bf16[128,1152]{1,0:T(8,128)(2,1)S(1)} collective-permute-done((bf16[128,1152]{1,0:T(8,128)(2,1)S(1)}, bf16[128,1152]{1,0:T(8,128)(2,1)S(1)}, u32[]{:S(2)}, u32[]{:S(2)}) %collective-permute-start.5) | collective-permute-done | bytes 294944 | tf_op jit(solution)/shard_map/ppermute | solution.py:52
  37.8 1.6 %shard_map.75 = (bf16[256,1024]{1,0:T(8,128)(2,1)S(1)}, bf16[256,1152]{1,0:T(8,128)(2,1)S(1)}) custom-call(f32[8,128]{1,0:T(8,128)S(1)} %concatenate.12.coefficients, bf16[256,1152]{1,0:T(8,128)(2,1)S(1)} %collective-permute-done.12.sib_c.refs_6_, bf16[256,1152]{1,0:T(8,128)(2,1)S(1)} %shard_map.68.refs_2_.quad.refs_1_.refs_0_, ...), custom_call_target="tpu_custom_call" | custom-call | flops 1207959552 | tf_op jit(solution)/shard_map/pallas_call | solution.py:179
  41.5 4.0 %collective-permute-start.17 = (bf16[256,1152]{1,0:T(8,128)(2,1)S(1)}, bf16[256,1152]{1,0:T(8,128)(2,1)S(1)}, u32[]{:S(2)}, u32[]{:S(2)}) collective-permute-start(bf16[256,1152]{1,0:T(8,128)(2,1)S(1)} %shard_map.76), channel_id=1, source_target_pairs={{0,135},{1,134},{2,133},{3,132},{4,131},{5,130},{6,129},{7,128},{8... | collective-permute-start | bytes 1769480 | tf_op jit(solution)/shard_map/ppermute | solution.py:52
  46.2 1.3 %collective-permute-start.15 = (bf16[128,1152]{1,0:T(8,128)(2,1)S(1)}, bf16[128,1152]{1,0:T(8,128)(2,1)S(1)}, u32[]{:S(2)}, u32[]{:S(2)}) collective-permute-start(bf16[128,1152]{1,0:T(8,128)(2,1)S(1)} %get-tuple-element.51), channel_id=1, source_target_pairs={{0,112},{1,113},{2,114},{3,115},{4,116},{5,117},{6,118},{7,119},{8... | collective-permute-start | bytes 884744 | tf_op jit(solution)/shard_map/ppermute | solution.py:52
  48.4 1.7 %collective-permute-start.18 = (bf16[256,1152]{1,0:T(8,128)(2,1)S(1)}, bf16[256,1152]{1,0:T(8,128)(2,1)S(1)}, u32[]{:S(2)}, u32[]{:S(2)}) collective-permute-start(bf16[256,1152]{1,0:T(8,128)(2,1)S(1)} %shard_map.79), channel_id=1, source_target_pairs={{0,3},{1,2},{2,1},{3,0},{4,7},{5,6},{6,5},{7,4},{8,9},{9,8},{10,11... | collective-permute-start | bytes 1769480 | tf_op jit(solution)/shard_map/ppermute | solution.py:52
  51.0 1.3 %collective-permute-start.19 = (bf16[256,1152]{1,0:T(8,128)(2,1)S(1)}, bf16[256,1152]{1,0:T(8,128)(2,1)S(1)}, u32[]{:S(2)}, u32[]{:S(2)}) collective-permute-start(bf16[256,1152]{1,0:T(8,128)(2,1)S(1)} %shard_map.80), channel_id=1, source_target_pairs={{0,132},{1,133},{2,134},{3,135},{4,128},{5,129},{6,130},{7,131},{8... | collective-permute-start | bytes 1769480 | tf_op jit(solution)/shard_map/ppermute | solution.py:52
  52.4 7.5 %collective-permute-done.15 = bf16[128,1152]{1,0:T(8,128)(2,1)S(1)} collective-permute-done((bf16[128,1152]{1,0:T(8,128)(2,1)S(1)}, bf16[128,1152]{1,0:T(8,128)(2,1)S(1)}, u32[]{:S(2)}, u32[]{:S(2)}) %collective-permute-start.15) | collective-permute-done | bytes 294944 | tf_op jit(solution)/shard_map/ppermute | solution.py:52
  61.3 3.2 %collective-permute-start.22 = (bf16[64,1152]{1,0:T(8,128)(2,1)S(1)}, bf16[64,1152]{1,0:T(8,128)(2,1)S(1)}, u32[]{:S(2)}, u32[]{:S(2)}) collective-permute-start(bf16[64,1152]{1,0:T(8,128)(2,1)S(1)} %get-tuple-element.48), channel_id=1, source_target_pairs={{0,5},{1,4},{2,7},{3,6},{4,1},{5,0},{6,3},{7,2},{8,143},{9,142},{1... | collective-permute-start | bytes 442376 | tf_op jit(solution)/shard_map/ppermute | solution.py:52
  64.6 3.0 %collective-permute-start.21 = (bf16[64,1152]{1,0:T(8,128)(2,1)S(1)}, bf16[64,1152]{1,0:T(8,128)(2,1)S(1)}, u32[]{:S(2)}, u32[]{:S(2)}) collective-permute-start(bf16[64,1152]{1,0:T(8,128)(2,1)S(1)} %get-tuple-element.49), channel_id=1, source_target_pairs={{0,1},{1,0},{2,3},{3,2},{4,5},{5,4},{6,7},{7,6},{8,11},{9,10},{10,... | collective-permute-start | bytes 442376 | tf_op jit(solution)/shard_map/ppermute | solution.py:52
  68.7 3.6 %collective-permute-done.21.rest_1_ = bf16[64,1152]{1,0:T(8,128)(2,1)S(1)} collective-permute-done((bf16[64,1152]{1,0:T(8,128)(2,1)S(1)}, bf16[64,1152]{1,0:T(8,128)(2,1)S(1)}, u32[]{:S(2)}, u32[]{:S(2)}) %collective-permute-start.21) | collective-permute-done | bytes 147488 | tf_op jit(solution)/shard_map/ppermute | solution.py:52
  72.7 1.0 %shard_map.81 = f32[64,1152]{1,0:T(8,128)} custom-call(f32[8,128]{1,0:T(8,128)S(1)} %concatenate.12.coefficients, bf16[64,1152]{1,0:T(8,128)(2,1)S(1)} %copy-done.1, bf16[64,1152]{1,0:T(8,128)(2,1)S(1)} %copy-done.3, f32[64,1152]{1,0:T(8,128)S(1)} %slice.101.sums, bf16[64,1152]{1,0:T(8,128)(2,1)S(1)} %collective-permute-done.20.rest_0_, ...), custom_call_target="tpu_custom_call" | custom-call | tf_op jit(solution)/shard_map/pallas_call | solution.py:102
  74.1 1.0 %shard_map.82 = f32[64,1152]{1,0:T(8,128)} custom-call(f32[8,128]{1,0:T(8,128)S(1)} %concatenate.12.coefficients, bf16[64,1152]{1,0:T(8,128)(2,1)S(1)} %copy-done.3, bf16[64,1152]{1,0:T(8,128)(2,1)S(1)} %copy-done.1, f32[64,1152]{1,0:T(8,128)S(1)} %slice.106.sums, bf16[64,1152]{1,0:T(8,128)(2,1)S(1)} %collective-permute-done.24.rest_0_), custom_call_target="tpu_custom_call" | custom-call | tf_op jit(solution)/shard_map/pallas_call | solution.py:102
  (73 shorter events, 15.5 us)
Async XLA Ops:
  0.6 12.8 %collective-permute-start = (bf16[64,1152]{1,0:T(8,128)(2,1)}, bf16[64,1152]{1,0:T(8,128)(2,1)S(1)}, u32[]{:S(2)}, u32[]{:S(2)}) collective-permute-start(bf16[64,1152]{1,0:T(8,128)(2,1)} %rows.7), channel_id=1, source_target_pairs={{0,112},{1,113},{2,114},{3,115},{4,116},{5,117},{6,118},{7,119},{8... | collective-permute-start | bytes 442376 | tf_op jit(solution)/shard_map/ppermute | solution.py:52
  6.6 6.9 %collective-permute-start.3 = (bf16[64,1152]{1,0:T(8,128)(2,1)}, bf16[64,1152]{1,0:T(8,128)(2,1)S(1)}, u32[]{:S(2)}, u32[]{:S(2)}) collective-permute-start(bf16[64,1152]{1,0:T(8,128)(2,1)} %others.3), channel_id=1, source_target_pairs={{0,5},{1,4},{2,7},{3,6},{4,1},{5,0},{6,3},{7,2},{8,143},{9,142},{1... | collective-permute-start | bytes 442376 | tf_op jit(solution)/shard_map/ppermute | solution.py:52
  7.9 5.5 %collective-permute-start.2 = (bf16[64,1152]{1,0:T(8,128)(2,1)}, bf16[64,1152]{1,0:T(8,128)(2,1)S(1)}, u32[]{:S(2)}, u32[]{:S(2)}) collective-permute-start(bf16[64,1152]{1,0:T(8,128)(2,1)} %others.3), channel_id=1, source_target_pairs={{0,1},{1,0},{2,3},{3,2},{4,5},{5,4},{6,7},{7,6},{8,11},{9,10},{10,... | collective-permute-start | bytes 442376 | tf_op jit(solution)/shard_map/ppermute | solution.py:52
  8.5 5.9 %collective-permute-start.1 = (bf16[64,1152]{1,0:T(8,128)(2,1)}, bf16[64,1152]{1,0:T(8,128)(2,1)S(1)}, u32[]{:S(2)}, u32[]{:S(2)}) collective-permute-start(bf16[64,1152]{1,0:T(8,128)(2,1)} %others.3), channel_id=1, source_target_pairs={{0,4},{1,5},{2,6},{3,7},{4,0},{5,1},{6,2},{7,3},{8,140},{9,141},{1... | collective-permute-start | bytes 442376 | tf_op jit(solution)/shard_map/ppermute | solution.py:52
  14.6 6.8 %collective-permute-start.4 = (bf16[128,1152]{1,0:T(8,128)(2,1)S(1)}, bf16[128,1152]{1,0:T(8,128)(2,1)S(1)}, u32[]{:S(2)}, u32[]{:S(2)}) collective-permute-start(bf16[128,1152]{1,0:T(8,128)(2,1)S(1)} %shard_map.67), channel_id=1, source_target_pairs={{0,16},{1,17},{2,18},{3,19},{4,20},{5,21},{6,22},{7,23},{8,120},{9... | collective-permute-start | bytes 884744 | tf_op jit(solution)/shard_map/ppermute | solution.py:52
  14.9 10.0 %collective-permute-start.9 = (bf16[256,1152]{1,0:T(8,128)(2,1)S(1)}, bf16[256,1152]{1,0:T(8,128)(2,1)S(1)}, u32[]{:S(2)}, u32[]{:S(2)}) collective-permute-start(bf16[256,1152]{1,0:T(8,128)(2,1)S(1)} %shard_map.68.refs_2_.quad.refs_1_.refs_0_), channel_id=1, source_target_pairs={{0,132},{1,133},{2,134},{3,135},{4,128},{5,129},{6,130},{7,131},{8... | collective-permute-start | bytes 1769480 | tf_op jit(solution)/shard_map/ppermute | solution.py:52
  16.8 11.1 %collective-permute-start.8 = (bf16[256,1152]{1,0:T(8,128)(2,1)S(1)}, bf16[256,1152]{1,0:T(8,128)(2,1)S(1)}, u32[]{:S(2)}, u32[]{:S(2)}) collective-permute-start(bf16[256,1152]{1,0:T(8,128)(2,1)S(1)} %shard_map.68.refs_2_.quad.refs_1_.refs_0_), channel_id=1, source_target_pairs={{0,3},{1,2},{2,1},{3,0},{4,7},{5,6},{6,5},{7,4},{8,9},{9,8},{10,11... | collective-permute-start | bytes 1769480 | tf_op jit(solution)/shard_map/ppermute | solution.py:52
  21.5 8.2 %collective-permute-start.7 = (bf16[256,1152]{1,0:T(8,128)(2,1)S(1)}, bf16[256,1152]{1,0:T(8,128)(2,1)S(1)}, u32[]{:S(2)}, u32[]{:S(2)}) collective-permute-start(bf16[256,1152]{1,0:T(8,128)(2,1)S(1)} %pad_maximum_fusion.refs_0_.refs_3_), channel_id=1, source_target_pairs={{0,8},{1,9},{2,10},{3,11},{4,12},{5,13},{6,14},{7,15},{8,0},{9,1},... | collective-permute-start | bytes 1769480 | tf_op jit(solution)/shard_map/ppermute | solution.py:52
  21.6 10.9 %collective-permute-start.6 = (bf16[128,1152]{1,0:T(8,128)(2,1)S(1)}, bf16[128,1152]{1,0:T(8,128)(2,1)S(1)}, u32[]{:S(2)}, u32[]{:S(2)}) collective-permute-start(bf16[128,1152]{1,0:T(8,128)(2,1)S(1)} %collective-permute-done.4), channel_id=1, source_target_pairs={{0,96},{1,97},{2,98},{3,99},{4,100},{5,101},{6,102},{7,103},{8,40}... | collective-permute-start | bytes 884744 | tf_op jit(solution)/shard_map/ppermute | solution.py:52
  23.1 12.4 %collective-permute-start.5 = (bf16[128,1152]{1,0:T(8,128)(2,1)S(1)}, bf16[128,1152]{1,0:T(8,128)(2,1)S(1)}, u32[]{:S(2)}, u32[]{:S(2)}) collective-permute-start(bf16[128,1152]{1,0:T(8,128)(2,1)S(1)} %collective-permute-done.4), channel_id=1, source_target_pairs={{0,112},{1,113},{2,114},{3,115},{4,116},{5,117},{6,118},{7,119},{8... | collective-permute-start | bytes 884744 | tf_op jit(solution)/shard_map/ppermute | solution.py:52
  24.9 11.0 %collective-permute-start.11 = (bf16[128,1152]{1,0:T(8,128)(2,1)S(1)}, bf16[128,1152]{1,0:T(8,128)(2,1)S(1)}, u32[]{:S(2)}, u32[]{:S(2)}) collective-permute-start(bf16[128,1152]{1,0:T(8,128)(2,1)S(1)} %slice.93), channel_id=1, source_target_pairs={{0,3},{1,2},{2,1},{3,0},{4,7},{5,6},{6,5},{7,4},{8,9},{9,8},{10,11... | collective-permute-start | bytes 884744 | tf_op jit(solution)/shard_map/ppermute | solution.py:52
  27.9 7.9 %collective-permute-start.10 = (bf16[128,1152]{1,0:T(8,128)(2,1)S(1)}, bf16[128,1152]{1,0:T(8,128)(2,1)S(1)}, u32[]{:S(2)}, u32[]{:S(2)}) collective-permute-start(bf16[128,1152]{1,0:T(8,128)(2,1)S(1)} %slice.92), channel_id=1, source_target_pairs={{0,132},{1,133},{2,134},{3,135},{4,128},{5,129},{6,130},{7,131},{8... | collective-permute-start | bytes 884744 | tf_op jit(solution)/shard_map/ppermute | solution.py:52
  39.4 6.0 %collective-permute-start.13 = (bf16[256,1152]{1,0:T(8,128)(2,1)S(1)}, bf16[256,1152]{1,0:T(8,128)(2,1)S(1)}, u32[]{:S(2)}, u32[]{:S(2)}) collective-permute-start(bf16[256,1152]{1,0:T(8,128)(2,1)S(1)} %get-tuple-element.38), channel_id=1, source_target_pairs={{0,8},{1,9},{2,10},{3,11},{4,12},{5,13},{6,14},{7,15},{8,0},{9,1},... | collective-permute-start | bytes 1769480 | tf_op jit(solution)/shard_map/ppermute | solution.py:52
  41.5 19.5 %collective-permute-start.17 = (bf16[256,1152]{1,0:T(8,128)(2,1)S(1)}, bf16[256,1152]{1,0:T(8,128)(2,1)S(1)}, u32[]{:S(2)}, u32[]{:S(2)}) collective-permute-start(bf16[256,1152]{1,0:T(8,128)(2,1)S(1)} %shard_map.76), channel_id=1, source_target_pairs={{0,135},{1,134},{2,133},{3,132},{4,131},{5,130},{6,129},{7,128},{8... | collective-permute-start | bytes 1769480 | tf_op jit(solution)/shard_map/ppermute | solution.py:52
  46.1 4.9 %collective-permute-start.14 = (bf16[256,1152]{1,0:T(8,128)(2,1)S(1)}, bf16[256,1152]{1,0:T(8,128)(2,1)S(1)}, u32[]{:S(2)}, u32[]{:S(2)}) collective-permute-start(bf16[256,1152]{1,0:T(8,128)(2,1)S(1)} %get-tuple-element.41), channel_id=1, source_target_pairs={{0,8},{1,9},{2,10},{3,11},{4,12},{5,13},{6,14},{7,15},{8,0},{9,1},... | collective-permute-start | bytes 1769480 | tf_op jit(solution)/shard_map/ppermute | solution.py:52
  46.2 13.7 %collective-permute-start.15 = (bf16[128,1152]{1,0:T(8,128)(2,1)S(1)}, bf16[128,1152]{1,0:T(8,128)(2,1)S(1)}, u32[]{:S(2)}, u32[]{:S(2)}) collective-permute-start(bf16[128,1152]{1,0:T(8,128)(2,1)S(1)} %get-tuple-element.51), channel_id=1, source_target_pairs={{0,112},{1,113},{2,114},{3,115},{4,116},{5,117},{6,118},{7,119},{8... | collective-permute-start | bytes 884744 | tf_op jit(solution)/shard_map/ppermute | solution.py:52
  47.5 12.4 %collective-permute-start.16 = (bf16[128,1152]{1,0:T(8,128)(2,1)S(1)}, bf16[128,1152]{1,0:T(8,128)(2,1)S(1)}, u32[]{:S(2)}, u32[]{:S(2)}) collective-permute-start(bf16[128,1152]{1,0:T(8,128)(2,1)S(1)} %get-tuple-element.52), channel_id=1, source_target_pairs={{0,32},{1,33},{2,34},{3,35},{4,36},{5,37},{6,38},{7,39},{8,104},{9... | collective-permute-start | bytes 884744 | tf_op jit(solution)/shard_map/ppermute | solution.py:52
  48.4 12.6 %collective-permute-start.18 = (bf16[256,1152]{1,0:T(8,128)(2,1)S(1)}, bf16[256,1152]{1,0:T(8,128)(2,1)S(1)}, u32[]{:S(2)}, u32[]{:S(2)}) collective-permute-start(bf16[256,1152]{1,0:T(8,128)(2,1)S(1)} %shard_map.79), channel_id=1, source_target_pairs={{0,3},{1,2},{2,1},{3,0},{4,7},{5,6},{6,5},{7,4},{8,9},{9,8},{10,11... | collective-permute-start | bytes 1769480 | tf_op jit(solution)/shard_map/ppermute | solution.py:52
  51.0 10.0 %collective-permute-start.19 = (bf16[256,1152]{1,0:T(8,128)(2,1)S(1)}, bf16[256,1152]{1,0:T(8,128)(2,1)S(1)}, u32[]{:S(2)}, u32[]{:S(2)}) collective-permute-start(bf16[256,1152]{1,0:T(8,128)(2,1)S(1)} %shard_map.80), channel_id=1, source_target_pairs={{0,132},{1,133},{2,134},{3,135},{4,128},{5,129},{6,130},{7,131},{8... | collective-permute-start | bytes 1769480 | tf_op jit(solution)/shard_map/ppermute | solution.py:52
  60.0 7.6 %collective-permute-start.23 = (bf16[128,1152]{1,0:T(8,128)(2,1)S(1)}, bf16[128,1152]{1,0:T(8,128)(2,1)S(1)}, u32[]{:S(2)}, u32[]{:S(2)}) collective-permute-start(bf16[128,1152]{1,0:T(8,128)(2,1)S(1)} %fusion), channel_id=1, source_target_pairs={{0,16},{1,17},{2,18},{3,19},{4,20},{5,21},{6,22},{7,23},{8,120},{9... | collective-permute-start | bytes 884744 | tf_op jit(solution)/shard_map/ppermute | solution.py:52
  61.3 7.3 %collective-permute-start.22 = (bf16[64,1152]{1,0:T(8,128)(2,1)S(1)}, bf16[64,1152]{1,0:T(8,128)(2,1)S(1)}, u32[]{:S(2)}, u32[]{:S(2)}) collective-permute-start(bf16[64,1152]{1,0:T(8,128)(2,1)S(1)} %get-tuple-element.48), channel_id=1, source_target_pairs={{0,5},{1,4},{2,7},{3,6},{4,1},{5,0},{6,3},{7,2},{8,143},{9,142},{1... | collective-permute-start | bytes 442376 | tf_op jit(solution)/shard_map/ppermute | solution.py:52
  64.6 7.7 %collective-permute-start.21 = (bf16[64,1152]{1,0:T(8,128)(2,1)S(1)}, bf16[64,1152]{1,0:T(8,128)(2,1)S(1)}, u32[]{:S(2)}, u32[]{:S(2)}) collective-permute-start(bf16[64,1152]{1,0:T(8,128)(2,1)S(1)} %get-tuple-element.49), channel_id=1, source_target_pairs={{0,1},{1,0},{2,3},{3,2},{4,5},{5,4},{6,7},{7,6},{8,11},{9,10},{10,... | collective-permute-start | bytes 442376 | tf_op jit(solution)/shard_map/ppermute | solution.py:52
  67.6 5.1 %collective-permute-start.20 = (bf16[64,1152]{1,0:T(8,128)(2,1)S(1)}, bf16[64,1152]{1,0:T(8,128)(2,1)S(1)}, u32[]{:S(2)}, u32[]{:S(2)}) collective-permute-start(bf16[64,1152]{1,0:T(8,128)(2,1)S(1)} %get-tuple-element.50), channel_id=1, source_target_pairs={{0,4},{1,5},{2,6},{3,7},{4,0},{5,1},{6,2},{7,3},{8,140},{9,141},{1... | collective-permute-start | bytes 442376 | tf_op jit(solution)/shard_map/ppermute | solution.py:52
  67.7 6.4 %collective-permute-start.24 = (bf16[64,1152]{1,0:T(8,128)(2,1)S(1)}, bf16[64,1152]{1,0:T(8,128)(2,1)S(1)}, u32[]{:S(2)}, u32[]{:S(2)}) collective-permute-start(bf16[64,1152]{1,0:T(8,128)(2,1)S(1)} %slice.113), channel_id=1, source_target_pairs={{0,112},{1,113},{2,114},{3,115},{4,116},{5,117},{6,118},{7,119},{8... | collective-permute-start | bytes 442376 | tf_op jit(solution)/shard_map/ppermute | solution.py:52
  (5 other events, 14.4 us)

commit v7 on v6

--- a/solution.py
+++ b/solution.py
@@ -88,13 +88,21 @@
 
 
 def grad_kernel(coefficients, rows, others, sums, *rest):
-    *arrived, grad = rest
-    unit, inverse = unit_rows(rows[...])
-    other_send = widened(rounded(unit_rows(others[...])[0]))
-    total = sums[...] - scale_and_bias(coefficients)[0] * other_send
-    for part in arrived:
-        total = total + widened(part[...])
-    grad[...] = through_norm(unit, inverse, total)
+    *arrived, grad, held, sent = rest
+    half = held.shape[0] // 2
+    copies = []
+    for index in range(2):
+        span = pl.ds(index * half, half)
+        unit, inverse = unit_rows(rows[span])
+        other_send = widened(rounded(unit_rows(others[span])[0]))
+        total = sums[span] - scale_and_bias(coefficients)[0] * other_send
+        for part in arrived:
+            total = total + widened(part[span])
+        held[span] = through_norm(unit, inverse, total)
+        copies.append(pltpu.make_async_copy(held.at[span], grad.at[span], sent.at[index]))
+        copies[-1].start()
+    for copy in copies:
+        copy.wait()
 
 
 def grad_rows(coefficients, rows, others, sums, *arrived):
@@ -103,7 +111,8 @@
         grad_kernel,
         out_shape=jax.ShapeDtypeStruct(rows.shape, jnp.float32),
         in_specs=[whole] * (4 + len(arrived)),
-        out_specs=whole,
+        out_specs=pl.BlockSpec(memory_space=pl.ANY),
+        scratch_shapes=[pltpu.VMEM(rows.shape, jnp.float32), pltpu.SemaphoreType.DMA((2,))],
         compiler_params=pltpu.CompilerParams(vmem_limit_bytes=4 * 2**20),
     )(coefficients, rows, others, sums, *arrived)
 

time: 75.4 us -> 75.5 us (level)
  no operation moved by 1% of the time
where the time goes in v7:
time: 75.5 us; the launch traced here: 75.3 us
  starting transfers between devices  38 us (50%)
  waiting for transfers between devices  18.6 us (25%)
  Pallas kernels  13.3 us (18%)
  between operations  2.45 us (3%)
  local copies, waits for them, and re-layouts  2.25 us (3%)
    ppermute x25, starting transfers between devices, permute(): return lambda value: lax.ppermute(value, AXES, pairs)  38 us
    ppermute x25, waiting for transfers between devices, permute(): return lambda value: lax.ppermute(value, AXES, pairs)  18.6 us
    pallas_call x16, Pallas kernels, on_device(): pl.pallas_call(kernel, out_shape=[jax.ShapeDtypeStruct(shape, kind) for s...  11.3 us
    pallas_call x2, Pallas kernels, grad_rows(): pl.pallas_call(grad_kernel, out_shape=jax.ShapeDtypeStruct(rows.shape, jn...  1.95 us
    unnamed x9, local copies, waits for them, and re-layouts  1.85 us
  transfers between devices with their start and end apart: 25, of which 10 were waited for; matrix products, arithmetic and copies ran while one was open for 1% of the time, Pallas kernels for 14%

profile of v7, /device:TPU:8, one launch (start us, length us, event | category | flops | bytes accessed | tf_op | source)
XLA Modules:
  0.0 75.3 jit_solution(2748856887849910137)
XLA Ops:
  0.6 5.9 %collective-permute-start = (bf16[64,1152]{1,0:T(8,128)(2,1)}, bf16[64,1152]{1,0:T(8,128)(2,1)S(1)}, u32[]{:S(2)}, u32[]{:S(2)}) collective-permute-start(bf16[64,1152]{1,0:T(8,128)(2,1)} %rows.7), channel_id=1, source_target_pairs={{0,112},{1,113},{2,114},{3,115},{4,116},{5,117},{6,118},{7,119},{8... | collective-permute-start | bytes 442376 | tf_op jit(solution)/shard_map/ppermute | solution.py:52
  6.6 1.4 %collective-permute-start.3 = (bf16[64,1152]{1,0:T(8,128)(2,1)}, bf16[64,1152]{1,0:T(8,128)(2,1)S(1)}, u32[]{:S(2)}, u32[]{:S(2)}) collective-permute-start(bf16[64,1152]{1,0:T(8,128)(2,1)} %others.3), channel_id=1, source_target_pairs={{0,5},{1,4},{2,7},{3,6},{4,1},{5,0},{6,3},{7,2},{8,143},{9,142},{1... | collective-permute-start | bytes 442376 | tf_op jit(solution)/shard_map/ppermute | solution.py:52
  8.5 1.6 %collective-permute-start.1 = (bf16[64,1152]{1,0:T(8,128)(2,1)}, bf16[64,1152]{1,0:T(8,128)(2,1)S(1)}, u32[]{:S(2)}, u32[]{:S(2)}) collective-permute-start(bf16[64,1152]{1,0:T(8,128)(2,1)} %others.3), channel_id=1, source_target_pairs={{0,4},{1,5},{2,6},{3,7},{4,0},{5,1},{6,2},{7,3},{8,140},{9,141},{1... | collective-permute-start | bytes 442376 | tf_op jit(solution)/shard_map/ppermute | solution.py:52
  14.9 1.9 %collective-permute-start.9 = (bf16[256,1152]{1,0:T(8,128)(2,1)S(1)}, bf16[256,1152]{1,0:T(8,128)(2,1)S(1)}, u32[]{:S(2)}, u32[]{:S(2)}) collective-permute-start(bf16[256,1152]{1,0:T(8,128)(2,1)S(1)} %shard_map.68.refs_2_.quad.refs_1_.refs_0_), channel_id=1, source_target_pairs={{0,132},{1,133},{2,134},{3,135},{4,128},{5,129},{6,130},{7,131},{8... | collective-permute-start | bytes 1769480 | tf_op jit(solution)/shard_map/ppermute | solution.py:52
  16.8 2.8 %collective-permute-start.8 = (bf16[256,1152]{1,0:T(8,128)(2,1)S(1)}, bf16[256,1152]{1,0:T(8,128)(2,1)S(1)}, u32[]{:S(2)}, u32[]{:S(2)}) collective-permute-start(bf16[256,1152]{1,0:T(8,128)(2,1)S(1)} %shard_map.68.refs_2_.quad.refs_1_.refs_0_), channel_id=1, source_target_pairs={{0,3},{1,2},{2,1},{3,0},{4,7},{5,6},{6,5},{7,4},{8,9},{9,8},{10,11... | collective-permute-start | bytes 1769480 | tf_op jit(solution)/shard_map/ppermute | solution.py:52
  19.6 1.8 %collective-permute-done.4 = bf16[128,1152]{1,0:T(8,128)(2,1)S(1)} collective-permute-done((bf16[128,1152]{1,0:T(8,128)(2,1)S(1)}, bf16[128,1152]{1,0:T(8,128)(2,1)S(1)}, u32[]{:S(2)}, u32[]{:S(2)}) %collective-permute-start.4) | collective-permute-done | bytes 294944 | tf_op jit(solution)/shard_map/ppermute | solution.py:52
  21.6 1.5 %collective-permute-start.6 = (bf16[128,1152]{1,0:T(8,128)(2,1)S(1)}, bf16[128,1152]{1,0:T(8,128)(2,1)S(1)}, u32[]{:S(2)}, u32[]{:S(2)}) collective-permute-start(bf16[128,1152]{1,0:T(8,128)(2,1)S(1)} %collective-permute-done.4), channel_id=1, source_target_pairs={{0,96},{1,97},{2,98},{3,99},{4,100},{5,101},{6,102},{7,103},{8,40}... | collective-permute-start | bytes 884744 | tf_op jit(solution)/shard_map/ppermute | solution.py:52
  23.1 1.4 %collective-permute-start.5 = (bf16[128,1152]{1,0:T(8,128)(2,1)S(1)}, bf16[128,1152]{1,0:T(8,128)(2,1)S(1)}, u32[]{:S(2)}, u32[]{:S(2)}) collective-permute-start(bf16[128,1152]{1,0:T(8,128)(2,1)S(1)} %collective-permute-done.4), channel_id=1, source_target_pairs={{0,112},{1,113},{2,114},{3,115},{4,116},{5,117},{6,118},{7,119},{8... | collective-permute-start | bytes 884744 | tf_op jit(solution)/shard_map/ppermute | solution.py:52
  24.9 2.8 %collective-permute-start.11 = (bf16[128,1152]{1,0:T(8,128)(2,1)S(1)}, bf16[128,1152]{1,0:T(8,128)(2,1)S(1)}, u32[]{:S(2)}, u32[]{:S(2)}) collective-permute-start(bf16[128,1152]{1,0:T(8,128)(2,1)S(1)} %slice.93), channel_id=1, source_target_pairs={{0,3},{1,2},{2,1},{3,0},{4,7},{5,6},{6,5},{7,4},{8,9},{9,8},{10,11... | collective-permute-start | bytes 884744 | tf_op jit(solution)/shard_map/ppermute | solution.py:52
  27.9 1.8 %collective-permute-start.10 = (bf16[128,1152]{1,0:T(8,128)(2,1)S(1)}, bf16[128,1152]{1,0:T(8,128)(2,1)S(1)}, u32[]{:S(2)}, u32[]{:S(2)}) collective-permute-start(bf16[128,1152]{1,0:T(8,128)(2,1)S(1)} %slice.92), channel_id=1, source_target_pairs={{0,132},{1,133},{2,134},{3,135},{4,128},{5,129},{6,130},{7,131},{8... | collective-permute-start | bytes 884744 | tf_op jit(solution)/shard_map/ppermute | solution.py:52
  30.3 1.0 %shard_map.70.w_axy = bf16[512,512]{1,0:T(8,128)(2,1)S(1)} custom-call(f32[8,128]{1,0:T(8,128)S(1)} %concatenate.12.coefficients, bf16[256,1152]{1,0:T(8,128)(2,1)S(1)} %pad_maximum_fusion.refs_0_.refs_3_, bf16[256,1152]{1,0:T(8,128)(2,1)S(1)} %collective-permute-done.7.refs_1_.refs_4_, bf16[256,1152]{1,0:T(8,128)(2,1)S(1)} %collective-permute-done.8.refs_2_.part_x.refs_1_, ...), custom_call_target="tpu_custom_call" | custom-call | tf_op jit(solution)/shard_map/pallas_call | solution.py:188
  31.3 1.2 %shard_map.71.part = f32[512,1152]{1,0:T(8,128)S(1)} custom-call(bf16[512,256]{1,0:T(8,128)(2,1)S(1)} %shard_map.69.w_aq.refs_0_, bf16[512,512]{1,0:T(8,128)(2,1)S(1)} %shard_map.70.w_axy, bf16[256,1152]{1,0:T(8,128)(2,1)S(1)} %shard_map.68.refs_2_.quad.refs_1_.refs_0_, bf16[256,1152]{1,0:T(8,128)(2,1)S(1)} %collective-permute-done.8.refs_2_.part_x.refs_1_, ...), custom_call_target="tpu_custom_call" | custom-call | tf_op jit(solution)/shard_map/pallas_call | solution.py:188
  32.5 3.0 %collective-permute-done.5 = bf16[128,1152]{1,0:T(8,128)(2,1)S(1)} collective-permute-done((bf16[128,1152]{1,0:T(8,128)(2,1)S(1)}, bf16[128,1152]{1,0:T(8,128)(2,1)S(1)}, u32[]{:S(2)}, u32[]{:S(2)}) %collective-permute-start.5) | collective-permute-done | bytes 294944 | tf_op jit(solution)/shard_map/ppermute | solution.py:52
  35.9 1.0 %shard_map.72.weights = bf16[256,1024]{1,0:T(8,128)(2,1)S(1)} custom-call(f32[8,128]{1,0:T(8,128)S(1)} %concatenate.12.coefficients, bf16[256,1152]{1,0:T(8,128)(2,1)S(1)} %constant_dynamic-update-slice_fusion.refs_0_.refs_5_, bf16[256,1152]{1,0:T(8,128)(2,1)S(1)} %shard_map.68.refs_2_.quad.refs_1_.refs_0_, ...), custom_call_target="tpu_custom_call" | custom-call | flops 603979776 | tf_op jit(solution)/shard_map/pallas_call | solution.py:188
  37.8 1.6 %shard_map.75 = (bf16[256,1024]{1,0:T(8,128)(2,1)S(1)}, bf16[256,1152]{1,0:T(8,128)(2,1)S(1)}) custom-call(f32[8,128]{1,0:T(8,128)S(1)} %concatenate.12.coefficients, bf16[256,1152]{1,0:T(8,128)(2,1)S(1)} %collective-permute-done.12.sib_c.refs_6_, bf16[256,1152]{1,0:T(8,128)(2,1)S(1)} %shard_map.68.refs_2_.quad.refs_1_.refs_0_, ...), custom_call_target="tpu_custom_call" | custom-call | flops 1207959552 | tf_op jit(solution)/shard_map/pallas_call | solution.py:188
  41.5 4.0 %collective-permute-start.17 = (bf16[256,1152]{1,0:T(8,128)(2,1)S(1)}, bf16[256,1152]{1,0:T(8,128)(2,1)S(1)}, u32[]{:S(2)}, u32[]{:S(2)}) collective-permute-start(bf16[256,1152]{1,0:T(8,128)(2,1)S(1)} %shard_map.76), channel_id=1, source_target_pairs={{0,135},{1,134},{2,133},{3,132},{4,131},{5,130},{6,129},{7,128},{8... | collective-permute-start | bytes 1769480 | tf_op jit(solution)/shard_map/ppermute | solution.py:52
  46.2 1.3 %collective-permute-start.15 = (bf16[128,1152]{1,0:T(8,128)(2,1)S(1)}, bf16[128,1152]{1,0:T(8,128)(2,1)S(1)}, u32[]{:S(2)}, u32[]{:S(2)}) collective-permute-start(bf16[128,1152]{1,0:T(8,128)(2,1)S(1)} %get-tuple-element.51), channel_id=1, source_target_pairs={{0,112},{1,113},{2,114},{3,115},{4,116},{5,117},{6,118},{7,119},{8... | collective-permute-start | bytes 884744 | tf_op jit(solution)/shard_map/ppermute | solution.py:52
  48.4 1.7 %collective-permute-start.18 = (bf16[256,1152]{1,0:T(8,128)(2,1)S(1)}, bf16[256,1152]{1,0:T(8,128)(2,1)S(1)}, u32[]{:S(2)}, u32[]{:S(2)}) collective-permute-start(bf16[256,1152]{1,0:T(8,128)(2,1)S(1)} %shard_map.79), channel_id=1, source_target_pairs={{0,3},{1,2},{2,1},{3,0},{4,7},{5,6},{6,5},{7,4},{8,9},{9,8},{10,11... | collective-permute-start | bytes 1769480 | tf_op jit(solution)/shard_map/ppermute | solution.py:52
  51.0 1.3 %collective-permute-start.19 = (bf16[256,1152]{1,0:T(8,128)(2,1)S(1)}, bf16[256,1152]{1,0:T(8,128)(2,1)S(1)}, u32[]{:S(2)}, u32[]{:S(2)}) collective-permute-start(bf16[256,1152]{1,0:T(8,128)(2,1)S(1)} %shard_map.80), channel_id=1, source_target_pairs={{0,132},{1,133},{2,134},{3,135},{4,128},{5,129},{6,130},{7,131},{8... | collective-permute-start | bytes 1769480 | tf_op jit(solution)/shard_map/ppermute | solution.py:52
  52.4 7.5 %collective-permute-done.15 = bf16[128,1152]{1,0:T(8,128)(2,1)S(1)} collective-permute-done((bf16[128,1152]{1,0:T(8,128)(2,1)S(1)}, bf16[128,1152]{1,0:T(8,128)(2,1)S(1)}, u32[]{:S(2)}, u32[]{:S(2)}) %collective-permute-start.15) | collective-permute-done | bytes 294944 | tf_op jit(solution)/shard_map/ppermute | solution.py:52
  61.3 3.2 %collective-permute-start.22 = (bf16[64,1152]{1,0:T(8,128)(2,1)S(1)}, bf16[64,1152]{1,0:T(8,128)(2,1)S(1)}, u32[]{:S(2)}, u32[]{:S(2)}) collective-permute-start(bf16[64,1152]{1,0:T(8,128)(2,1)S(1)} %get-tuple-element.48), channel_id=1, source_target_pairs={{0,5},{1,4},{2,7},{3,6},{4,1},{5,0},{6,3},{7,2},{8,143},{9,142},{1... | collective-permute-start | bytes 442376 | tf_op jit(solution)/shard_map/ppermute | solution.py:52
  64.6 3.0 %collective-permute-start.21 = (bf16[64,1152]{1,0:T(8,128)(2,1)S(1)}, bf16[64,1152]{1,0:T(8,128)(2,1)S(1)}, u32[]{:S(2)}, u32[]{:S(2)}) collective-permute-start(bf16[64,1152]{1,0:T(8,128)(2,1)S(1)} %get-tuple-element.49), channel_id=1, source_target_pairs={{0,1},{1,0},{2,3},{3,2},{4,5},{5,4},{6,7},{7,6},{8,11},{9,10},{10,... | collective-permute-start | bytes 442376 | tf_op jit(solution)/shard_map/ppermute | solution.py:52
  68.7 3.6 %collective-permute-done.21.rest_1_ = bf16[64,1152]{1,0:T(8,128)(2,1)S(1)} collective-permute-done((bf16[64,1152]{1,0:T(8,128)(2,1)S(1)}, bf16[64,1152]{1,0:T(8,128)(2,1)S(1)}, u32[]{:S(2)}, u32[]{:S(2)}) %collective-permute-start.21) | collective-permute-done | bytes 147488 | tf_op jit(solution)/shard_map/ppermute | solution.py:52
  72.7 1.0 %shard_map.81 = f32[64,1152]{1,0:T(8,128)} custom-call(f32[8,128]{1,0:T(8,128)S(1)} %concatenate.12.coefficients, bf16[64,1152]{1,0:T(8,128)(2,1)S(1)} %copy-done.1, bf16[64,1152]{1,0:T(8,128)(2,1)S(1)} %copy-done.3, f32[64,1152]{1,0:T(8,128)S(1)} %slice.101.sums, bf16[64,1152]{1,0:T(8,128)(2,1)S(1)} %collective-permute-done.20.rest_0_, ...), custom_call_target="tpu_custom_call" | custom-call | tf_op jit(solution)/shard_map/pallas_call | solution.py:110
  (73 shorter events, 15.5 us)
Async XLA Ops:
  0.6 12.8 %collective-permute-start = (bf16[64,1152]{1,0:T(8,128)(2,1)}, bf16[64,1152]{1,0:T(8,128)(2,1)S(1)}, u32[]{:S(2)}, u32[]{:S(2)}) collective-permute-start(bf16[64,1152]{1,0:T(8,128)(2,1)} %rows.7), channel_id=1, source_target_pairs={{0,112},{1,113},{2,114},{3,115},{4,116},{5,117},{6,118},{7,119},{8... | collective-permute-start | bytes 442376 | tf_op jit(solution)/shard_map/ppermute | solution.py:52
  6.6 6.9 %collective-permute-start.3 = (bf16[64,1152]{1,0:T(8,128)(2,1)}, bf16[64,1152]{1,0:T(8,128)(2,1)S(1)}, u32[]{:S(2)}, u32[]{:S(2)}) collective-permute-start(bf16[64,1152]{1,0:T(8,128)(2,1)} %others.3), channel_id=1, source_target_pairs={{0,5},{1,4},{2,7},{3,6},{4,1},{5,0},{6,3},{7,2},{8,143},{9,142},{1... | collective-permute-start | bytes 442376 | tf_op jit(solution)/shard_map/ppermute | solution.py:52
  7.9 5.5 %collective-permute-start.2 = (bf16[64,1152]{1,0:T(8,128)(2,1)}, bf16[64,1152]{1,0:T(8,128)(2,1)S(1)}, u32[]{:S(2)}, u32[]{:S(2)}) collective-permute-start(bf16[64,1152]{1,0:T(8,128)(2,1)} %others.3), channel_id=1, source_target_pairs={{0,1},{1,0},{2,3},{3,2},{4,5},{5,4},{6,7},{7,6},{8,11},{9,10},{10,... | collective-permute-start | bytes 442376 | tf_op jit(solution)/shard_map/ppermute | solution.py:52
  8.5 5.9 %collective-permute-start.1 = (bf16[64,1152]{1,0:T(8,128)(2,1)}, bf16[64,1152]{1,0:T(8,128)(2,1)S(1)}, u32[]{:S(2)}, u32[]{:S(2)}) collective-permute-start(bf16[64,1152]{1,0:T(8,128)(2,1)} %others.3), channel_id=1, source_target_pairs={{0,4},{1,5},{2,6},{3,7},{4,0},{5,1},{6,2},{7,3},{8,140},{9,141},{1... | collective-permute-start | bytes 442376 | tf_op jit(solution)/shard_map/ppermute | solution.py:52
  14.6 6.8 %collective-permute-start.4 = (bf16[128,1152]{1,0:T(8,128)(2,1)S(1)}, bf16[128,1152]{1,0:T(8,128)(2,1)S(1)}, u32[]{:S(2)}, u32[]{:S(2)}) collective-permute-start(bf16[128,1152]{1,0:T(8,128)(2,1)S(1)} %shard_map.67), channel_id=1, source_target_pairs={{0,16},{1,17},{2,18},{3,19},{4,20},{5,21},{6,22},{7,23},{8,120},{9... | collective-permute-start | bytes 884744 | tf_op jit(solution)/shard_map/ppermute | solution.py:52
  14.9 10.0 %collective-permute-start.9 = (bf16[256,1152]{1,0:T(8,128)(2,1)S(1)}, bf16[256,1152]{1,0:T(8,128)(2,1)S(1)}, u32[]{:S(2)}, u32[]{:S(2)}) collective-permute-start(bf16[256,1152]{1,0:T(8,128)(2,1)S(1)} %shard_map.68.refs_2_.quad.refs_1_.refs_0_), channel_id=1, source_target_pairs={{0,132},{1,133},{2,134},{3,135},{4,128},{5,129},{6,130},{7,131},{8... | collective-permute-start | bytes 1769480 | tf_op jit(solution)/shard_map/ppermute | solution.py:52
  16.8 11.1 %collective-permute-start.8 = (bf16[256,1152]{1,0:T(8,128)(2,1)S(1)}, bf16[256,1152]{1,0:T(8,128)(2,1)S(1)}, u32[]{:S(2)}, u32[]{:S(2)}) collective-permute-start(bf16[256,1152]{1,0:T(8,128)(2,1)S(1)} %shard_map.68.refs_2_.quad.refs_1_.refs_0_), channel_id=1, source_target_pairs={{0,3},{1,2},{2,1},{3,0},{4,7},{5,6},{6,5},{7,4},{8,9},{9,8},{10,11... | collective-permute-start | bytes 1769480 | tf_op jit(solution)/shard_map/ppermute | solution.py:52
  21.5 8.2 %collective-permute-start.7 = (bf16[256,1152]{1,0:T(8,128)(2,1)S(1)}, bf16[256,1152]{1,0:T(8,128)(2,1)S(1)}, u32[]{:S(2)}, u32[]{:S(2)}) collective-permute-start(bf16[256,1152]{1,0:T(8,128)(2,1)S(1)} %pad_maximum_fusion.refs_0_.refs_3_), channel_id=1, source_target_pairs={{0,8},{1,9},{2,10},{3,11},{4,12},{5,13},{6,14},{7,15},{8,0},{9,1},... | collective-permute-start | bytes 1769480 | tf_op jit(solution)/shard_map/ppermute | solution.py:52
  21.6 10.9 %collective-permute-start.6 = (bf16[128,1152]{1,0:T(8,128)(2,1)S(1)}, bf16[128,1152]{1,0:T(8,128)(2,1)S(1)}, u32[]{:S(2)}, u32[]{:S(2)}) collective-permute-start(bf16[128,1152]{1,0:T(8,128)(2,1)S(1)} %collective-permute-done.4), channel_id=1, source_target_pairs={{0,96},{1,97},{2,98},{3,99},{4,100},{5,101},{6,102},{7,103},{8,40}... | collective-permute-start | bytes 884744 | tf_op jit(solution)/shard_map/ppermute | solution.py:52
  23.1 12.4 %collective-permute-start.5 = (bf16[128,1152]{1,0:T(8,128)(2,1)S(1)}, bf16[128,1152]{1,0:T(8,128)(2,1)S(1)}, u32[]{:S(2)}, u32[]{:S(2)}) collective-permute-start(bf16[128,1152]{1,0:T(8,128)(2,1)S(1)} %collective-permute-done.4), channel_id=1, source_target_pairs={{0,112},{1,113},{2,114},{3,115},{4,116},{5,117},{6,118},{7,119},{8... | collective-permute-start | bytes 884744 | tf_op jit(solution)/shard_map/ppermute | solution.py:52
  24.9 11.0 %collective-permute-start.11 = (bf16[128,1152]{1,0:T(8,128)(2,1)S(1)}, bf16[128,1152]{1,0:T(8,128)(2,1)S(1)}, u32[]{:S(2)}, u32[]{:S(2)}) collective-permute-start(bf16[128,1152]{1,0:T(8,128)(2,1)S(1)} %slice.93), channel_id=1, source_target_pairs={{0,3},{1,2},{2,1},{3,0},{4,7},{5,6},{6,5},{7,4},{8,9},{9,8},{10,11... | collective-permute-start | bytes 884744 | tf_op jit(solution)/shard_map/ppermute | solution.py:52
  27.9 7.9 %collective-permute-start.10 = (bf16[128,1152]{1,0:T(8,128)(2,1)S(1)}, bf16[128,1152]{1,0:T(8,128)(2,1)S(1)}, u32[]{:S(2)}, u32[]{:S(2)}) collective-permute-start(bf16[128,1152]{1,0:T(8,128)(2,1)S(1)} %slice.92), channel_id=1, source_target_pairs={{0,132},{1,133},{2,134},{3,135},{4,128},{5,129},{6,130},{7,131},{8... | collective-permute-start | bytes 884744 | tf_op jit(solution)/shard_map/ppermute | solution.py:52
  39.4 6.0 %collective-permute-start.13 = (bf16[256,1152]{1,0:T(8,128)(2,1)S(1)}, bf16[256,1152]{1,0:T(8,128)(2,1)S(1)}, u32[]{:S(2)}, u32[]{:S(2)}) collective-permute-start(bf16[256,1152]{1,0:T(8,128)(2,1)S(1)} %get-tuple-element.38), channel_id=1, source_target_pairs={{0,8},{1,9},{2,10},{3,11},{4,12},{5,13},{6,14},{7,15},{8,0},{9,1},... | collective-permute-start | bytes 1769480 | tf_op jit(solution)/shard_map/ppermute | solution.py:52
  41.5 19.5 %collective-permute-start.17 = (bf16[256,1152]{1,0:T(8,128)(2,1)S(1)}, bf16[256,1152]{1,0:T(8,128)(2,1)S(1)}, u32[]{:S(2)}, u32[]{:S(2)}) collective-permute-start(bf16[256,1152]{1,0:T(8,128)(2,1)S(1)} %shard_map.76), channel_id=1, source_target_pairs={{0,135},{1,134},{2,133},{3,132},{4,131},{5,130},{6,129},{7,128},{8... | collective-permute-start | bytes 1769480 | tf_op jit(solution)/shard_map/ppermute | solution.py:52
  46.1 4.9 %collective-permute-start.14 = (bf16[256,1152]{1,0:T(8,128)(2,1)S(1)}, bf16[256,1152]{1,0:T(8,128)(2,1)S(1)}, u32[]{:S(2)}, u32[]{:S(2)}) collective-permute-start(bf16[256,1152]{1,0:T(8,128)(2,1)S(1)} %get-tuple-element.41), channel_id=1, source_target_pairs={{0,8},{1,9},{2,10},{3,11},{4,12},{5,13},{6,14},{7,15},{8,0},{9,1},... | collective-permute-start | bytes 1769480 | tf_op jit(solution)/shard_map/ppermute | solution.py:52
  46.2 13.7 %collective-permute-start.15 = (bf16[128,1152]{1,0:T(8,128)(2,1)S(1)}, bf16[128,1152]{1,0:T(8,128)(2,1)S(1)}, u32[]{:S(2)}, u32[]{:S(2)}) collective-permute-start(bf16[128,1152]{1,0:T(8,128)(2,1)S(1)} %get-tuple-element.51), channel_id=1, source_target_pairs={{0,112},{1,113},{2,114},{3,115},{4,116},{5,117},{6,118},{7,119},{8... | collective-permute-start | bytes 884744 | tf_op jit(solution)/shard_map/ppermute | solution.py:52
  47.5 12.4 %collective-permute-start.16 = (bf16[128,1152]{1,0:T(8,128)(2,1)S(1)}, bf16[128,1152]{1,0:T(8,128)(2,1)S(1)}, u32[]{:S(2)}, u32[]{:S(2)}) collective-permute-start(bf16[128,1152]{1,0:T(8,128)(2,1)S(1)} %get-tuple-element.52), channel_id=1, source_target_pairs={{0,32},{1,33},{2,34},{3,35},{4,36},{5,37},{6,38},{7,39},{8,104},{9... | collective-permute-start | bytes 884744 | tf_op jit(solution)/shard_map/ppermute | solution.py:52
  48.4 12.6 %collective-permute-start.18 = (bf16[256,1152]{1,0:T(8,128)(2,1)S(1)}, bf16[256,1152]{1,0:T(8,128)(2,1)S(1)}, u32[]{:S(2)}, u32[]{:S(2)}) collective-permute-start(bf16[256,1152]{1,0:T(8,128)(2,1)S(1)} %shard_map.79), channel_id=1, source_target_pairs={{0,3},{1,2},{2,1},{3,0},{4,7},{5,6},{6,5},{7,4},{8,9},{9,8},{10,11... | collective-permute-start | bytes 1769480 | tf_op jit(solution)/shard_map/ppermute | solution.py:52
  51.0 10.0 %collective-permute-start.19 = (bf16[256,1152]{1,0:T(8,128)(2,1)S(1)}, bf16[256,1152]{1,0:T(8,128)(2,1)S(1)}, u32[]{:S(2)}, u32[]{:S(2)}) collective-permute-start(bf16[256,1152]{1,0:T(8,128)(2,1)S(1)} %shard_map.80), channel_id=1, source_target_pairs={{0,132},{1,133},{2,134},{3,135},{4,128},{5,129},{6,130},{7,131},{8... | collective-permute-start | bytes 1769480 | tf_op jit(solution)/shard_map/ppermute | solution.py:52
  60.0 7.6 %collective-permute-start.23 = (bf16[128,1152]{1,0:T(8,128)(2,1)S(1)}, bf16[128,1152]{1,0:T(8,128)(2,1)S(1)}, u32[]{:S(2)}, u32[]{:S(2)}) collective-permute-start(bf16[128,1152]{1,0:T(8,128)(2,1)S(1)} %fusion), channel_id=1, source_target_pairs={{0,16},{1,17},{2,18},{3,19},{4,20},{5,21},{6,22},{7,23},{8,120},{9... | collective-permute-start | bytes 884744 | tf_op jit(solution)/shard_map/ppermute | solution.py:52
  61.3 7.3 %collective-permute-start.22 = (bf16[64,1152]{1,0:T(8,128)(2,1)S(1)}, bf16[64,1152]{1,0:T(8,128)(2,1)S(1)}, u32[]{:S(2)}, u32[]{:S(2)}) collective-permute-start(bf16[64,1152]{1,0:T(8,128)(2,1)S(1)} %get-tuple-element.48), channel_id=1, source_target_pairs={{0,5},{1,4},{2,7},{3,6},{4,1},{5,0},{6,3},{7,2},{8,143},{9,142},{1... | collective-permute-start | bytes 442376 | tf_op jit(solution)/shard_map/ppermute | solution.py:52
  64.6 7.7 %collective-permute-start.21 = (bf16[64,1152]{1,0:T(8,128)(2,1)S(1)}, bf16[64,1152]{1,0:T(8,128)(2,1)S(1)}, u32[]{:S(2)}, u32[]{:S(2)}) collective-permute-start(bf16[64,1152]{1,0:T(8,128)(2,1)S(1)} %get-tuple-element.49), channel_id=1, source_target_pairs={{0,1},{1,0},{2,3},{3,2},{4,5},{5,4},{6,7},{7,6},{8,11},{9,10},{10,... | collective-permute-start | bytes 442376 | tf_op jit(solution)/shard_map/ppermute | solution.py:52
  67.6 5.1 %collective-permute-start.20 = (bf16[64,1152]{1,0:T(8,128)(2,1)S(1)}, bf16[64,1152]{1,0:T(8,128)(2,1)S(1)}, u32[]{:S(2)}, u32[]{:S(2)}) collective-permute-start(bf16[64,1152]{1,0:T(8,128)(2,1)S(1)} %get-tuple-element.50), channel_id=1, source_target_pairs={{0,4},{1,5},{2,6},{3,7},{4,0},{5,1},{6,2},{7,3},{8,140},{9,141},{1... | collective-permute-start | bytes 442376 | tf_op jit(solution)/shard_map/ppermute | solution.py:52
  67.7 6.4 %collective-permute-start.24 = (bf16[64,1152]{1,0:T(8,128)(2,1)S(1)}, bf16[64,1152]{1,0:T(8,128)(2,1)S(1)}, u32[]{:S(2)}, u32[]{:S(2)}) collective-permute-start(bf16[64,1152]{1,0:T(8,128)(2,1)S(1)} %slice.113), channel_id=1, source_target_pairs={{0,112},{1,113},{2,114},{3,115},{4,116},{5,117},{6,118},{7,119},{8... | collective-permute-start | bytes 442376 | tf_op jit(solution)/shard_map/ppermute | solution.py:52
  (5 other events, 14.4 us)

commit v8 on v6

--- a/solution.py
+++ b/solution.py
@@ -260,7 +260,7 @@
 
     send_d = image_part(bf16, w_ad, *late(3))
     back_d = d2(send_d)
-    s4 = rounded(after(sums_own_c, send_d) + widened(back_c))
+    s4 = rounded(sums_own_c + widened(back_c))
     send_x = image_part(bf16, w_axy[:, :q], *late(1, s4))
     send_y = image_part(bf16, w_axy[:, q:], *late(2, s4))
     back_x, back_y = x2(send_x), y2(send_y)

time: 75.4 us -> 75.4 us (level)
  no operation moved by 1% of the time
where the time goes in v8:
time: 75.4 us; the launch traced here: 75.1 us
  starting transfers between devices  38 us (50%)
  waiting for transfers between devices  18.6 us (25%)
  Pallas kernels  13.3 us (18%)
  between operations  2.28 us (3%)
  local copies, waits for them, and re-layouts  2.25 us (3%)
    ppermute x25, starting transfers between devices, permute(): return lambda value: lax.ppermute(value, AXES, pairs)  38 us
    ppermute x25, waiting for transfers between devices, permute(): return lambda value: lax.ppermute(value, AXES, pairs)  18.6 us
    pallas_call x16, Pallas kernels, on_device(): pl.pallas_call(kernel, out_shape=[jax.ShapeDtypeStruct(shape, kind) for s...  11.3 us
    pallas_call x2, Pallas kernels, grad_rows(): pl.pallas_call(grad_kernel, out_shape=jax.ShapeDtypeStruct(rows.shape, jn...  2.03 us
    unnamed x9, local copies, waits for them, and re-layouts  1.85 us
  transfers between devices with their start and end apart: 25, of which 10 were waited for; matrix products, arithmetic and copies ran while one was open for 1% of the time, Pallas kernels for 14%

profile of v8, /device:TPU:8, one launch (start us, length us, event | category | flops | bytes accessed | tf_op | source)
XLA Modules:
  0.0 75.1 jit_solution(15200846818346977592)
XLA Ops:
  0.6 5.9 %collective-permute-start = (bf16[64,1152]{1,0:T(8,128)(2,1)}, bf16[64,1152]{1,0:T(8,128)(2,1)S(1)}, u32[]{:S(2)}, u32[]{:S(2)}) collective-permute-start(bf16[64,1152]{1,0:T(8,128)(2,1)} %rows.7), channel_id=1, source_target_pairs={{0,112},{1,113},{2,114},{3,115},{4,116},{5,117},{6,118},{7,119},{8... | collective-permute-start | bytes 442376 | tf_op jit(solution)/shard_map/ppermute | solution.py:52
  6.6 1.4 %collective-permute-start.3 = (bf16[64,1152]{1,0:T(8,128)(2,1)}, bf16[64,1152]{1,0:T(8,128)(2,1)S(1)}, u32[]{:S(2)}, u32[]{:S(2)}) collective-permute-start(bf16[64,1152]{1,0:T(8,128)(2,1)} %others.3), channel_id=1, source_target_pairs={{0,5},{1,4},{2,7},{3,6},{4,1},{5,0},{6,3},{7,2},{8,143},{9,142},{1... | collective-permute-start | bytes 442376 | tf_op jit(solution)/shard_map/ppermute | solution.py:52
  8.5 1.6 %collective-permute-start.1 = (bf16[64,1152]{1,0:T(8,128)(2,1)}, bf16[64,1152]{1,0:T(8,128)(2,1)S(1)}, u32[]{:S(2)}, u32[]{:S(2)}) collective-permute-start(bf16[64,1152]{1,0:T(8,128)(2,1)} %others.3), channel_id=1, source_target_pairs={{0,4},{1,5},{2,6},{3,7},{4,0},{5,1},{6,2},{7,3},{8,140},{9,141},{1... | collective-permute-start | bytes 442376 | tf_op jit(solution)/shard_map/ppermute | solution.py:52
  14.9 1.9 %collective-permute-start.9 = (bf16[256,1152]{1,0:T(8,128)(2,1)S(1)}, bf16[256,1152]{1,0:T(8,128)(2,1)S(1)}, u32[]{:S(2)}, u32[]{:S(2)}) collective-permute-start(bf16[256,1152]{1,0:T(8,128)(2,1)S(1)} %shard_map.68.refs_2_.quad.refs_1_.refs_0_), channel_id=1, source_target_pairs={{0,132},{1,133},{2,134},{3,135},{4,128},{5,129},{6,130},{7,131},{8... | collective-permute-start | bytes 1769480 | tf_op jit(solution)/shard_map/ppermute | solution.py:52
  16.8 2.8 %collective-permute-start.8 = (bf16[256,1152]{1,0:T(8,128)(2,1)S(1)}, bf16[256,1152]{1,0:T(8,128)(2,1)S(1)}, u32[]{:S(2)}, u32[]{:S(2)}) collective-permute-start(bf16[256,1152]{1,0:T(8,128)(2,1)S(1)} %shard_map.68.refs_2_.quad.refs_1_.refs_0_), channel_id=1, source_target_pairs={{0,3},{1,2},{2,1},{3,0},{4,7},{5,6},{6,5},{7,4},{8,9},{9,8},{10,11... | collective-permute-start | bytes 1769480 | tf_op jit(solution)/shard_map/ppermute | solution.py:52
  19.6 1.8 %collective-permute-done.4 = bf16[128,1152]{1,0:T(8,128)(2,1)S(1)} collective-permute-done((bf16[128,1152]{1,0:T(8,128)(2,1)S(1)}, bf16[128,1152]{1,0:T(8,128)(2,1)S(1)}, u32[]{:S(2)}, u32[]{:S(2)}) %collective-permute-start.4) | collective-permute-done | bytes 294944 | tf_op jit(solution)/shard_map/ppermute | solution.py:52
  21.6 1.5 %collective-permute-start.6 = (bf16[128,1152]{1,0:T(8,128)(2,1)S(1)}, bf16[128,1152]{1,0:T(8,128)(2,1)S(1)}, u32[]{:S(2)}, u32[]{:S(2)}) collective-permute-start(bf16[128,1152]{1,0:T(8,128)(2,1)S(1)} %collective-permute-done.4), channel_id=1, source_target_pairs={{0,96},{1,97},{2,98},{3,99},{4,100},{5,101},{6,102},{7,103},{8,40}... | collective-permute-start | bytes 884744 | tf_op jit(solution)/shard_map/ppermute | solution.py:52
  23.1 1.4 %collective-permute-start.5 = (bf16[128,1152]{1,0:T(8,128)(2,1)S(1)}, bf16[128,1152]{1,0:T(8,128)(2,1)S(1)}, u32[]{:S(2)}, u32[]{:S(2)}) collective-permute-start(bf16[128,1152]{1,0:T(8,128)(2,1)S(1)} %collective-permute-done.4), channel_id=1, source_target_pairs={{0,112},{1,113},{2,114},{3,115},{4,116},{5,117},{6,118},{7,119},{8... | collective-permute-start | bytes 884744 | tf_op jit(solution)/shard_map/ppermute | solution.py:52
  24.9 2.8 %collective-permute-start.11 = (bf16[128,1152]{1,0:T(8,128)(2,1)S(1)}, bf16[128,1152]{1,0:T(8,128)(2,1)S(1)}, u32[]{:S(2)}, u32[]{:S(2)}) collective-permute-start(bf16[128,1152]{1,0:T(8,128)(2,1)S(1)} %slice.93), channel_id=1, source_target_pairs={{0,3},{1,2},{2,1},{3,0},{4,7},{5,6},{6,5},{7,4},{8,9},{9,8},{10,11... | collective-permute-start | bytes 884744 | tf_op jit(solution)/shard_map/ppermute | solution.py:52
  27.9 1.8 %collective-permute-start.10 = (bf16[128,1152]{1,0:T(8,128)(2,1)S(1)}, bf16[128,1152]{1,0:T(8,128)(2,1)S(1)}, u32[]{:S(2)}, u32[]{:S(2)}) collective-permute-start(bf16[128,1152]{1,0:T(8,128)(2,1)S(1)} %slice.92), channel_id=1, source_target_pairs={{0,132},{1,133},{2,134},{3,135},{4,128},{5,129},{6,130},{7,131},{8... | collective-permute-start | bytes 884744 | tf_op jit(solution)/shard_map/ppermute | solution.py:52
  30.3 1.0 %shard_map.70.w_axy = bf16[512,512]{1,0:T(8,128)(2,1)S(1)} custom-call(f32[8,128]{1,0:T(8,128)S(1)} %concatenate.12.coefficients, bf16[256,1152]{1,0:T(8,128)(2,1)S(1)} %pad_maximum_fusion.refs_0_.refs_3_, bf16[256,1152]{1,0:T(8,128)(2,1)S(1)} %collective-permute-done.7.refs_1_.refs_4_, bf16[256,1152]{1,0:T(8,128)(2,1)S(1)} %collective-permute-done.8.refs_2_.part_x.refs_1_, ...), custom_call_target="tpu_custom_call" | custom-call | tf_op jit(solution)/shard_map/pallas_call | solution.py:179
  31.3 1.2 %shard_map.71.part = f32[512,1152]{1,0:T(8,128)S(1)} custom-call(bf16[512,256]{1,0:T(8,128)(2,1)S(1)} %shard_map.69.w_aq.refs_0_, bf16[512,512]{1,0:T(8,128)(2,1)S(1)} %shard_map.70.w_axy, bf16[256,1152]{1,0:T(8,128)(2,1)S(1)} %shard_map.68.refs_2_.quad.refs_1_.refs_0_, bf16[256,1152]{1,0:T(8,128)(2,1)S(1)} %collective-permute-done.8.refs_2_.part_x.refs_1_, ...), custom_call_target="tpu_custom_call" | custom-call | tf_op jit(solution)/shard_map/pallas_call | solution.py:179
  32.5 3.0 %collective-permute-done.5 = bf16[128,1152]{1,0:T(8,128)(2,1)S(1)} collective-permute-done((bf16[128,1152]{1,0:T(8,128)(2,1)S(1)}, bf16[128,1152]{1,0:T(8,128)(2,1)S(1)}, u32[]{:S(2)}, u32[]{:S(2)}) %collective-permute-start.5) | collective-permute-done | bytes 294944 | tf_op jit(solution)/shard_map/ppermute | solution.py:52
  37.8 1.6 %shard_map.75 = (bf16[256,1024]{1,0:T(8,128)(2,1)S(1)}, bf16[256,1152]{1,0:T(8,128)(2,1)S(1)}) custom-call(f32[8,128]{1,0:T(8,128)S(1)} %concatenate.12.coefficients, bf16[256,1152]{1,0:T(8,128)(2,1)S(1)} %collective-permute-done.12.sib_c.refs_6_, bf16[256,1152]{1,0:T(8,128)(2,1)S(1)} %shard_map.68.refs_2_.quad.refs_1_.refs_0_, ...), custom_call_target="tpu_custom_call" | custom-call | flops 1207959552 | tf_op jit(solution)/shard_map/pallas_call | solution.py:179
  41.5 4.0 %collective-permute-start.17 = (bf16[256,1152]{1,0:T(8,128)(2,1)S(1)}, bf16[256,1152]{1,0:T(8,128)(2,1)S(1)}, u32[]{:S(2)}, u32[]{:S(2)}) collective-permute-start(bf16[256,1152]{1,0:T(8,128)(2,1)S(1)} %shard_map.78), channel_id=1, source_target_pairs={{0,135},{1,134},{2,133},{3,132},{4,131},{5,130},{6,129},{7,128},{8... | collective-permute-start | bytes 1769480 | tf_op jit(solution)/shard_map/ppermute | solution.py:52
  46.2 1.3 %collective-permute-start.15 = (bf16[128,1152]{1,0:T(8,128)(2,1)S(1)}, bf16[128,1152]{1,0:T(8,128)(2,1)S(1)}, u32[]{:S(2)}, u32[]{:S(2)}) collective-permute-start(bf16[128,1152]{1,0:T(8,128)(2,1)S(1)} %get-tuple-element.49), channel_id=1, source_target_pairs={{0,112},{1,113},{2,114},{3,115},{4,116},{5,117},{6,118},{7,119},{8... | collective-permute-start | bytes 884744 | tf_op jit(solution)/shard_map/ppermute | solution.py:52
  48.4 1.7 %collective-permute-start.18 = (bf16[256,1152]{1,0:T(8,128)(2,1)S(1)}, bf16[256,1152]{1,0:T(8,128)(2,1)S(1)}, u32[]{:S(2)}, u32[]{:S(2)}) collective-permute-start(bf16[256,1152]{1,0:T(8,128)(2,1)S(1)} %shard_map.79), channel_id=1, source_target_pairs={{0,3},{1,2},{2,1},{3,0},{4,7},{5,6},{6,5},{7,4},{8,9},{9,8},{10,11... | collective-permute-start | bytes 1769480 | tf_op jit(solution)/shard_map/ppermute | solution.py:52
  51.0 1.3 %collective-permute-start.19 = (bf16[256,1152]{1,0:T(8,128)(2,1)S(1)}, bf16[256,1152]{1,0:T(8,128)(2,1)S(1)}, u32[]{:S(2)}, u32[]{:S(2)}) collective-permute-start(bf16[256,1152]{1,0:T(8,128)(2,1)S(1)} %shard_map.80), channel_id=1, source_target_pairs={{0,132},{1,133},{2,134},{3,135},{4,128},{5,129},{6,130},{7,131},{8... | collective-permute-start | bytes 1769480 | tf_op jit(solution)/shard_map/ppermute | solution.py:52
  52.4 7.5 %collective-permute-done.15 = bf16[128,1152]{1,0:T(8,128)(2,1)S(1)} collective-permute-done((bf16[128,1152]{1,0:T(8,128)(2,1)S(1)}, bf16[128,1152]{1,0:T(8,128)(2,1)S(1)}, u32[]{:S(2)}, u32[]{:S(2)}) %collective-permute-start.15) | collective-permute-done | bytes 294944 | tf_op jit(solution)/shard_map/ppermute | solution.py:52
  61.3 3.2 %collective-permute-start.22 = (bf16[64,1152]{1,0:T(8,128)(2,1)S(1)}, bf16[64,1152]{1,0:T(8,128)(2,1)S(1)}, u32[]{:S(2)}, u32[]{:S(2)}) collective-permute-start(bf16[64,1152]{1,0:T(8,128)(2,1)S(1)} %get-tuple-element.46), channel_id=1, source_target_pairs={{0,5},{1,4},{2,7},{3,6},{4,1},{5,0},{6,3},{7,2},{8,143},{9,142},{1... | collective-permute-start | bytes 442376 | tf_op jit(solution)/shard_map/ppermute | solution.py:52
  64.6 3.0 %collective-permute-start.21 = (bf16[64,1152]{1,0:T(8,128)(2,1)S(1)}, bf16[64,1152]{1,0:T(8,128)(2,1)S(1)}, u32[]{:S(2)}, u32[]{:S(2)}) collective-permute-start(bf16[64,1152]{1,0:T(8,128)(2,1)S(1)} %get-tuple-element.47), channel_id=1, source_target_pairs={{0,1},{1,0},{2,3},{3,2},{4,5},{5,4},{6,7},{7,6},{8,11},{9,10},{10,... | collective-permute-start | bytes 442376 | tf_op jit(solution)/shard_map/ppermute | solution.py:52
  68.7 3.6 %collective-permute-done.21.rest_1_ = bf16[64,1152]{1,0:T(8,128)(2,1)S(1)} collective-permute-done((bf16[64,1152]{1,0:T(8,128)(2,1)S(1)}, bf16[64,1152]{1,0:T(8,128)(2,1)S(1)}, u32[]{:S(2)}, u32[]{:S(2)}) %collective-permute-start.21) | collective-permute-done | bytes 147488 | tf_op jit(solution)/shard_map/ppermute | solution.py:52
  72.7 1.0 %shard_map.81 = f32[64,1152]{1,0:T(8,128)} custom-call(f32[8,128]{1,0:T(8,128)S(1)} %concatenate.12.coefficients, bf16[64,1152]{1,0:T(8,128)(2,1)S(1)} %copy-done.1, bf16[64,1152]{1,0:T(8,128)(2,1)S(1)} %copy-done.3, f32[64,1152]{1,0:T(8,128)S(1)} %slice.101.sums, bf16[64,1152]{1,0:T(8,128)(2,1)S(1)} %collective-permute-done.20.rest_0_, ...), custom_call_target="tpu_custom_call" | custom-call | tf_op jit(solution)/shard_map/pallas_call | solution.py:102
  74.1 1.0 %shard_map.82 = f32[64,1152]{1,0:T(8,128)} custom-call(f32[8,128]{1,0:T(8,128)S(1)} %concatenate.12.coefficients, bf16[64,1152]{1,0:T(8,128)(2,1)S(1)} %copy-done.3, bf16[64,1152]{1,0:T(8,128)(2,1)S(1)} %copy-done.1, f32[64,1152]{1,0:T(8,128)S(1)} %slice.106.sums, bf16[64,1152]{1,0:T(8,128)(2,1)S(1)} %collective-permute-done.24.rest_0_), custom_call_target="tpu_custom_call" | custom-call | tf_op jit(solution)/shard_map/pallas_call | solution.py:102
  (73 shorter events, 15.5 us)
Async XLA Ops:
  0.6 12.8 %collective-permute-start = (bf16[64,1152]{1,0:T(8,128)(2,1)}, bf16[64,1152]{1,0:T(8,128)(2,1)S(1)}, u32[]{:S(2)}, u32[]{:S(2)}) collective-permute-start(bf16[64,1152]{1,0:T(8,128)(2,1)} %rows.7), channel_id=1, source_target_pairs={{0,112},{1,113},{2,114},{3,115},{4,116},{5,117},{6,118},{7,119},{8... | collective-permute-start | bytes 442376 | tf_op jit(solution)/shard_map/ppermute | solution.py:52
  6.6 6.9 %collective-permute-start.3 = (bf16[64,1152]{1,0:T(8,128)(2,1)}, bf16[64,1152]{1,0:T(8,128)(2,1)S(1)}, u32[]{:S(2)}, u32[]{:S(2)}) collective-permute-start(bf16[64,1152]{1,0:T(8,128)(2,1)} %others.3), channel_id=1, source_target_pairs={{0,5},{1,4},{2,7},{3,6},{4,1},{5,0},{6,3},{7,2},{8,143},{9,142},{1... | collective-permute-start | bytes 442376 | tf_op jit(solution)/shard_map/ppermute | solution.py:52
  7.9 5.5 %collective-permute-start.2 = (bf16[64,1152]{1,0:T(8,128)(2,1)}, bf16[64,1152]{1,0:T(8,128)(2,1)S(1)}, u32[]{:S(2)}, u32[]{:S(2)}) collective-permute-start(bf16[64,1152]{1,0:T(8,128)(2,1)} %others.3), channel_id=1, source_target_pairs={{0,1},{1,0},{2,3},{3,2},{4,5},{5,4},{6,7},{7,6},{8,11},{9,10},{10,... | collective-permute-start | bytes 442376 | tf_op jit(solution)/shard_map/ppermute | solution.py:52
  8.5 5.9 %collective-permute-start.1 = (bf16[64,1152]{1,0:T(8,128)(2,1)}, bf16[64,1152]{1,0:T(8,128)(2,1)S(1)}, u32[]{:S(2)}, u32[]{:S(2)}) collective-permute-start(bf16[64,1152]{1,0:T(8,128)(2,1)} %others.3), channel_id=1, source_target_pairs={{0,4},{1,5},{2,6},{3,7},{4,0},{5,1},{6,2},{7,3},{8,140},{9,141},{1... | collective-permute-start | bytes 442376 | tf_op jit(solution)/shard_map/ppermute | solution.py:52
  14.6 6.8 %collective-permute-start.4 = (bf16[128,1152]{1,0:T(8,128)(2,1)S(1)}, bf16[128,1152]{1,0:T(8,128)(2,1)S(1)}, u32[]{:S(2)}, u32[]{:S(2)}) collective-permute-start(bf16[128,1152]{1,0:T(8,128)(2,1)S(1)} %shard_map.67), channel_id=1, source_target_pairs={{0,16},{1,17},{2,18},{3,19},{4,20},{5,21},{6,22},{7,23},{8,120},{9... | collective-permute-start | bytes 884744 | tf_op jit(solution)/shard_map/ppermute | solution.py:52
  14.9 10.0 %collective-permute-start.9 = (bf16[256,1152]{1,0:T(8,128)(2,1)S(1)}, bf16[256,1152]{1,0:T(8,128)(2,1)S(1)}, u32[]{:S(2)}, u32[]{:S(2)}) collective-permute-start(bf16[256,1152]{1,0:T(8,128)(2,1)S(1)} %shard_map.68.refs_2_.quad.refs_1_.refs_0_), channel_id=1, source_target_pairs={{0,132},{1,133},{2,134},{3,135},{4,128},{5,129},{6,130},{7,131},{8... | collective-permute-start | bytes 1769480 | tf_op jit(solution)/shard_map/ppermute | solution.py:52
  16.8 11.1 %collective-permute-start.8 = (bf16[256,1152]{1,0:T(8,128)(2,1)S(1)}, bf16[256,1152]{1,0:T(8,128)(2,1)S(1)}, u32[]{:S(2)}, u32[]{:S(2)}) collective-permute-start(bf16[256,1152]{1,0:T(8,128)(2,1)S(1)} %shard_map.68.refs_2_.quad.refs_1_.refs_0_), channel_id=1, source_target_pairs={{0,3},{1,2},{2,1},{3,0},{4,7},{5,6},{6,5},{7,4},{8,9},{9,8},{10,11... | collective-permute-start | bytes 1769480 | tf_op jit(solution)/shard_map/ppermute | solution.py:52
  21.5 8.2 %collective-permute-start.7 = (bf16[256,1152]{1,0:T(8,128)(2,1)S(1)}, bf16[256,1152]{1,0:T(8,128)(2,1)S(1)}, u32[]{:S(2)}, u32[]{:S(2)}) collective-permute-start(bf16[256,1152]{1,0:T(8,128)(2,1)S(1)} %pad_maximum_fusion.refs_0_.refs_3_), channel_id=1, source_target_pairs={{0,8},{1,9},{2,10},{3,11},{4,12},{5,13},{6,14},{7,15},{8,0},{9,1},... | collective-permute-start | bytes 1769480 | tf_op jit(solution)/shard_map/ppermute | solution.py:52
  21.6 10.9 %collective-permute-start.6 = (bf16[128,1152]{1,0:T(8,128)(2,1)S(1)}, bf16[128,1152]{1,0:T(8,128)(2,1)S(1)}, u32[]{:S(2)}, u32[]{:S(2)}) collective-permute-start(bf16[128,1152]{1,0:T(8,128)(2,1)S(1)} %collective-permute-done.4), channel_id=1, source_target_pairs={{0,96},{1,97},{2,98},{3,99},{4,100},{5,101},{6,102},{7,103},{8,40}... | collective-permute-start | bytes 884744 | tf_op jit(solution)/shard_map/ppermute | solution.py:52
  23.1 12.4 %collective-permute-start.5 = (bf16[128,1152]{1,0:T(8,128)(2,1)S(1)}, bf16[128,1152]{1,0:T(8,128)(2,1)S(1)}, u32[]{:S(2)}, u32[]{:S(2)}) collective-permute-start(bf16[128,1152]{1,0:T(8,128)(2,1)S(1)} %collective-permute-done.4), channel_id=1, source_target_pairs={{0,112},{1,113},{2,114},{3,115},{4,116},{5,117},{6,118},{7,119},{8... | collective-permute-start | bytes 884744 | tf_op jit(solution)/shard_map/ppermute | solution.py:52
  24.9 11.0 %collective-permute-start.11 = (bf16[128,1152]{1,0:T(8,128)(2,1)S(1)}, bf16[128,1152]{1,0:T(8,128)(2,1)S(1)}, u32[]{:S(2)}, u32[]{:S(2)}) collective-permute-start(bf16[128,1152]{1,0:T(8,128)(2,1)S(1)} %slice.93), channel_id=1, source_target_pairs={{0,3},{1,2},{2,1},{3,0},{4,7},{5,6},{6,5},{7,4},{8,9},{9,8},{10,11... | collective-permute-start | bytes 884744 | tf_op jit(solution)/shard_map/ppermute | solution.py:52
  27.9 7.9 %collective-permute-start.10 = (bf16[128,1152]{1,0:T(8,128)(2,1)S(1)}, bf16[128,1152]{1,0:T(8,128)(2,1)S(1)}, u32[]{:S(2)}, u32[]{:S(2)}) collective-permute-start(bf16[128,1152]{1,0:T(8,128)(2,1)S(1)} %slice.92), channel_id=1, source_target_pairs={{0,132},{1,133},{2,134},{3,135},{4,128},{5,129},{6,130},{7,131},{8... | collective-permute-start | bytes 884744 | tf_op jit(solution)/shard_map/ppermute | solution.py:52
  39.4 6.0 %collective-permute-start.13 = (bf16[256,1152]{1,0:T(8,128)(2,1)S(1)}, bf16[256,1152]{1,0:T(8,128)(2,1)S(1)}, u32[]{:S(2)}, u32[]{:S(2)}) collective-permute-start(bf16[256,1152]{1,0:T(8,128)(2,1)S(1)} %get-tuple-element.35), channel_id=1, source_target_pairs={{0,8},{1,9},{2,10},{3,11},{4,12},{5,13},{6,14},{7,15},{8,0},{9,1},... | collective-permute-start | bytes 1769480 | tf_op jit(solution)/shard_map/ppermute | solution.py:52
  41.5 19.5 %collective-permute-start.17 = (bf16[256,1152]{1,0:T(8,128)(2,1)S(1)}, bf16[256,1152]{1,0:T(8,128)(2,1)S(1)}, u32[]{:S(2)}, u32[]{:S(2)}) collective-permute-start(bf16[256,1152]{1,0:T(8,128)(2,1)S(1)} %shard_map.78), channel_id=1, source_target_pairs={{0,135},{1,134},{2,133},{3,132},{4,131},{5,130},{6,129},{7,128},{8... | collective-permute-start | bytes 1769480 | tf_op jit(solution)/shard_map/ppermute | solution.py:52
  46.1 4.9 %collective-permute-start.14 = (bf16[256,1152]{1,0:T(8,128)(2,1)S(1)}, bf16[256,1152]{1,0:T(8,128)(2,1)S(1)}, u32[]{:S(2)}, u32[]{:S(2)}) collective-permute-start(bf16[256,1152]{1,0:T(8,128)(2,1)S(1)} %get-tuple-element.38), channel_id=1, source_target_pairs={{0,8},{1,9},{2,10},{3,11},{4,12},{5,13},{6,14},{7,15},{8,0},{9,1},... | collective-permute-start | bytes 1769480 | tf_op jit(solution)/shard_map/ppermute | solution.py:52
  46.2 13.7 %collective-permute-start.15 = (bf16[128,1152]{1,0:T(8,128)(2,1)S(1)}, bf16[128,1152]{1,0:T(8,128)(2,1)S(1)}, u32[]{:S(2)}, u32[]{:S(2)}) collective-permute-start(bf16[128,1152]{1,0:T(8,128)(2,1)S(1)} %get-tuple-element.49), channel_id=1, source_target_pairs={{0,112},{1,113},{2,114},{3,115},{4,116},{5,117},{6,118},{7,119},{8... | collective-permute-start | bytes 884744 | tf_op jit(solution)/shard_map/ppermute | solution.py:52
  47.5 12.4 %collective-permute-start.16 = (bf16[128,1152]{1,0:T(8,128)(2,1)S(1)}, bf16[128,1152]{1,0:T(8,128)(2,1)S(1)}, u32[]{:S(2)}, u32[]{:S(2)}) collective-permute-start(bf16[128,1152]{1,0:T(8,128)(2,1)S(1)} %get-tuple-element.50), channel_id=1, source_target_pairs={{0,32},{1,33},{2,34},{3,35},{4,36},{5,37},{6,38},{7,39},{8,104},{9... | collective-permute-start | bytes 884744 | tf_op jit(solution)/shard_map/ppermute | solution.py:52
  48.4 12.6 %collective-permute-start.18 = (bf16[256,1152]{1,0:T(8,128)(2,1)S(1)}, bf16[256,1152]{1,0:T(8,128)(2,1)S(1)}, u32[]{:S(2)}, u32[]{:S(2)}) collective-permute-start(bf16[256,1152]{1,0:T(8,128)(2,1)S(1)} %shard_map.79), channel_id=1, source_target_pairs={{0,3},{1,2},{2,1},{3,0},{4,7},{5,6},{6,5},{7,4},{8,9},{9,8},{10,11... | collective-permute-start | bytes 1769480 | tf_op jit(solution)/shard_map/ppermute | solution.py:52
  51.0 10.0 %collective-permute-start.19 = (bf16[256,1152]{1,0:T(8,128)(2,1)S(1)}, bf16[256,1152]{1,0:T(8,128)(2,1)S(1)}, u32[]{:S(2)}, u32[]{:S(2)}) collective-permute-start(bf16[256,1152]{1,0:T(8,128)(2,1)S(1)} %shard_map.80), channel_id=1, source_target_pairs={{0,132},{1,133},{2,134},{3,135},{4,128},{5,129},{6,130},{7,131},{8... | collective-permute-start | bytes 1769480 | tf_op jit(solution)/shard_map/ppermute | solution.py:52
  60.0 7.6 %collective-permute-start.23 = (bf16[128,1152]{1,0:T(8,128)(2,1)S(1)}, bf16[128,1152]{1,0:T(8,128)(2,1)S(1)}, u32[]{:S(2)}, u32[]{:S(2)}) collective-permute-start(bf16[128,1152]{1,0:T(8,128)(2,1)S(1)} %fusion), channel_id=1, source_target_pairs={{0,16},{1,17},{2,18},{3,19},{4,20},{5,21},{6,22},{7,23},{8,120},{9... | collective-permute-start | bytes 884744 | tf_op jit(solution)/shard_map/ppermute | solution.py:52
  61.3 7.3 %collective-permute-start.22 = (bf16[64,1152]{1,0:T(8,128)(2,1)S(1)}, bf16[64,1152]{1,0:T(8,128)(2,1)S(1)}, u32[]{:S(2)}, u32[]{:S(2)}) collective-permute-start(bf16[64,1152]{1,0:T(8,128)(2,1)S(1)} %get-tuple-element.46), channel_id=1, source_target_pairs={{0,5},{1,4},{2,7},{3,6},{4,1},{5,0},{6,3},{7,2},{8,143},{9,142},{1... | collective-permute-start | bytes 442376 | tf_op jit(solution)/shard_map/ppermute | solution.py:52
  64.6 7.7 %collective-permute-start.21 = (bf16[64,1152]{1,0:T(8,128)(2,1)S(1)}, bf16[64,1152]{1,0:T(8,128)(2,1)S(1)}, u32[]{:S(2)}, u32[]{:S(2)}) collective-permute-start(bf16[64,1152]{1,0:T(8,128)(2,1)S(1)} %get-tuple-element.47), channel_id=1, source_target_pairs={{0,1},{1,0},{2,3},{3,2},{4,5},{5,4},{6,7},{7,6},{8,11},{9,10},{10,... | collective-permute-start | bytes 442376 | tf_op jit(solution)/shard_map/ppermute | solution.py:52
  67.6 5.1 %collective-permute-start.20 = (bf16[64,1152]{1,0:T(8,128)(2,1)S(1)}, bf16[64,1152]{1,0:T(8,128)(2,1)S(1)}, u32[]{:S(2)}, u32[]{:S(2)}) collective-permute-start(bf16[64,1152]{1,0:T(8,128)(2,1)S(1)} %get-tuple-element.48), channel_id=1, source_target_pairs={{0,4},{1,5},{2,6},{3,7},{4,0},{5,1},{6,2},{7,3},{8,140},{9,141},{1... | collective-permute-start | bytes 442376 | tf_op jit(solution)/shard_map/ppermute | solution.py:52
  67.7 6.4 %collective-permute-start.24 = (bf16[64,1152]{1,0:T(8,128)(2,1)S(1)}, bf16[64,1152]{1,0:T(8,128)(2,1)S(1)}, u32[]{:S(2)}, u32[]{:S(2)}) collective-permute-start(bf16[64,1152]{1,0:T(8,128)(2,1)S(1)} %slice.113), channel_id=1, source_target_pairs={{0,112},{1,113},{2,114},{3,115},{4,116},{5,117},{6,118},{7,119},{8... | collective-permute-start | bytes 442376 | tf_op jit(solution)/shard_map/ppermute | solution.py:52
  (5 other events, 14.4 us)
